TPU v7x, 256 devices: a whole 4x4x8 slice. The times are simulated.
256 devices in a mesh: path: 64 (over y, z, core), fsdp: 4 (over x).
Axes of the slice: x: 4, y: 4, z: 8, core: 2. Of those that a mesh axis runs over, the one named last changes fastest.
Arguments:
- inputs: bfloat16 [112640, 1024], P(('path', 'fsdp')), may hold values from -6 to 6
- cotangent: bfloat16 [112640, 1024], P(('path', 'fsdp')), may hold values from -6 to 6
- master: bfloat16 [16, 2, 1024, 4096], P(None, None, 'path', 'fsdp'), may hold values from -4 to 4
- momentum: float32 [16, 2, 1024, 4096], P(None, None, 'path', 'fsdp'), may hold values from -2 to 2
- sharing: int32 [64, 1], replicated, may hold values from 0 to 15
- block_owner: int32 [64], replicated, may hold values from 0 to 63, each once
Outputs:
- new_state: float32 [16, 2, 1024, 4096], P(None, None, 'path', 'fsdp')
- path_modules: bfloat16 [64, 2, 1024, 4096], P('path', None, None, 'fsdp')
Inputs may be any that keep to these rules, and one draw needn't show every extreme that they name: `sharing`: each path names one module, and every module is named by one or more paths. `block_owner`: a permutation of the path indices.
All inputs are finite; a program needn't handle non-finite values.
Results may differ from a plain program's by a relative error of at most 0.0034.
Values may be sent and summed in bfloat16 or wider, within the bound.
No kernel may reach another device: no remote copies, remote signals or barrier semaphores. Data moves between devices by JAX's collectives and lax.ppermute only.
A program may use at most 128 MiB of HBM per device.

v0:
```python
import math

import jax
import jax.numpy as jnp
from jax import lax
from jax.sharding import PartitionSpec as P

inner_rate = 10.0
outer_rate = 0.7
outer_decay = 0.9


def silu_slope(values):
    sig = jax.nn.sigmoid(values)
    return sig * (1.0 + values * (1.0 - sig))


def shards(inputs, cotangent, master, momentum, sharing, block_owner):
    path_count = lax.axis_size("path")
    modules = master.shape[0]
    block_rows = master.shape[2]
    block_cols = master.shape[3]
    module_of = sharing[:, 0]
    inverse = jnp.argsort(block_owner)
    tokens_all, grads_all = (
        lax.all_gather(inputs, "fsdp", axis=0, tiled=True),
        lax.all_gather(cotangent, "fsdp", axis=0, tiled=True),
    )
    tok_rows = tokens_all.shape[0]
    model_width = tokens_all.shape[1]
    hidden_units = block_cols * lax.axis_size("fsdp")
    scale_in = 1.0 / math.sqrt(model_width)
    scale_hid = 1.0 / math.sqrt(hidden_units)
    step_rate = inner_rate / math.sqrt(tok_rows)
    ordered = jnp.transpose(master, (1, 0, 2, 3))
    outgoing = jnp.take(ordered, module_of, axis=1)
    arrived = lax.all_to_all(outgoing, "path", split_axis=1, concat_axis=1, tiled=True)
    module = jnp.take(arrived, block_owner, axis=1).reshape(2, model_width, block_cols)
    up_weight = module[0]
    down_weight = module[1]
    pre_act = jnp.dot(tokens_all, up_weight, preferred_element_type=jnp.float32) * scale_in
    activation = jax.nn.silu(pre_act).astype(jnp.bfloat16)
    back_grad = jnp.dot(grads_all, down_weight, preferred_element_type=jnp.float32) * scale_hid
    slope_grad = (back_grad * silu_slope(pre_act)).astype(jnp.bfloat16)
    grad_down = (
        lax.dot_general(
            grads_all, activation, (((0,), (0,)), ((), ())), preferred_element_type=jnp.float32
        )
        * scale_hid
    )
    delta_down = (grad_down * step_rate).astype(jnp.bfloat16)
    grad_up = (
        lax.dot_general(
            tokens_all, slope_grad, (((0,), (0,)), ((), ())), preferred_element_type=jnp.float32
        )
        * scale_in
    )
    delta_up = (grad_up * step_rate).astype(jnp.bfloat16)
    stacked = jnp.stack([delta_up, delta_down]).reshape(2, path_count, block_rows, block_cols)
    received = lax.all_to_all(
        jnp.take(stacked, inverse, axis=1), "path", split_axis=1, concat_axis=1, tiled=True
    )
    onehot = module_of[None, :] == jnp.arange(modules, dtype=jnp.int32)[:, None]
    counts = jnp.sum(onehot, axis=1).astype(jnp.float32)
    totals = lax.dot_general(
        onehot.astype(jnp.bfloat16),
        received.reshape(2, path_count, block_rows * block_cols),
        (((1,), (1,)), ((), ())),
        preferred_element_type=jnp.float32,
    )
    averaged = totals.reshape(modules, 2, block_rows, block_cols) / counts[:, None, None, None]
    new_state = outer_decay * momentum + averaged
    updated = (
        master.astype(jnp.float32) - outer_rate * (averaged + outer_decay * new_state)
    ).astype(jnp.bfloat16)
    sending = jnp.take(jnp.transpose(updated, (1, 0, 2, 3)), module_of, axis=1)
    back_home = lax.all_to_all(sending, "path", split_axis=1, concat_axis=1, tiled=True)
    own_module = jnp.take(back_home, block_owner, axis=1).reshape(2, model_width, block_cols)
    return (new_state, own_module[None])


def solution(mesh):
    placed = (
        P(("path", "fsdp"), None),
        P(("path", "fsdp"), None),
        P(None, None, "path", "fsdp"),
        P(None, None, "path", "fsdp"),
        P(),
        P(),
    )
    return jax.shard_map(
        shards,
        mesh=mesh,
        in_specs=placed,
        out_specs=(P(None, None, "path", "fsdp"), P("path", None, None, "fsdp")),
        check_vma=False,
    )
```

profile of v0, /device:TPU:1, one launch (start us, length us, event | category | flops | bytes accessed | tf_op | source)
XLA Modules:
  0.0 434.1 jit_solution(692745030152496853)
XLA Ops:
  8.6 4.1 gather_fusion
  12.6 4.6 %select_bitcast_fusion.4 = bf16[2,64,16,1024]{3,2,0,1:T(8,128)(2,1)} fusion(bf16[64,2,16,1024]{3,2,1,0:T(8,128)(2,1)} %gather_fusion, pred[64]{0:T(512)(128)(4,1)S(1)} %compare_and_fusion.2), kind=kLoop, calls=%fused_computation.24 | loop fusion | flops 2097152 | bytes 8388672 | tf_op jit(solution)/shard_map/jit(_take)/select_n | solution.py:36
  17.3 13.5 %all-to-all-start = ((bf16[2,64,16,1024]{3,2,0,1:T(8,128)(2,1)}), bf16[2,64,16,1024]{3,2,0,1:T(8,128)(2,1)}, u32[]{:S(2)}, u32[]{:S(2)}) async-start(bf16[2,64,16,1024]{3,2,0,1:T(8,128)(2,1)} %select_bitcast_fusion.4), calls=%async_computation | async-start | bytes 8388608 | tf_op jit(solution)/shard_map/all_to_all | solution.py:37
  33.6 93.0 %all-to-all-done = bf16[2,64,16,1024]{3,2,0,1:T(8,128)(2,1)} async-done(((bf16[2,64,16,1024]{3,2,0,1:T(8,128)(2,1)}), bf16[2,64,16,1024]{3,2,0,1:T(8,128)(2,1)}, u32[]{:S(2)}, u32[]{:S(2)}) %all-to-all-start) | async-done | bytes 4194336 | tf_op jit(solution)/shard_map/all_to_all | solution.py:37
  126.7 5.0 %gather_fusion.1 = bf16[64,2,16,1024]{3,2,1,0:T(8,128)(2,1)} fusion(bf16[2,64,16,1024]{3,2,0,1:T(8,128)(2,1)} %all-to-all-done, s32[1024]{0:T(1024)S(1)} %pad_clamp_fusion.1), kind=kCustom, calls=%fused_computation.1.clone | custom fusion | bytes 8388864 | tf_op jit(solution)/shard_map/jit(_take)/gather | solution.py:38
  131.7 2.6 select_bitcast_fusion.3
  136.1 9.5 %fusion.34 = f32[1024,1760]{0,1:T(8,128)} fusion(bf16[1760,1024]{1,0:T(8,128)(2,1)} %all-gather.5.cloned.1.call-done, bf16[1024,1024]{1,0:T(8,128)(2,1)} %bitcast.93), kind=kOutput, calls=%fused_computation.53 | convolution fusion | flops 3690987520 | bytes 12910592 | tf_op jit(solution)/shard_map/dot_general | solution.py:41
  145.6 9.6 %multiply_convert_fusion = bf16[1024,1024]{0,1:T(8,128)(2,1)} fusion(bf16[1760,1024]{1,0:T(8,128)(2,1)} %all-gather.3.cloned.1.call-done, f32[1024,1760]{0,1:T(8,128)} %fusion.34), kind=kOutput, calls=%fused_computation.25 | convolution fusion | flops 3703898112 | bytes 12910592 | tf_op jit(solution)/shard_map/dot_general | solution.py:46
  155.2 15.5 %multiply_convert_fusion.1 = bf16[1024,1024]{0,1:T(8,128)(2,1)} fusion(bf16[1760,1024]{1,0:T(8,128)(2,1)} %all-gather.5.cloned.1.call-done, f32[1024,1760]{0,1:T(8,128)} %fusion.34, bf16[1760,1024]{1,0:T(8,128)(2,1)} %all-gather.3.cloned.1.call-done, bf16[1024,1024]{1,0:T(8,128)(2,1)S(1)} %bitcast.92), kind=kOutput, calls=%fused_computation.26 | convolution fusion | flops 7403896832 | bytes 18612224 | tf_op jit(solution)/shard_map/dot_general | solution.py:53
  170.7 4.6 %pad_maximum_fusion = bf16[2,64,16,1024]{3,2,1,0:T(8,128)(2,1)} fusion(bf16[1,64,16,1024]{3,2,1,0:T(8,128)(2,1)} %bitcast.94, bf16[1,64,16,1024]{3,2,1,0:T(8,128)(2,1)} %bitcast.95), kind=kLoop, calls=%fused_computation.19 | loop fusion | flops 2097152 | bytes 8388608 | tf_op jit(solution)/shard_map/stack | solution.py:59
  175.4 4.9 %gather_fusion.2 = bf16[64,2,16,1024]{3,2,1,0:T(8,128)(2,1)} fusion(bf16[2,64,16,1024]{3,2,1,0:T(8,128)(2,1)} %pad_maximum_fusion, s32[1024]{0:T(1024)S(1)} %pad_clamp_fusion), kind=kCustom, calls=%fused_computation.3.clone | custom fusion | bytes 8388864 | tf_op jit(solution)/shard_map/jit(_take)/gather | solution.py:61
  180.3 4.6 %select_bitcast_fusion.2 = bf16[2,64,16,1024]{3,2,0,1:T(8,128)(2,1)} fusion(bf16[64,2,16,1024]{3,2,1,0:T(8,128)(2,1)} %gather_fusion.2, pred[64]{0:T(512)(128)(4,1)S(1)} %compare_and_fusion), kind=kLoop, calls=%fused_computation.22 | loop fusion | flops 2097152 | bytes 8388672 | tf_op jit(solution)/shard_map/jit(_take)/select_n | solution.py:61
  184.9 5.9 %all-to-all-start.1 = ((bf16[2,64,16,1024]{3,2,0,1:T(8,128)(2,1)}), bf16[2,64,16,1024]{3,2,0,1:T(8,128)(2,1)}, u32[]{:S(2)}, u32[]{:S(2)}) async-start(bf16[2,64,16,1024]{3,2,0,1:T(8,128)(2,1)} %select_bitcast_fusion.2), calls=%async_computation.1 | async-start | bytes 8388608 | tf_op jit(solution)/shard_map/all_to_all | solution.py:60
  191.0 95.8 %all-to-all-done.1 = bf16[2,64,16,1024]{3,2,0,1:T(8,128)(2,1)} async-done(((bf16[2,64,16,1024]{3,2,0,1:T(8,128)(2,1)}), bf16[2,64,16,1024]{3,2,0,1:T(8,128)(2,1)}, u32[]{:S(2)}, u32[]{:S(2)}) %all-to-all-start.1) | async-done | bytes 4194336 | tf_op jit(solution)/shard_map/all_to_all | solution.py:60
  286.7 7.8 %reshape.90 = bf16[2,64,16384]{2,0,1:T(2,128)(2,1)} reshape(bf16[2,64,16,1024]{3,2,0,1:T(8,128)(2,1)} %all-to-all-done.1) | data formatting | bytes 8388608 | tf_op jit(solution)/shard_map/reshape | solution.py:67
  294.5 4.7 %copy.20 = bf16[2,64,16384]{2,1,0:T(8,128)(2,1)S(1)} copy(bf16[2,64,16384]{2,0,1:T(2,128)(2,1)} %reshape.90) | data formatting | bytes 8388608 | tf_op jit(solution)/shard_map/reshape | solution.py:67
  299.2 3.1 fusion.20
  302.9 2.8 gather_fusion.3
  305.7 4.6 %select_bitcast_fusion.1 = bf16[2,64,16,1024]{3,2,0,1:T(8,128)(2,1)} fusion(bf16[64,2,16,1024]{3,2,1,0:T(8,128)(2,1)} %gather_fusion.3, pred[64]{0:T(512)(128)(4,1)S(1)} %compare_and_fusion.2), kind=kLoop, calls=%fused_computation.21 | loop fusion | flops 2097152 | bytes 8388672 | tf_op jit(solution)/shard_map/jit(_take)/select_n | solution.py:76
  310.3 5.9 %all-to-all-start.2 = ((bf16[2,64,16,1024]{3,2,0,1:T(8,128)(2,1)}), bf16[2,64,16,1024]{3,2,0,1:T(8,128)(2,1)}, u32[]{:S(2)}, u32[]{:S(2)}) async-start(bf16[2,64,16,1024]{3,2,0,1:T(8,128)(2,1)} %select_bitcast_fusion.1), calls=%async_computation.2 | async-start | bytes 8388608 | tf_op jit(solution)/shard_map/all_to_all | solution.py:77
  318.8 93.3 %all-to-all-done.2 = bf16[2,64,16,1024]{3,2,0,1:T(8,128)(2,1)} async-done(((bf16[2,64,16,1024]{3,2,0,1:T(8,128)(2,1)}), bf16[2,64,16,1024]{3,2,0,1:T(8,128)(2,1)}, u32[]{:S(2)}, u32[]{:S(2)}) %all-to-all-start.2) | async-done | bytes 4194336 | tf_op jit(solution)/shard_map/all_to_all | solution.py:77
  412.2 5.0 %copy.16 = bf16[2,64,16,1024]{3,2,1,0:T(8,128)(2,1)} copy(bf16[2,64,16,1024]{3,2,0,1:T(8,128)(2,1)} %all-to-all-done.2) | data formatting | bytes 8388608 | tf_op jit(solution)/shard_map/all_to_all | solution.py:77
  417.2 4.9 %gather_fusion.4 = bf16[64,2,16,1024]{3,2,1,0:T(8,128)(2,1)} fusion(bf16[2,64,16,1024]{3,2,1,0:T(8,128)(2,1)} %copy.16, s32[1024]{0:T(1024)S(1)} %pad_clamp_fusion.1), kind=kCustom, calls=%fused_computation.4.clone | custom fusion | bytes 8388864 | tf_op jit(solution)/shard_map/jit(_take)/gather | solution.py:78
  422.1 2.6 select_bitcast_fusion
  (31 shorter events, 11.7 us)
Async XLA Ops:
  7.2 128.9 %all-gather.5.cloned.1.call-start = ((), (), s32[]{:S(2)}) async-start(), calls=%async_computation.4 | async-start | bytes 4505600 | tf_op jit(solution)/shard_map/all_gather | solution.py:26
  8.6 4.1 copy-start.3
  17.3 14.3 %copy-start.2 = (s32[64]{0:T(128)S(1)}, s32[64]{0:T(128)}, u32[]{:S(2)}) copy-start(s32[64]{0:T(128)} %param.15) | copy-start | bytes 772
  17.3 109.4 %all-to-all-start = ((bf16[2,64,16,1024]{3,2,0,1:T(8,128)(2,1)}), bf16[2,64,16,1024]{3,2,0,1:T(8,128)(2,1)}, u32[]{:S(2)}, u32[]{:S(2)}) async-start(bf16[2,64,16,1024]{3,2,0,1:T(8,128)(2,1)} %select_bitcast_fusion.4), calls=%async_computation | async-start | bytes 8388608 | tf_op jit(solution)/shard_map/all_to_all | solution.py:37
  30.8 114.9 %all-gather.3.cloned.1.call-start = ((), (), s32[]{:S(2)}) async-start(), calls=%async_computation.3 | async-start | bytes 4505600 | tf_op jit(solution)/shard_map/all_gather | solution.py:27
  184.9 101.8 %all-to-all-start.1 = ((bf16[2,64,16,1024]{3,2,0,1:T(8,128)(2,1)}), bf16[2,64,16,1024]{3,2,0,1:T(8,128)(2,1)}, u32[]{:S(2)}, u32[]{:S(2)}) async-start(bf16[2,64,16,1024]{3,2,0,1:T(8,128)(2,1)} %select_bitcast_fusion.2), calls=%async_computation.1 | async-start | bytes 8388608 | tf_op jit(solution)/shard_map/all_to_all | solution.py:60
  294.5 4.7 %copy-start = (bf16[16,2,16,1024]{3,2,1,0:T(8,128)(2,1)S(1)}, bf16[16,2,16,1024]{3,2,1,0:T(8,128)(2,1)}, u32[]{:S(2)}) copy-start(bf16[16,2,16,1024]{3,2,1,0:T(8,128)(2,1)} %param.12) | copy-start | bytes 3145732
  294.5 4.7 %copy-start.1 = (f32[16,2,16,1024]{3,2,1,0:T(8,128)S(1)}, f32[16,2,16,1024]{3,2,1,0:T(8,128)}, u32[]{:S(2)}) copy-start(f32[16,2,16,1024]{3,2,1,0:T(8,128)} %param.13) | copy-start | bytes 6291460
  310.3 101.8 %all-to-all-start.2 = ((bf16[2,64,16,1024]{3,2,0,1:T(8,128)(2,1)}), bf16[2,64,16,1024]{3,2,0,1:T(8,128)(2,1)}, u32[]{:S(2)}, u32[]{:S(2)}) async-start(bf16[2,64,16,1024]{3,2,0,1:T(8,128)(2,1)} %select_bitcast_fusion.1), calls=%async_computation.2 | async-start | bytes 8388608 | tf_op jit(solution)/shard_map/all_to_all | solution.py:77
Sparse Core Ops, SparseCore 0:
  9.8 49.6 all-gather.4
  61.3 46.1 all-gather.2
where the time goes:
time: 435 us; the launch traced here: 434 us
  waiting for transfers between devices  283 us (65%)
  local copies, waits for them, and re-layouts  46.7 us (11%)
  matrix products  37.7 us (9%)
  other arithmetic  26.6 us (6%)
  starting transfers between devices  25.4 us (6%)
  between operations  14.2 us (3%)
    all_to_all x1, waiting for transfers between devices, shards(): lax.all_to_all(jnp.take(stacked, inverse, axis=1), 'path', split_axis=1,...  95.8 us
    all_to_all x1, waiting for transfers between devices, shards(): lax.all_to_all(sending, 'path', split_axis=1, concat_axis=1, tiled=True)  93.3 us
    all_to_all x1, waiting for transfers between devices, shards(): lax.all_to_all(outgoing, 'path', split_axis=1, concat_axis=1, tiled=True)  93 us
    dot_general x1, matrix products, shards(): lax.dot_general(tokens_all, slope_grad, (((0,), (0,)), ((), ())), preferr...  15.5 us
    all_to_all x1, starting transfers between devices, shards(): lax.all_to_all(outgoing, 'path', split_axis=1, concat_axis=1, tiled=True)  13.5 us
    reshape x2, local copies, waits for them, and re-layouts, shards(): received.reshape(2, path_count, block_rows * block_cols)  12.4 us
    dot_general x1, matrix products, shards(): lax.dot_general(grads_all, activation, (((0,), (0,)), ((), ())), preferre...  9.6 us
    dot_general x1, matrix products, shards(): jnp.dot(tokens_all, up_weight, preferred_element_type=jnp.float32)  9.53 us
  transfers between devices with their start and end apart: 5, of which 3 were waited for; matrix products, arithmetic and copies ran while one was open for 8% of the time, Pallas kernels for 0%

commit v1 on v0

v1 whole, which is shorter than its diff:
```python
import functools
import math

import jax
import jax.numpy as jnp
from jax import lax
from jax.experimental import pallas as pl
from jax.experimental.pallas import tpu as pltpu
from jax.sharding import PartitionSpec as P

inner_rate = 10.0
outer_rate = 0.7
outer_decay = 0.9

VMEM_LIMIT = 56 * 1024 * 1024
ANY = pl.BlockSpec(memory_space=pl.ANY)
SMEM = pl.BlockSpec(memory_space=pltpu.SMEM)
VMEM = pl.BlockSpec(memory_space=pltpu.VMEM)


def params():
    return pltpu.CompilerParams(vmem_limit_bytes=VMEM_LIMIT)


def cost(flops, moved):
    return pl.CostEstimate(flops=flops, bytes_accessed=moved, transcendentals=0)


def wait_bytes(ref, sem):
    pltpu.make_async_copy(ref, ref, sem).wait()


def f32_dot(left, right):
    return jnp.dot(left, right, preferred_element_type=jnp.float32)


def pick_kernel(module_of, stored, out, sem):
    @pl.loop(0, out.shape[0])
    def _(path):
        pltpu.make_async_copy(stored.at[module_of[path]], out.at[path], sem).start()

    wait_bytes(out, sem)


def pick(module_of, stored):
    paths = module_of.shape[0]
    shape = (paths,) + stored.shape[1:]
    return pl.pallas_call(
        pick_kernel,
        out_shape=jax.ShapeDtypeStruct(shape, stored.dtype),
        in_specs=[SMEM, VMEM],
        out_specs=ANY,
        scratch_shapes=[pltpu.SemaphoreType.DMA],
        compiler_params=params(),
        cost_estimate=cost(0, 2 * math.prod(shape)),
        name="pick",
    )(module_of, stored)


def load_logical(owner, arrived, half, weight, sem):
    rows = arrived.shape[2]

    @pl.loop(0, arrived.shape[0])
    def _(block):
        pltpu.make_async_copy(
            arrived.at[owner[block], half],
            weight.at[pl.ds(pl.multiple_of(block * rows, rows), rows)],
            sem,
        ).start()


def store_blocks(owner, delta, out, first, count, sem):
    rows = out.shape[1]

    @pl.loop(first, first + count)
    def _(block):
        pltpu.make_async_copy(
            delta.at[pl.ds(pl.multiple_of(block * rows, rows), rows)],
            out.at[owner[block]],
            sem,
        ).start()


def sigmoid(values):
    return 1.0 / (1.0 + jnp.exp(-values))


def delta_rows(owner, left, right, scale, rate, delta, out, sem, tile):
    rows = out.shape[1]

    @pl.loop(0, left.shape[0] // tile)
    def _(step):
        at = pl.ds(pl.multiple_of(step * tile, tile), tile)
        grad = f32_dot(left[at, :], right[...]) * scale
        delta[at, :] = (grad * rate).astype(jnp.bfloat16)
        store_blocks(owner, delta, out, step * (tile // rows), tile // rows, sem)

    wait_bytes(delta, sem)


def down_kernel(
    scales, tile, parts, owner, arrived, tokens, grads_t, out,
    up_weight, tok, grd, act, delta, sems,
):
    scale_in, scale_hid, rate = scales
    part = tokens.shape[0] // parts
    load_logical(owner, arrived, 0, up_weight, sems.at[0])
    copies = [
        pltpu.make_async_copy(
            tokens.at[pl.ds(i * part, part)], tok.at[pl.ds(i * part, part)], sems.at[1 + i]
        )
        for i in range(parts)
    ]
    for copy in copies:
        copy.start()
    grads_copy = pltpu.make_async_copy(grads_t, grd, sems.at[1 + parts])
    grads_copy.start()
    wait_bytes(up_weight, sems.at[0])
    for i, copy in enumerate(copies):
        copy.wait()

        @pl.loop(0, act.shape[1] // tile)
        def _(step):
            at = pl.ds(pl.multiple_of(step * tile, tile), tile)
            pre = f32_dot(tok[pl.ds(i * part, part), :], up_weight[:, at]) * scale_in
            act[pl.ds(i * part, part), at] = (pre * sigmoid(pre)).astype(jnp.bfloat16)

    grads_copy.wait()
    delta_rows(owner, grd, act, scale_hid, rate, delta, out, sems.at[2 + parts], tile)


def up_kernel(
    scales, tile, parts, owner, arrived, tokens, grads, tokens_t, earlier, out,
    up_weight, down_weight, tok, grd, tok_t, slope, delta, sems,
):
    scale_in, scale_hid, rate = scales
    part = tokens.shape[0] // parts
    load_logical(owner, arrived, 0, up_weight, sems.at[0])
    load_logical(owner, arrived, 1, down_weight, sems.at[1])
    copies = [
        pltpu.make_async_copy(tokens, tok, sems.at[2]),
        pltpu.make_async_copy(grads, grd, sems.at[3]),
        pltpu.make_async_copy(tokens_t, tok_t, sems.at[4]),
    ]
    for copy in copies:
        copy.start()
    wait_bytes(up_weight, sems.at[0])
    wait_bytes(down_weight, sems.at[1])
    for copy in copies:
        copy.wait()
    for i in range(parts):

        @pl.loop(0, slope.shape[1] // tile)
        def _(step):
            at = pl.ds(pl.multiple_of(step * tile, tile), tile)
            rows = pl.ds(i * part, part)
            pre = f32_dot(tok[rows, :], up_weight[:, at]) * scale_in
            back = f32_dot(grd[rows, :], down_weight[:, at]) * scale_hid
            sig = sigmoid(pre)
            slope[rows, at] = (back * (sig * (1.0 + pre * (1.0 - sig)))).astype(jnp.bfloat16)

    delta_rows(owner, tok_t, slope, scale_in, rate, delta, out, sems.at[5], tile)


def delta_down(scales, owner, arrived, tokens, grads_t):
    paths, _, rows, cols = arrived.shape
    count, width = tokens.shape
    bf16 = jnp.bfloat16
    return pl.pallas_call(
        functools.partial(down_kernel, scales, 256, 2),
        out_shape=jax.ShapeDtypeStruct((paths, rows, cols), bf16),
        in_specs=[SMEM, ANY, ANY, ANY],
        out_specs=ANY,
        scratch_shapes=[
            pltpu.VMEM((width, cols), bf16),
            pltpu.VMEM((count, width), bf16),
            pltpu.VMEM((width, count), bf16),
            pltpu.VMEM((count, cols), bf16),
            pltpu.VMEM((width, cols), bf16),
            pltpu.SemaphoreType.DMA((5,)),
        ],
        compiler_params=params(),
        cost_estimate=cost(4 * count * width * cols, 4 * (2 * count * width + 2 * width * cols)),
        name="delta_down",
    )(owner, arrived, tokens, grads_t)


def delta_up(scales, owner, arrived, tokens, grads, tokens_t, earlier):
    paths, _, rows, cols = arrived.shape
    count, width = tokens.shape
    bf16 = jnp.bfloat16
    return pl.pallas_call(
        functools.partial(up_kernel, scales, 256, 2),
        out_shape=jax.ShapeDtypeStruct((paths, rows, cols), bf16),
        in_specs=[SMEM, ANY, ANY, ANY, ANY, ANY],
        out_specs=ANY,
        scratch_shapes=[
            pltpu.VMEM((width, cols), bf16),
            pltpu.VMEM((width, cols), bf16),
            pltpu.VMEM((count, width), bf16),
            pltpu.VMEM((count, width), bf16),
            pltpu.VMEM((width, count), bf16),
            pltpu.VMEM((count, cols), bf16),
            pltpu.VMEM((width, cols), bf16),
            pltpu.SemaphoreType.DMA((6,)),
        ],
        compiler_params=params(),
        cost_estimate=cost(6 * count * width * cols, 4 * (3 * count * width + 3 * width * cols)),
        name="delta_up",
    )(owner, arrived, tokens, grads, tokens_t, earlier)


def outer_step(module_of, received, master, momentum, state, updated, total):
    modules = total.shape[0]
    paths = received.shape[0]
    total[...] = jnp.zeros_like(total)

    @pl.loop(0, paths)
    def _(path):
        total[module_of[path]] += received[path].astype(jnp.float32)

    @pl.loop(0, modules)
    def _(module):
        count = lax.fori_loop(
            0, paths, lambda p, n: n + (module_of[p] == module).astype(jnp.int32), 0
        )
        averaged = total[module] / jnp.full(total.shape[1:], count, jnp.int32).astype(jnp.float32)
        new = outer_decay * momentum[module] + averaged
        state[module] = new
        weights = master[module].astype(jnp.float32)
        updated[module] = (weights - outer_rate * (averaged + outer_decay * new)).astype(
            jnp.bfloat16
        )


def outer_kernel(
    half, module_of, received, master, momentum, *refs,
):
    refs = refs[2:] if half == 0 else refs
    new_state, sending, got, mas, mom, state, updated, total, sems = refs
    copies = [
        pltpu.make_async_copy(received, got, sems.at[0]),
        pltpu.make_async_copy(master.at[:, half], mas, sems.at[1]),
        pltpu.make_async_copy(momentum.at[:, half], mom, sems.at[2]),
    ]
    for copy in copies:
        copy.start()
    for copy in copies:
        copy.wait()
    outer_step(module_of, got, mas, mom, state, updated, total)

    @pl.loop(0, sending.shape[0])
    def _(path):
        pltpu.make_async_copy(
            updated.at[module_of[path]], sending.at[path, half], sems.at[3]
        ).start()

    store = pltpu.make_async_copy(state, new_state.at[:, half], sems.at[4])
    store.start()
    wait_bytes(got, sems.at[3])
    store.wait()


def outer(half, module_of, received, master, momentum, earlier):
    paths, rows, cols = received.shape
    modules = master.shape[0]
    f32, bf16 = jnp.float32, jnp.bfloat16
    operands = (module_of, received, master, momentum) + earlier
    return pl.pallas_call(
        functools.partial(outer_kernel, half),
        out_shape=(
            jax.ShapeDtypeStruct(momentum.shape, f32),
            jax.ShapeDtypeStruct((paths, 2, rows, cols), bf16),
        ),
        in_specs=[SMEM] + [ANY] * (len(operands) - 1),
        out_specs=(ANY, ANY),
        scratch_shapes=[
            pltpu.VMEM((paths, rows, cols), bf16),
            pltpu.VMEM((modules, rows, cols), bf16),
            pltpu.VMEM((modules, rows, cols), f32),
            pltpu.VMEM((modules, rows, cols), f32),
            pltpu.VMEM((modules, rows, cols), bf16),
            pltpu.VMEM((modules, rows, cols), f32),
            pltpu.SemaphoreType.DMA((5,)),
        ],
        input_output_aliases={4: 0, 5: 1} if earlier else {},
        compiler_params=params(),
        cost_estimate=cost(paths * rows * cols, 4 * paths * rows * cols),
        name="outer",
    )(*operands)


def home_kernel(owner, back, out, sem):
    @pl.loop(0, back.shape[0])
    def _(block):
        for half in range(2):
            pltpu.make_async_copy(
                back.at[owner[block], half], out.at[half, block], sem
            ).start()

    wait_bytes(out, sem)


def bring_home(owner, back):
    paths, halves, rows, cols = back.shape
    return pl.pallas_call(
        home_kernel,
        out_shape=jax.ShapeDtypeStruct((halves, paths, rows, cols), back.dtype),
        in_specs=[SMEM, ANY],
        out_specs=ANY,
        scratch_shapes=[pltpu.SemaphoreType.DMA],
        compiler_params=params(),
        cost_estimate=cost(0, 4 * paths * halves * rows * cols),
        name="bring_home",
    )(owner, back)


def exchange(blocks):
    return lax.all_to_all(blocks, "path", split_axis=0, concat_axis=0, tiled=True)


def shards(inputs, cotangent, master, momentum, sharing, block_owner):
    block_cols = master.shape[3]
    module_of = sharing[:, 0]
    grads_all = lax.all_gather(cotangent, "fsdp", axis=0, tiled=True)
    tokens_all = lax.all_gather(inputs, "fsdp", axis=0, tiled=True)
    tok_rows, model_width = tokens_all.shape
    hidden_units = block_cols * lax.axis_size("fsdp")
    scales = (
        1.0 / math.sqrt(model_width),
        1.0 / math.sqrt(hidden_units),
        inner_rate / math.sqrt(tok_rows),
    )
    arrived = exchange(pick(module_of, master))
    down = delta_down(scales, block_owner, arrived, tokens_all, grads_all.T)
    got_down = exchange(down)
    up = delta_up(scales, block_owner, arrived, tokens_all, grads_all, tokens_all.T, down)
    got_up = exchange(up)
    earlier = outer(1, module_of, got_down, master, momentum, ())
    new_state, sending = outer(0, module_of, got_up, master, momentum, tuple(earlier))
    own_module = bring_home(block_owner, exchange(sending))
    return (new_state, own_module.reshape(1, 2, model_width, block_cols))


def solution(mesh):
    placed = (
        P(("path", "fsdp"), None),
        P(("path", "fsdp"), None),
        P(None, None, "path", "fsdp"),
        P(None, None, "path", "fsdp"),
        P(),
        P(),
    )
    return jax.shard_map(
        shards,
        mesh=mesh,
        in_specs=placed,
        out_specs=(P(None, None, "path", "fsdp"), P("path", None, None, "fsdp")),
        check_vma=False,
    )
```

time: 435 us -> 500 us (1.15)
  Pallas kernels: 0 us -> 194 us
  waiting for transfers between devices: 283 us -> 152 us
  blocking collectives: 0 us -> 102 us
  matrix products: 37.7 us -> 0 us
  local copies, waits for them, and re-layouts: 46.7 us -> 11.8 us
  other arithmetic: 26.6 us -> 0 us
    all_to_all x3, waiting for transfers between devices: 282 us -> 74.4 us  [exchange(): lax.all_to_all(blocks, 'path', split_axis=0, concat_axis=0, tiled=True)]
    pallas_call x0 -> x6, Pallas kernels: none -> 194 us  [the longest x1 129 us: bring_home(): pl.pallas_call(home_kernel, out_shape=jax.ShapeDtypeStruct((halves, paths...]
    all_to_all x0 -> x1, blocking collectives: none -> 102 us  [exchange(): lax.all_to_all(blocks, 'path', split_axis=0, concat_axis=0, tiled=True)]
    all_gather x2, waiting for transfers between devices: 0.01 us -> 76.4 us  [the longest x1 42.1 us: shards(): tokens_all = lax.all_gather(inputs, 'fsdp', axis=0, tiled=True)]
    dot_general x4 -> x0, matrix products: 37.7 us -> none  [the longest x1 15.5 us: shards(): lax.dot_general(tokens_all, slope_grad, (((0,), (0,)), ((), ())), preferr...]
    gather x5 -> x0, local copies, waits for them, and re-layouts: 21.8 us -> none  [the longest x1 5.01 us: shards(): jnp.take(arrived, block_owner, axis=1).reshape(2, model_width, block_cols)]
    select_n x8 -> x0, other arithmetic: 19.8 us -> none  [the longest x2 5.3 us: shards(): outgoing = jnp.take(ordered, module_of, axis=1)]
    reshape x2 -> x0, local copies, waits for them, and re-layouts: 12.4 us -> none  [shards(): received.reshape(2, path_count, block_rows * block_cols)]
  transfers between devices with their start and end apart: 5 -> 5, of which waited for: 3 -> 5; matrix products, arithmetic and copies ran while one was open for 8% -> 2% of each run, Pallas kernels for 0% -> 8%
where the time goes in v1:
time: 500 us; the launch traced here: 499 us
  Pallas kernels  194 us (39%)
  waiting for transfers between devices  152 us (30%)
  blocking collectives  102 us (20%)
  starting transfers between devices  25.2 us (5%)
  between operations  14.1 us (3%)
  local copies, waits for them, and re-layouts  11.8 us (2%)
    pallas_call x1, Pallas kernels, bring_home(): pl.pallas_call(home_kernel, out_shape=jax.ShapeDtypeStruct((halves, paths...  129 us
    all_to_all x1, blocking collectives, exchange(): lax.all_to_all(blocks, 'path', split_axis=0, concat_axis=0, tiled=True)  102 us
    all_to_all x3, waiting for transfers between devices, exchange(): lax.all_to_all(blocks, 'path', split_axis=0, concat_axis=0, tiled=True)  74.4 us
    all_gather x1, waiting for transfers between devices, shards(): tokens_all = lax.all_gather(inputs, 'fsdp', axis=0, tiled=True)  42.1 us
    all_gather x1, waiting for transfers between devices, shards(): grads_all = lax.all_gather(cotangent, 'fsdp', axis=0, tiled=True)  34.3 us
    all_to_all x3, starting transfers between devices, exchange(): lax.all_to_all(blocks, 'path', split_axis=0, concat_axis=0, tiled=True)  25.1 us
    pallas_call x2, Pallas kernels, outer(): pl.pallas_call(functools.partial(outer_kernel, half), out_shape=(jax.Shap...  24.9 us
    pallas_call x1, Pallas kernels, delta_up(): pl.pallas_call(functools.partial(up_kernel, scales, 256, 2), out_shape=ja...  22.4 us
  transfers between devices with their start and end apart: 5, of which 5 were waited for; matrix products, arithmetic and copies ran while one was open for 2% of the time, Pallas kernels for 8%

profile of v1, /device:TPU:1, one launch (start us, length us, event | category | flops | bytes accessed | tf_op | source)
XLA Modules:
  0.0 499.0 jit_solution(1799415045368657546)
XLA Ops:
  7.2 0.0 all-gather.5.cloned.1.call-start
  7.2 0.7 all-gather.5.cloned.1.call-update
  7.9 3.2 pick.1
  11.1 13.4 %all-to-all-start = ((bf16[64,2,16,1024]{3,2,1,0:T(8,128)(2,1)}), bf16[64,2,16,1024]{3,2,1,0:T(8,128)(2,1)}, u32[]{:S(2)}, u32[]{:S(2)}) async-start(bf16[64,2,16,1024]{3,2,1,0:T(8,128)(2,1)} %pick.1), calls=%async_computation | async-start | bytes 8388608 | tf_op jit(solution)/shard_map/all_to_all | solution.py:319
  24.5 0.0 all-gather.3.cloned.1.call-start
  24.5 0.7 all-gather.3.cloned.1.call-update
  25.2 34.3 %all-gather.5.cloned.1.call-done.grads = bf16[1760,1024]{1,0:T(8,128)(2,1)} async-done(((bf16[440,1024]{1,0:T(8,128)(2,1)}), bf16[1760,1024]{1,0:T(8,128)(2,1)}) %all-gather.5.cloned.1.call-update) | async-done | bytes 3604496 | tf_op jit(solution)/shard_map/all_gather | solution.py:325
  59.5 5.9 %copy.15.grads_t = bf16[1024,1760]{1,0:T(8,128)(2,1)} copy(bf16[1024,1760]{0,1:T(8,128)(2,1)} %bitcast.6) | data formatting | bytes 7208960 | tf_op jit(solution)/shard_map/transpose | solution.py:335
  65.4 42.1 %all-gather.3.cloned.1.call-done.tokens = bf16[1760,1024]{1,0:T(8,128)(2,1)} async-done(((bf16[440,1024]{1,0:T(8,128)(2,1)}), bf16[1760,1024]{1,0:T(8,128)(2,1)}) %all-gather.3.cloned.1.call-update) | async-done | bytes 3604496 | tf_op jit(solution)/shard_map/all_gather | solution.py:326
  107.6 12.8 %all-to-all-done.arrived = bf16[64,2,16,1024]{3,2,1,0:T(8,128)(2,1)} async-done(((bf16[64,2,16,1024]{3,2,1,0:T(8,128)(2,1)}), bf16[64,2,16,1024]{3,2,1,0:T(8,128)(2,1)}, u32[]{:S(2)}, u32[]{:S(2)}) %all-to-all-start) | async-done | bytes 4194336 | tf_op jit(solution)/shard_map/all_to_all | solution.py:319
  120.4 14.2 %delta_down.1.earlier = bf16[64,16,1024]{2,1,0:T(8,128)(2,1)} custom-call(s32[64]{0:T(128)} %owner.5, bf16[64,2,16,1024]{3,2,1,0:T(8,128)(2,1)} %all-to-all-done.arrived, bf16[1760,1024]{1,0:T(8,128)(2,1)} %all-gather.3.cloned.1.call-done.tokens, bf16[1024,1760]{1,0:T(8,128)(2,1)} %copy.15.grads_t), custom_call_target="tpu_custom_call" | custom-call | flops 7381975040 | bytes 22806528 | tf_op jit(solution)/shard_map/delta_down/pallas_call | solution.py:169
  134.5 5.7 %all-to-all-start.2 = ((bf16[64,16,1024]{2,1,0:T(8,128)(2,1)}), bf16[64,16,1024]{2,1,0:T(8,128)(2,1)S(1)}, u32[]{:S(2)}, u32[]{:S(2)}) async-start(bf16[64,16,1024]{2,1,0:T(8,128)(2,1)} %delta_down.1.earlier), calls=%async_computation.2 | async-start | bytes 4194304 | tf_op jit(solution)/shard_map/all_to_all | solution.py:319
  140.3 5.8 %copy.14 = bf16[1760,1024]{0,1:T(8,128)(2,1)} copy(bf16[1760,1024]{1,0:T(8,128)(2,1)} %all-gather.3.cloned.1.call-done.tokens) | data formatting | bytes 7208960 | tf_op jit(solution)/shard_map/all_gather | solution.py:326
  146.1 22.4 %delta_up.1 = bf16[64,16,1024]{2,1,0:T(8,128)(2,1)} custom-call(s32[64]{0:T(128)} %owner.5, bf16[64,2,16,1024]{3,2,1,0:T(8,128)(2,1)} %all-to-all-done.arrived, bf16[1760,1024]{1,0:T(8,128)(2,1)} %all-gather.3.cloned.1.call-done.tokens, bf16[1760,1024]{1,0:T(8,128)(2,1)} %all-gather.5.cloned.1.call-done.grads, bf16[1024,1760]{1,0:T(8,128)(2,1)} %bitcast.5, ...), custom_call_target="tpu_custom_call" | custom-call | flops 11072962560 | bytes 34209792 | tf_op jit(solution)/shard_map/delta_up/pallas_call | solution.py:192
  168.6 23.0 %all-to-all-done.2.received = bf16[64,16,1024]{2,1,0:T(8,128)(2,1)S(1)} async-done(((bf16[64,16,1024]{2,1,0:T(8,128)(2,1)}), bf16[64,16,1024]{2,1,0:T(8,128)(2,1)S(1)}, u32[]{:S(2)}, u32[]{:S(2)}) %all-to-all-start.2) | async-done | bytes 2097184 | tf_op jit(solution)/shard_map/all_to_all | solution.py:319
  191.5 0.0 copy-start
  191.5 6.0 %all-to-all-start.1 = ((bf16[64,16,1024]{2,1,0:T(8,128)(2,1)}), bf16[64,16,1024]{2,1,0:T(8,128)(2,1)}, u32[]{:S(2)}, u32[]{:S(2)}) async-start(bf16[64,16,1024]{2,1,0:T(8,128)(2,1)} %delta_up.1), calls=%async_computation.1 | async-start | bytes 4194304 | tf_op jit(solution)/shard_map/all_to_all | solution.py:319
  197.6 0.0 copy-done
  197.6 12.5 %outer.2 = (f32[16,2,16,1024]{3,2,1,0:T(8,128)}, bf16[64,2,16,1024]{3,2,1,0:T(8,128)(2,1)}) custom-call(s32[64]{0:T(128)} %bitcast.8, bf16[64,16,1024]{2,1,0:T(8,128)(2,1)} %copy-done, bf16[16,2,16,1024]{3,2,1,0:T(8,128)(2,1)} %master.3, f32[16,2,16,1024]{3,2,1,0:T(8,128)} %momentum.3), custom_call_target="tpu_custom_call" | custom-call | flops 1048576 | bytes 4194304 | tf_op jit(solution)/shard_map/outer/pallas_call | solution.py:269
  210.0 38.7 %all-to-all-done.1.received = bf16[64,16,1024]{2,1,0:T(8,128)(2,1)} async-done(((bf16[64,16,1024]{2,1,0:T(8,128)(2,1)}), bf16[64,16,1024]{2,1,0:T(8,128)(2,1)}, u32[]{:S(2)}, u32[]{:S(2)}) %all-to-all-start.1) | async-done | bytes 2097184 | tf_op jit(solution)/shard_map/all_to_all | solution.py:319
  248.7 12.5 %outer.3 = (f32[16,2,16,1024]{3,2,1,0:T(8,128)}, bf16[64,2,16,1024]{3,2,1,0:T(8,128)(2,1)}) custom-call(s32[64]{0:T(128)} %bitcast.9, bf16[64,16,1024]{2,1,0:T(8,128)(2,1)} %all-to-all-done.1.received, bf16[16,2,16,1024]{3,2,1,0:T(8,128)(2,1)} %master.3, f32[16,2,16,1024]{3,2,1,0:T(8,128)} %momentum.3, ...), custom_call_target="tpu_custom_call", output_to_operand_aliasing={{0}: (4, {}), {1}: (5, {})} | custom-call | flops 1048576 | bytes 4194304 | tf_op jit(solution)/shard_map/outer/pallas_call | solution.py:269
  261.2 102.1 %all_to_all.20.back = bf16[64,2,16,1024]{3,2,1,0:T(8,128)(2,1)} all-to-all(bf16[64,2,16,1024]{3,2,1,0:T(8,128)(2,1)} %get-tuple-element.9), channel_id=1, replica_groups=mesh['path'=64,'fsdp'=4] {'path'}, dimensions={0} | all-to-all | bytes 8388608 | tf_op jit(solution)/shard_map/all_to_all | solution.py:319
  363.3 128.8 %bring_home.1 = bf16[2,64,16,1024]{3,2,1,0:T(8,128)(2,1)} custom-call(s32[64]{0:T(128)} %owner.5, bf16[64,2,16,1024]{3,2,1,0:T(8,128)(2,1)} %all_to_all.20.back), custom_call_target="tpu_custom_call" | custom-call | bytes 8388608 | tf_op jit(solution)/shard_map/bring_home/pallas_call | solution.py:306
Async XLA Ops:
  7.2 52.4 %all-gather.5.cloned.1.call-start = ((), (), s32[]{:S(2)}) async-start(), calls=%async_computation.5 | async-start | bytes 4505600 | tf_op jit(solution)/shard_map/all_gather | solution.py:325
  11.1 109.3 %all-to-all-start = ((bf16[64,2,16,1024]{3,2,1,0:T(8,128)(2,1)}), bf16[64,2,16,1024]{3,2,1,0:T(8,128)(2,1)}, u32[]{:S(2)}, u32[]{:S(2)}) async-start(bf16[64,2,16,1024]{3,2,1,0:T(8,128)(2,1)} %pick.1), calls=%async_computation | async-start | bytes 8388608 | tf_op jit(solution)/shard_map/all_to_all | solution.py:319
  24.5 83.1 %all-gather.3.cloned.1.call-start = ((), (), s32[]{:S(2)}) async-start(), calls=%async_computation.4 | async-start | bytes 4505600 | tf_op jit(solution)/shard_map/all_gather | solution.py:326
  134.5 57.0 %all-to-all-start.2 = ((bf16[64,16,1024]{2,1,0:T(8,128)(2,1)}), bf16[64,16,1024]{2,1,0:T(8,128)(2,1)S(1)}, u32[]{:S(2)}, u32[]{:S(2)}) async-start(bf16[64,16,1024]{2,1,0:T(8,128)(2,1)} %delta_down.1.earlier), calls=%async_computation.2 | async-start | bytes 4194304 | tf_op jit(solution)/shard_map/all_to_all | solution.py:319
  191.5 6.0 %copy-start = (bf16[64,16,1024]{2,1,0:T(8,128)(2,1)}, bf16[64,16,1024]{2,1,0:T(8,128)(2,1)S(1)}, u32[]{:S(2)}) copy-start(bf16[64,16,1024]{2,1,0:T(8,128)(2,1)S(1)} %all-to-all-done.2.received) | copy-start | bytes 6291460
  191.5 57.2 %all-to-all-start.1 = ((bf16[64,16,1024]{2,1,0:T(8,128)(2,1)}), bf16[64,16,1024]{2,1,0:T(8,128)(2,1)}, u32[]{:S(2)}, u32[]{:S(2)}) async-start(bf16[64,16,1024]{2,1,0:T(8,128)(2,1)} %delta_up.1), calls=%async_computation.1 | async-start | bytes 4194304 | tf_op jit(solution)/shard_map/all_to_all | solution.py:319
Sparse Core Ops, SparseCore 0:
  9.8 49.6 all-gather.4
  61.3 46.1 all-gather.2

commit v2 on v1

--- a/solution.py
+++ b/solution.py
@@ -210,34 +210,11 @@
     )(owner, arrived, tokens, grads, tokens_t, earlier)
 
 
-def outer_step(module_of, received, master, momentum, state, updated, total):
-    modules = total.shape[0]
-    paths = received.shape[0]
-    total[...] = jnp.zeros_like(total)
-
-    @pl.loop(0, paths)
-    def _(path):
-        total[module_of[path]] += received[path].astype(jnp.float32)
-
-    @pl.loop(0, modules)
-    def _(module):
-        count = lax.fori_loop(
-            0, paths, lambda p, n: n + (module_of[p] == module).astype(jnp.int32), 0
-        )
-        averaged = total[module] / jnp.full(total.shape[1:], count, jnp.int32).astype(jnp.float32)
-        new = outer_decay * momentum[module] + averaged
-        state[module] = new
-        weights = master[module].astype(jnp.float32)
-        updated[module] = (weights - outer_rate * (averaged + outer_decay * new)).astype(
-            jnp.bfloat16
-        )
-
-
-def outer_kernel(
-    half, module_of, received, master, momentum, *refs,
-):
+def outer_kernel(half, module_of, order, received, master, momentum, *refs):
     refs = refs[2:] if half == 0 else refs
-    new_state, sending, got, mas, mom, state, updated, total, sems = refs
+    new_state, sending, got, mas, mom, state, updated, first, sems = refs
+    modules, rows, cols = state.shape
+    paths = got.shape[0]
     copies = [
         pltpu.make_async_copy(received, got, sems.at[0]),
         pltpu.make_async_copy(master.at[:, half], mas, sems.at[1]),
@@ -245,34 +222,59 @@
     ]
     for copy in copies:
         copy.start()
+
+    for module in range(modules + 1):
+        first[module] = 0
+
+    @pl.loop(0, paths)
+    def _(path):
+        first[module_of[path] + 1] += 1
+
+    for module in range(modules):
+        first[module + 1] += first[module]
     for copy in copies:
         copy.wait()
-    outer_step(module_of, got, mas, mom, state, updated, total)
-
-    @pl.loop(0, sending.shape[0])
-    def _(path):
-        pltpu.make_async_copy(
-            updated.at[module_of[path]], sending.at[path, half], sems.at[3]
-        ).start()
-
-    store = pltpu.make_async_copy(state, new_state.at[:, half], sems.at[4])
-    store.start()
+
+    @pl.loop(0, modules)
+    def _(module):
+        begin, end = first[module], first[module + 1]
+        total = lax.fori_loop(
+            begin,
+            end,
+            lambda i, acc: acc + got[order[i]].astype(jnp.float32),
+            jnp.zeros((rows, cols), jnp.float32),
+        )
+        averaged = total / jnp.full((rows, cols), end - begin, jnp.int32).astype(jnp.float32)
+        new = outer_decay * mom[module] + averaged
+        state[module] = new
+        pltpu.make_async_copy(state.at[module], new_state.at[module, half], sems.at[4]).start()
+        weights = mas[module].astype(jnp.float32)
+        updated[module] = (weights - outer_rate * (averaged + outer_decay * new)).astype(
+            jnp.bfloat16
+        )
+
+        @pl.loop(begin, end)
+        def _(i):
+            pltpu.make_async_copy(
+                updated.at[module], sending.at[order[i], half], sems.at[3]
+            ).start()
+
     wait_bytes(got, sems.at[3])
-    store.wait()
-
-
-def outer(half, module_of, received, master, momentum, earlier):
+    wait_bytes(state, sems.at[4])
+
+
+def outer(half, module_of, order, received, master, momentum, earlier):
     paths, rows, cols = received.shape
     modules = master.shape[0]
     f32, bf16 = jnp.float32, jnp.bfloat16
-    operands = (module_of, received, master, momentum) + earlier
+    operands = (module_of, order, received, master, momentum) + earlier
     return pl.pallas_call(
         functools.partial(outer_kernel, half),
         out_shape=(
             jax.ShapeDtypeStruct(momentum.shape, f32),
             jax.ShapeDtypeStruct((paths, 2, rows, cols), bf16),
         ),
-        in_specs=[SMEM] + [ANY] * (len(operands) - 1),
+        in_specs=[SMEM, SMEM] + [ANY] * (len(operands) - 2),
         out_specs=(ANY, ANY),
         scratch_shapes=[
             pltpu.VMEM((paths, rows, cols), bf16),
@@ -280,35 +282,54 @@
             pltpu.VMEM((modules, rows, cols), f32),
             pltpu.VMEM((modules, rows, cols), f32),
             pltpu.VMEM((modules, rows, cols), bf16),
-            pltpu.VMEM((modules, rows, cols), f32),
+            pltpu.SMEM((modules + 1,), jnp.int32),
             pltpu.SemaphoreType.DMA((5,)),
         ],
-        input_output_aliases={4: 0, 5: 1} if earlier else {},
+        input_output_aliases={5: 0, 6: 1} if earlier else {},
         compiler_params=params(),
         cost_estimate=cost(paths * rows * cols, 4 * paths * rows * cols),
         name="outer",
     )(*operands)
 
 
-def home_kernel(owner, back, out, sem):
-    @pl.loop(0, back.shape[0])
-    def _(block):
-        for half in range(2):
+def home_kernel(groups, owner, back, out, buf, sems):
+    halves, blocks = out.shape[:2]
+    per = blocks // groups
+    parts = [(half, pl.ds(g * per, per)) for half in range(halves) for g in range(groups)]
+    for i, (half, part) in enumerate(parts):
+
+        @pl.loop(0, per)
+        def _(step):
+            block = part.start + step
             pltpu.make_async_copy(
-                back.at[owner[block], half], out.at[half, block], sem
+                back.at[owner[block], half], buf.at[half, block], sems.at[i]
             ).start()
 
-    wait_bytes(out, sem)
+    stores = []
+    for i, (half, part) in enumerate(parts):
+        wait_bytes(buf.at[half, part], sems.at[i])
+        store = pltpu.make_async_copy(
+            buf.at[half, part], out.at[half, part], sems.at[len(parts) + i]
+        )
+        store.start()
+        stores.append(store)
+    for store in stores:
+        store.wait()
 
 
 def bring_home(owner, back):
     paths, halves, rows, cols = back.shape
-    return pl.pallas_call(
-        home_kernel,
-        out_shape=jax.ShapeDtypeStruct((halves, paths, rows, cols), back.dtype),
+    shape = (halves, paths, rows, cols)
+    groups = 4
+    return pl.pallas_call(
+        functools.partial(home_kernel, groups),
+        out_shape=jax.ShapeDtypeStruct(shape, back.dtype),
         in_specs=[SMEM, ANY],
         out_specs=ANY,
-        scratch_shapes=[pltpu.SemaphoreType.DMA],
+        scratch_shapes=[
+            pltpu.VMEM(shape, back.dtype),
+            pltpu.SemaphoreType.DMA((2 * halves * groups,)),
+        ],
         compiler_params=params(),
         cost_estimate=cost(0, 4 * paths * halves * rows * cols),
         name="bring_home",
@@ -322,6 +343,7 @@
 def shards(inputs, cotangent, master, momentum, sharing, block_owner):
     block_cols = master.shape[3]
     module_of = sharing[:, 0]
+    order = jnp.argsort(module_of)
     grads_all = lax.all_gather(cotangent, "fsdp", axis=0, tiled=True)
     tokens_all = lax.all_gather(inputs, "fsdp", axis=0, tiled=True)
     tok_rows, model_width = tokens_all.shape
@@ -336,8 +358,8 @@
     got_down = exchange(down)
     up = delta_up(scales, block_owner, arrived, tokens_all, grads_all, tokens_all.T, down)
     got_up = exchange(up)
-    earlier = outer(1, module_of, got_down, master, momentum, ())
-    new_state, sending = outer(0, module_of, got_up, master, momentum, tuple(earlier))
+    earlier = outer(1, module_of, order, got_down, master, momentum, ())
+    new_state, sending = outer(0, module_of, order, got_up, master, momentum, tuple(earlier))
     own_module = bring_home(block_owner, exchange(sending))
     return (new_state, own_module.reshape(1, 2, model_width, block_cols))
 

time: 500 us -> 368 us (0.74)
  Pallas kernels: 194 us -> 54.4 us
  waiting for transfers between devices: 152 us -> 158 us
    pallas_call x1, Pallas kernels: 129 us -> 4.53 us  [bring_home(): pl.pallas_call(functools.partial(home_kernel, groups), out_shape=jax.Shap...]
    pallas_call x2, Pallas kernels: 24.9 us -> 10.1 us  [outer(): pl.pallas_call(functools.partial(outer_kernel, half), out_shape=(jax.Shap...]
    all_to_all x3, waiting for transfers between devices: 74.4 us -> 79.8 us  [exchange(): lax.all_to_all(blocks, 'path', split_axis=0, concat_axis=0, tiled=True)]
  transfers between devices with their start and end apart: 5 -> 5, of which waited for: 5 -> 5; matrix products, arithmetic and copies ran while one was open for 2% -> 4% of each run, Pallas kernels for 8% -> 8%
where the time goes in v2:
time: 368 us; the launch traced here: 367 us
  waiting for transfers between devices  158 us (43%)
  blocking collectives  102 us (28%)
  Pallas kernels  54.4 us (15%)
  starting transfers between devices  25.2 us (7%)
  between operations  14.1 us (4%)
  local copies, waits for them, and re-layouts  11.8 us (3%)
    all_to_all x1, blocking collectives, exchange(): lax.all_to_all(blocks, 'path', split_axis=0, concat_axis=0, tiled=True)  102 us
    all_to_all x3, waiting for transfers between devices, exchange(): lax.all_to_all(blocks, 'path', split_axis=0, concat_axis=0, tiled=True)  79.8 us
    all_gather x1, waiting for transfers between devices, shards(): tokens_all = lax.all_gather(inputs, 'fsdp', axis=0, tiled=True)  42.1 us
    all_gather x1, waiting for transfers between devices, shards(): grads_all = lax.all_gather(cotangent, 'fsdp', axis=0, tiled=True)  34.3 us
    all_to_all x3, starting transfers between devices, exchange(): lax.all_to_all(blocks, 'path', split_axis=0, concat_axis=0, tiled=True)  25.1 us
    pallas_call x1, Pallas kernels, delta_up(): pl.pallas_call(functools.partial(up_kernel, scales, 256, 2), out_shape=ja...  22.5 us
    pallas_call x1, Pallas kernels, delta_down(): pl.pallas_call(functools.partial(down_kernel, scales, 256, 2), out_shape=...  14.2 us
    pallas_call x2, Pallas kernels, outer(): pl.pallas_call(functools.partial(outer_kernel, half), out_shape=(jax.Shap...  10.1 us
  transfers between devices with their start and end apart: 5, of which 5 were waited for; matrix products, arithmetic and copies ran while one was open for 4% of the time, Pallas kernels for 8%

profile of v2, /device:TPU:1, one launch (start us, length us, event | category | flops | bytes accessed | tf_op | source)
XLA Modules:
  0.0 367.3 jit_solution(1144182110850376176)
XLA Ops:
  7.2 0.0 all-gather.5.cloned.1.call-start
  7.2 0.7 all-gather.5.cloned.1.call-update
  7.9 3.2 pick.1
  11.1 13.4 %all-to-all-start = ((bf16[64,2,16,1024]{3,2,1,0:T(8,128)(2,1)}), bf16[64,2,16,1024]{3,2,1,0:T(8,128)(2,1)}, u32[]{:S(2)}, u32[]{:S(2)}) async-start(bf16[64,2,16,1024]{3,2,1,0:T(8,128)(2,1)} %pick.1), calls=%async_computation | async-start | bytes 8388608 | tf_op jit(solution)/shard_map/all_to_all | solution.py:340
  24.5 0.0 all-gather.3.cloned.1.call-start
  24.5 0.7 all-gather.3.cloned.1.call-update
  25.2 34.3 %all-gather.5.cloned.1.call-done.grads = bf16[1760,1024]{1,0:T(8,128)(2,1)} async-done(((bf16[440,1024]{1,0:T(8,128)(2,1)}), bf16[1760,1024]{1,0:T(8,128)(2,1)}) %all-gather.5.cloned.1.call-update) | async-done | bytes 3604496 | tf_op jit(solution)/shard_map/all_gather | solution.py:347
  59.5 5.9 %copy.15.grads_t = bf16[1024,1760]{1,0:T(8,128)(2,1)} copy(bf16[1024,1760]{0,1:T(8,128)(2,1)} %bitcast.6) | data formatting | bytes 7208960 | tf_op jit(solution)/shard_map/transpose | solution.py:357
  65.4 42.1 %all-gather.3.cloned.1.call-done.tokens = bf16[1760,1024]{1,0:T(8,128)(2,1)} async-done(((bf16[440,1024]{1,0:T(8,128)(2,1)}), bf16[1760,1024]{1,0:T(8,128)(2,1)}) %all-gather.3.cloned.1.call-update) | async-done | bytes 3604496 | tf_op jit(solution)/shard_map/all_gather | solution.py:348
  107.6 12.8 %all-to-all-done.arrived = bf16[64,2,16,1024]{3,2,1,0:T(8,128)(2,1)} async-done(((bf16[64,2,16,1024]{3,2,1,0:T(8,128)(2,1)}), bf16[64,2,16,1024]{3,2,1,0:T(8,128)(2,1)}, u32[]{:S(2)}, u32[]{:S(2)}) %all-to-all-start) | async-done | bytes 4194336 | tf_op jit(solution)/shard_map/all_to_all | solution.py:340
  120.4 14.2 %delta_down.1.earlier = bf16[64,16,1024]{2,1,0:T(8,128)(2,1)} custom-call(s32[64]{0:T(128)} %owner.5, bf16[64,2,16,1024]{3,2,1,0:T(8,128)(2,1)} %all-to-all-done.arrived, bf16[1760,1024]{1,0:T(8,128)(2,1)} %all-gather.3.cloned.1.call-done.tokens, bf16[1024,1760]{1,0:T(8,128)(2,1)} %copy.15.grads_t), custom_call_target="tpu_custom_call" | custom-call | flops 7381975040 | bytes 22806528 | tf_op jit(solution)/shard_map/delta_down/pallas_call | solution.py:169
  134.5 5.8 %all-to-all-start.2 = ((bf16[64,16,1024]{2,1,0:T(8,128)(2,1)}), bf16[64,16,1024]{2,1,0:T(8,128)(2,1)S(1)}, u32[]{:S(2)}, u32[]{:S(2)}) async-start(bf16[64,16,1024]{2,1,0:T(8,128)(2,1)} %delta_down.1.earlier), calls=%async_computation.2 | async-start | bytes 4194304 | tf_op jit(solution)/shard_map/all_to_all | solution.py:340
  140.3 5.8 %copy.14 = bf16[1760,1024]{0,1:T(8,128)(2,1)} copy(bf16[1760,1024]{1,0:T(8,128)(2,1)} %all-gather.3.cloned.1.call-done.tokens) | data formatting | bytes 7208960 | tf_op jit(solution)/shard_map/all_gather | solution.py:348
  146.2 22.5 %delta_up.1 = bf16[64,16,1024]{2,1,0:T(8,128)(2,1)} custom-call(s32[64]{0:T(128)} %owner.5, bf16[64,2,16,1024]{3,2,1,0:T(8,128)(2,1)} %all-to-all-done.arrived, bf16[1760,1024]{1,0:T(8,128)(2,1)} %all-gather.3.cloned.1.call-done.tokens, bf16[1760,1024]{1,0:T(8,128)(2,1)} %all-gather.5.cloned.1.call-done.grads, bf16[1024,1760]{1,0:T(8,128)(2,1)} %bitcast.5, ...), custom_call_target="tpu_custom_call" | custom-call | flops 11072962560 | bytes 34209792 | tf_op jit(solution)/shard_map/delta_up/pallas_call | solution.py:192
  168.6 0.0 copy-start.1
  168.6 22.9 %all-to-all-done.2.received = bf16[64,16,1024]{2,1,0:T(8,128)(2,1)S(1)} async-done(((bf16[64,16,1024]{2,1,0:T(8,128)(2,1)}), bf16[64,16,1024]{2,1,0:T(8,128)(2,1)S(1)}, u32[]{:S(2)}, u32[]{:S(2)}) %all-to-all-start.2) | async-done | bytes 2097184 | tf_op jit(solution)/shard_map/all_to_all | solution.py:340
  191.5 6.0 %all-to-all-start.1 = ((bf16[64,16,1024]{2,1,0:T(8,128)(2,1)}), bf16[64,16,1024]{2,1,0:T(8,128)(2,1)}, u32[]{:S(2)}, u32[]{:S(2)}) async-start(bf16[64,16,1024]{2,1,0:T(8,128)(2,1)} %delta_up.1), calls=%async_computation.1 | async-start | bytes 4194304 | tf_op jit(solution)/shard_map/all_to_all | solution.py:340
  197.6 0.0 copy-done.1
  197.6 2.0 sort.17
  199.6 5.0 %outer.2 = (f32[16,2,16,1024]{3,2,1,0:T(8,128)}, bf16[64,2,16,1024]{3,2,1,0:T(8,128)(2,1)}) custom-call(s32[64]{0:T(128)} %bitcast.8, s32[64]{0:T(128)} %get-tuple-element.7.order, bf16[64,16,1024]{2,1,0:T(8,128)(2,1)} %copy-done, bf16[16,2,16,1024]{3,2,1,0:T(8,128)(2,1)} %master.3, f32[16,2,16,1024]{3,2,1,0:T(8,128)} %momentum.3), custom_call_target="tpu_custom_call" | custom-call | flops 1048576 | bytes 4194304 | tf_op jit(solution)/shard_map/outer/pallas_call | solution.py:271
  204.7 44.1 %all-to-all-done.1.received = bf16[64,16,1024]{2,1,0:T(8,128)(2,1)} async-done(((bf16[64,16,1024]{2,1,0:T(8,128)(2,1)}), bf16[64,16,1024]{2,1,0:T(8,128)(2,1)}, u32[]{:S(2)}, u32[]{:S(2)}) %all-to-all-start.1) | async-done | bytes 2097184 | tf_op jit(solution)/shard_map/all_to_all | solution.py:340
  248.7 5.0 %outer.3 = (f32[16,2,16,1024]{3,2,1,0:T(8,128)}, bf16[64,2,16,1024]{3,2,1,0:T(8,128)(2,1)}) custom-call(s32[64]{0:T(128)} %bitcast.9, s32[64]{0:T(128)} %get-tuple-element.7.order, bf16[64,16,1024]{2,1,0:T(8,128)(2,1)} %all-to-all-done.1.received, bf16[16,2,16,1024]{3,2,1,0:T(8,128)(2,1)} %master.3, ...), custom_call_target="tpu_custom_call", output_to_operand_aliasing={{0}: (5, {}), {1}: (6, {})} | custom-call | flops 1048576 | bytes 4194304 | tf_op jit(solution)/shard_map/outer/pallas_call | solution.py:271
  253.8 102.1 %all_to_all.20.back = bf16[64,2,16,1024]{3,2,1,0:T(8,128)(2,1)} all-to-all(bf16[64,2,16,1024]{3,2,1,0:T(8,128)(2,1)} %get-tuple-element.11), channel_id=1, replica_groups=mesh['path'=64,'fsdp'=4] {'path'}, dimensions={0} | all-to-all | bytes 8388608 | tf_op jit(solution)/shard_map/all_to_all | solution.py:340
  355.9 4.5 %bring_home.1 = bf16[2,64,16,1024]{3,2,1,0:T(8,128)(2,1)} custom-call(s32[64]{0:T(128)} %owner.5, bf16[64,2,16,1024]{3,2,1,0:T(8,128)(2,1)} %all_to_all.20.back), custom_call_target="tpu_custom_call" | custom-call | bytes 8388608 | tf_op jit(solution)/shard_map/bring_home/pallas_call | solution.py:324
  (3 shorter events, 0.0 us)
Async XLA Ops:
  7.2 52.4 %all-gather.5.cloned.1.call-start = ((), (), s32[]{:S(2)}) async-start(), calls=%async_computation.5 | async-start | bytes 4505600 | tf_op jit(solution)/shard_map/all_gather | solution.py:347
  11.1 109.3 %all-to-all-start = ((bf16[64,2,16,1024]{3,2,1,0:T(8,128)(2,1)}), bf16[64,2,16,1024]{3,2,1,0:T(8,128)(2,1)}, u32[]{:S(2)}, u32[]{:S(2)}) async-start(bf16[64,2,16,1024]{3,2,1,0:T(8,128)(2,1)} %pick.1), calls=%async_computation | async-start | bytes 8388608 | tf_op jit(solution)/shard_map/all_to_all | solution.py:340
  24.5 83.1 %all-gather.3.cloned.1.call-start = ((), (), s32[]{:S(2)}) async-start(), calls=%async_computation.4 | async-start | bytes 4505600 | tf_op jit(solution)/shard_map/all_gather | solution.py:348
  134.5 57.0 %all-to-all-start.2 = ((bf16[64,16,1024]{2,1,0:T(8,128)(2,1)}), bf16[64,16,1024]{2,1,0:T(8,128)(2,1)S(1)}, u32[]{:S(2)}, u32[]{:S(2)}) async-start(bf16[64,16,1024]{2,1,0:T(8,128)(2,1)} %delta_down.1.earlier), calls=%async_computation.2 | async-start | bytes 4194304 | tf_op jit(solution)/shard_map/all_to_all | solution.py:340
  168.6 29.0 %copy-start.1 = (s32[64,1]{0,1:T(1,128)S(1)}, s32[64,1]{0,1:T(1,128)}, u32[]{:S(2)}) copy-start(s32[64,1]{0,1:T(1,128)} %param.10) | copy-start | bytes 772
  191.5 8.1 %copy-start = (bf16[64,16,1024]{2,1,0:T(8,128)(2,1)}, bf16[64,16,1024]{2,1,0:T(8,128)(2,1)S(1)}, u32[]{:S(2)}) copy-start(bf16[64,16,1024]{2,1,0:T(8,128)(2,1)S(1)} %all-to-all-done.2.received) | copy-start | bytes 6291460
  191.5 57.2 %all-to-all-start.1 = ((bf16[64,16,1024]{2,1,0:T(8,128)(2,1)}), bf16[64,16,1024]{2,1,0:T(8,128)(2,1)}, u32[]{:S(2)}, u32[]{:S(2)}) async-start(bf16[64,16,1024]{2,1,0:T(8,128)(2,1)} %delta_up.1), calls=%async_computation.1 | async-start | bytes 4194304 | tf_op jit(solution)/shard_map/all_to_all | solution.py:340
Sparse Core Ops, SparseCore 0:
  9.8 49.6 all-gather.4
  61.3 46.1 all-gather.2

commit v3 on v2

--- a/solution.py
+++ b/solution.py
@@ -167,7 +167,7 @@
     count, width = tokens.shape
     bf16 = jnp.bfloat16
     return pl.pallas_call(
-        functools.partial(down_kernel, scales, 256, 2),
+        functools.partial(down_kernel, scales, 512, 2),
         out_shape=jax.ShapeDtypeStruct((paths, rows, cols), bf16),
         in_specs=[SMEM, ANY, ANY, ANY],
         out_specs=ANY,
@@ -190,7 +190,7 @@
     count, width = tokens.shape
     bf16 = jnp.bfloat16
     return pl.pallas_call(
-        functools.partial(up_kernel, scales, 256, 2),
+        functools.partial(up_kernel, scales, 512, 2),
         out_shape=jax.ShapeDtypeStruct((paths, rows, cols), bf16),
         in_specs=[SMEM, ANY, ANY, ANY, ANY, ANY],
         out_specs=ANY,
@@ -336,6 +336,22 @@
     )(owner, back)
 
 
+def collect(tokens, grads):
+    count = lax.axis_size("fsdp")
+    right = [(i, (i + 1) % count) for i in range(count)]
+    left = [(i, (i - 1) % count) for i in range(count)]
+    tok_left = lax.ppermute(tokens, "fsdp", right)
+    grd_right = lax.ppermute(grads, "fsdp", left)
+    grd_left = lax.ppermute(grads, "fsdp", right)
+    tok_right = lax.ppermute(tokens, "fsdp", left)
+    grd_far = lax.ppermute(grd_right, "fsdp", left)
+    tok_far = lax.ppermute(tok_left, "fsdp", right)
+    return (
+        jnp.concatenate([tokens, tok_left, tok_right, tok_far]),
+        jnp.concatenate([grads, grd_left, grd_right, grd_far]),
+    )
+
+
 def exchange(blocks):
     return lax.all_to_all(blocks, "path", split_axis=0, concat_axis=0, tiled=True)
 
@@ -344,8 +360,7 @@
     block_cols = master.shape[3]
     module_of = sharing[:, 0]
     order = jnp.argsort(module_of)
-    grads_all = lax.all_gather(cotangent, "fsdp", axis=0, tiled=True)
-    tokens_all = lax.all_gather(inputs, "fsdp", axis=0, tiled=True)
+    tokens_all, grads_all = collect(inputs, cotangent)
     tok_rows, model_width = tokens_all.shape
     hidden_units = block_cols * lax.axis_size("fsdp")
     scales = (

time: 368 us -> 355 us (0.965)
  waiting for transfers between devices: 158 us -> 131 us
  local copies, waits for them, and re-layouts: 11.8 us -> 33 us
  between operations: 14.1 us -> 0.94 us
  starting transfers between devices: 25.2 us -> 32.2 us
    all_gather x2 -> x0, waiting for transfers between devices: 76.4 us -> none  [the longest x1 42.1 us: shards(): tokens_all = lax.all_gather(inputs, 'fsdp', axis=0, tiled=True)]
    ppermute x0 -> x6, waiting for transfers between devices: none -> 44.2 us  [the longest x1 18.2 us: collect(): tok_left = lax.ppermute(tokens, 'fsdp', right)]
    concatenate x0 -> x3, local copies, waits for them, and re-layouts: none -> 14.8 us  [the longest x2 12.6 us: collect(): jnp.concatenate([tokens, tok_left, tok_right, tok_far])]
    all_to_all x3, waiting for transfers between devices: 79.8 us -> 87 us  [exchange(): lax.all_to_all(blocks, 'path', split_axis=0, concat_axis=0, tiled=True)]
    unnamed x4 -> x10, local copies, waits for them, and re-layouts: 0.01 us -> 7.04 us
    ppermute x0 -> x6, starting transfers between devices: none -> 6.9 us  [the longest x1 2.67 us: collect(): grd_far = lax.ppermute(grd_right, 'fsdp', left)]
    all_gather x1 -> x0, local copies, waits for them, and re-layouts: 5.85 us -> none  [shards(): tokens_all = lax.all_gather(inputs, 'fsdp', axis=0, tiled=True)]
    ppermute x0 -> x3, local copies, waits for them, and re-layouts: none -> 5.15 us  [the longest x1 2.24 us: collect(): tok_far = lax.ppermute(tok_left, 'fsdp', right)]
  transfers between devices with their start and end apart: 5 -> 9, of which waited for: 5 -> 6; matrix products, arithmetic and copies ran while one was open for 4% -> 10% of each run, Pallas kernels for 8% -> 7%
where the time goes in v3:
time: 355 us; the launch traced here: 353 us
  waiting for transfers between devices  131 us (37%)
  blocking collectives  102 us (29%)
  Pallas kernels  51.7 us (15%)
  local copies, waits for them, and re-layouts  33 us (9%)
  starting transfers between devices  32.2 us (9%)
    all_to_all x1, blocking collectives, exchange(): lax.all_to_all(blocks, 'path', split_axis=0, concat_axis=0, tiled=True)  102 us
    all_to_all x3, waiting for transfers between devices, exchange(): lax.all_to_all(blocks, 'path', split_axis=0, concat_axis=0, tiled=True)  87 us
    all_to_all x3, starting transfers between devices, exchange(): lax.all_to_all(blocks, 'path', split_axis=0, concat_axis=0, tiled=True)  25.3 us
    pallas_call x1, Pallas kernels, delta_up(): pl.pallas_call(functools.partial(up_kernel, scales, 512, 2), out_shape=ja...  20 us
    ppermute x1, waiting for transfers between devices, collect(): tok_left = lax.ppermute(tokens, 'fsdp', right)  18.2 us
    pallas_call x1, Pallas kernels, delta_down(): pl.pallas_call(functools.partial(down_kernel, scales, 512, 2), out_shape=...  13.9 us
    ppermute x1, waiting for transfers between devices, collect(): tok_far = lax.ppermute(tok_left, 'fsdp', right)  13.6 us
    concatenate x2, local copies, waits for them, and re-layouts, collect(): jnp.concatenate([tokens, tok_left, tok_right, tok_far])  12.6 us
  transfers between devices with their start and end apart: 9, of which 6 were waited for; matrix products, arithmetic and copies ran while one was open for 10% of the time, Pallas kernels for 7%

profile of v3, /device:TPU:1, one launch (start us, length us, event | category | flops | bytes accessed | tf_op | source)
XLA Modules:
  0.0 353.2 jit_solution(16380244514921245583)
XLA Ops:
  0.6 3.2 pick.1
  3.9 13.5 %all-to-all-start = ((bf16[64,2,16,1024]{3,2,1,0:T(8,128)(2,1)}), bf16[64,2,16,1024]{3,2,1,0:T(8,128)(2,1)}, u32[]{:S(2)}, u32[]{:S(2)}) async-start(bf16[64,2,16,1024]{3,2,1,0:T(8,128)(2,1)} %pick.1), calls=%async_computation | async-start | bytes 8388608 | tf_op jit(solution)/shard_map/all_to_all | solution.py:356
  21.6 18.2 %collective-permute-done = bf16[440,1024]{1,0:T(8,128)(2,1)} collective-permute-done((bf16[440,1024]{1,0:T(8,128)(2,1)S(1)}, bf16[440,1024]{1,0:T(8,128)(2,1)}, u32[]{:S(2)}, u32[]{:S(2)}) %collective-permute-start) | collective-permute-done | bytes 901152 | tf_op jit(solution)/shard_map/ppermute | solution.py:343
  39.8 2.7 collective-permute-start.5
  43.0 2.2 constant_dynamic-update-slice_fusion.3
  46.6 12.4 %collective-permute-done.1 = bf16[440,1024]{1,0:T(8,128)(2,1)} collective-permute-done((bf16[440,1024]{1,0:T(8,128)(2,1)S(1)}, bf16[440,1024]{1,0:T(8,128)(2,1)}, u32[]{:S(2)}, u32[]{:S(2)}) %collective-permute-start.1) | collective-permute-done | bytes 901152 | tf_op jit(solution)/shard_map/ppermute | solution.py:346
  60.5 2.2 constant_dynamic-update-slice_fusion.2
  64.8 13.6 %collective-permute-done.2 = bf16[440,1024]{1,0:T(8,128)(2,1)} collective-permute-done((bf16[440,1024]{1,0:T(8,128)(2,1)}, bf16[440,1024]{1,0:T(8,128)(2,1)}, u32[]{:S(2)}, u32[]{:S(2)}) %collective-permute-start.2) | collective-permute-done | bytes 901152 | tf_op jit(solution)/shard_map/ppermute | solution.py:348
  78.4 2.2 copy.19
  80.6 6.7 %concatenate.6 = bf16[1760,1024]{0,1:T(8,128)(2,1)} concatenate(bf16[440,1024]{0,1:T(8,128)(2,1)S(1)} %copy.16, bf16[440,1024]{0,1:T(8,128)(2,1)S(1)} %copy.17, bf16[440,1024]{0,1:T(8,128)(2,1)S(1)} %copy.18, bf16[440,1024]{0,1:T(8,128)(2,1)} %copy.19), dimensions={0} | concatenate | bytes 7208960 | tf_op jit(solution)/shard_map/concatenate | solution.py:350
  87.3 5.9 %copy.22.tokens = bf16[1760,1024]{1,0:T(8,128)(2,1)} copy(bf16[1760,1024]{0,1:T(8,128)(2,1)} %concatenate.6) | data formatting | bytes 7208960 | tf_op jit(solution)/shard_map/concatenate | solution.py:350
  93.3 2.2 constant_dynamic-update-slice_fusion.grads
  95.5 6.0 %copy.21.grads_t = bf16[1024,1760]{1,0:T(8,128)(2,1)} copy(bf16[1024,1760]{0,1:T(8,128)(2,1)} %bitcast.5) | data formatting | bytes 7208960 | tf_op jit(solution)/shard_map/transpose | solution.py:372
  101.4 11.8 %all-to-all-done.arrived = bf16[64,2,16,1024]{3,2,1,0:T(8,128)(2,1)} async-done(((bf16[64,2,16,1024]{3,2,1,0:T(8,128)(2,1)}), bf16[64,2,16,1024]{3,2,1,0:T(8,128)(2,1)}, u32[]{:S(2)}, u32[]{:S(2)}) %all-to-all-start) | async-done | bytes 4194336 | tf_op jit(solution)/shard_map/all_to_all | solution.py:356
  113.2 13.9 %delta_down.1.earlier = bf16[64,16,1024]{2,1,0:T(8,128)(2,1)} custom-call(s32[64]{0:T(128)} %owner.5, bf16[64,2,16,1024]{3,2,1,0:T(8,128)(2,1)} %all-to-all-done.arrived, bf16[1760,1024]{1,0:T(8,128)(2,1)} %copy.22.tokens, bf16[1024,1760]{1,0:T(8,128)(2,1)} %copy.21.grads_t), custom_call_target="tpu_custom_call" | custom-call | flops 7381975040 | bytes 22806528 | tf_op jit(solution)/shard_map/delta_down/pallas_call | solution.py:169
  127.1 5.8 %all-to-all-start.2 = ((bf16[64,16,1024]{2,1,0:T(8,128)(2,1)}), bf16[64,16,1024]{2,1,0:T(8,128)(2,1)S(1)}, u32[]{:S(2)}, u32[]{:S(2)}) async-start(bf16[64,16,1024]{2,1,0:T(8,128)(2,1)} %delta_down.1.earlier), calls=%async_computation.2 | async-start | bytes 4194304 | tf_op jit(solution)/shard_map/all_to_all | solution.py:356
  132.9 20.0 %delta_up.1 = bf16[64,16,1024]{2,1,0:T(8,128)(2,1)} custom-call(s32[64]{0:T(128)} %owner.5, bf16[64,2,16,1024]{3,2,1,0:T(8,128)(2,1)} %all-to-all-done.arrived, bf16[1760,1024]{1,0:T(8,128)(2,1)} %copy.22.tokens, bf16[1760,1024]{1,0:T(8,128)(2,1)} %constant_dynamic-update-slice_fusion.grads, bf16[1024,1760]{1,0:T(8,128)(2,1)} %bitcast.4, ...), custom_call_target="tpu_custom_call" | custom-call | flops 11072962560 | bytes 34209792 | tf_op jit(solution)/shard_map/delta_up/pallas_call | solution.py:192
  152.9 31.2 %all-to-all-done.2.received = bf16[64,16,1024]{2,1,0:T(8,128)(2,1)S(1)} async-done(((bf16[64,16,1024]{2,1,0:T(8,128)(2,1)}), bf16[64,16,1024]{2,1,0:T(8,128)(2,1)S(1)}, u32[]{:S(2)}, u32[]{:S(2)}) %all-to-all-start.2) | async-done | bytes 2097184 | tf_op jit(solution)/shard_map/all_to_all | solution.py:356
  184.1 6.0 %all-to-all-start.1 = ((bf16[64,16,1024]{2,1,0:T(8,128)(2,1)}), bf16[64,16,1024]{2,1,0:T(8,128)(2,1)}, u32[]{:S(2)}, u32[]{:S(2)}) async-start(bf16[64,16,1024]{2,1,0:T(8,128)(2,1)} %delta_up.1), calls=%async_computation.1 | async-start | bytes 4194304 | tf_op jit(solution)/shard_map/all_to_all | solution.py:356
  192.2 5.0 %outer.2 = (f32[16,2,16,1024]{3,2,1,0:T(8,128)}, bf16[64,2,16,1024]{3,2,1,0:T(8,128)(2,1)}) custom-call(s32[64]{0:T(128)} %bitcast.8, s32[64]{0:T(128)} %get-tuple-element.7.order, bf16[64,16,1024]{2,1,0:T(8,128)(2,1)} %copy-done, bf16[16,2,16,1024]{3,2,1,0:T(8,128)(2,1)} %master.3, f32[16,2,16,1024]{3,2,1,0:T(8,128)} %momentum.3), custom_call_target="tpu_custom_call" | custom-call | flops 1048576 | bytes 4194304 | tf_op jit(solution)/shard_map/outer/pallas_call | solution.py:271
  197.3 44.1 %all-to-all-done.1.received = bf16[64,16,1024]{2,1,0:T(8,128)(2,1)} async-done(((bf16[64,16,1024]{2,1,0:T(8,128)(2,1)}), bf16[64,16,1024]{2,1,0:T(8,128)(2,1)}, u32[]{:S(2)}, u32[]{:S(2)}) %all-to-all-start.1) | async-done | bytes 2097184 | tf_op jit(solution)/shard_map/all_to_all | solution.py:356
  241.3 5.0 %outer.3 = (f32[16,2,16,1024]{3,2,1,0:T(8,128)}, bf16[64,2,16,1024]{3,2,1,0:T(8,128)(2,1)}) custom-call(s32[64]{0:T(128)} %bitcast.9, s32[64]{0:T(128)} %get-tuple-element.7.order, bf16[64,16,1024]{2,1,0:T(8,128)(2,1)} %all-to-all-done.1.received, bf16[16,2,16,1024]{3,2,1,0:T(8,128)(2,1)} %master.3, ...), custom_call_target="tpu_custom_call", output_to_operand_aliasing={{0}: (5, {}), {1}: (6, {})} | custom-call | flops 1048576 | bytes 4194304 | tf_op jit(solution)/shard_map/outer/pallas_call | solution.py:271
  246.4 102.1 %all_to_all.20.back = bf16[64,2,16,1024]{3,2,1,0:T(8,128)(2,1)} all-to-all(bf16[64,2,16,1024]{3,2,1,0:T(8,128)(2,1)} %get-tuple-element.11), channel_id=1, replica_groups=mesh['path'=64,'fsdp'=4] {'path'}, dimensions={0} | all-to-all | bytes 8388608 | tf_op jit(solution)/shard_map/all_to_all | solution.py:356
  348.5 4.5 %bring_home.1 = bf16[2,64,16,1024]{3,2,1,0:T(8,128)(2,1)} custom-call(s32[64]{0:T(128)} %owner.5, bf16[64,2,16,1024]{3,2,1,0:T(8,128)(2,1)} %all_to_all.20.back), custom_call_target="tpu_custom_call" | custom-call | bytes 8388608 | tf_op jit(solution)/shard_map/bring_home/pallas_call | solution.py:324
  (20 shorter events, 11.9 us)
Async XLA Ops:
  3.8 13.5 %copy-start.1 = (bf16[440,1024]{1,0:T(8,128)(2,1)S(1)}, bf16[440,1024]{1,0:T(8,128)(2,1)}, u32[]{:S(2)}) copy-start(bf16[440,1024]{1,0:T(8,128)(2,1)} %param.6) | copy-start | bytes 2703364
  3.9 109.4 %all-to-all-start = ((bf16[64,2,16,1024]{3,2,1,0:T(8,128)(2,1)}), bf16[64,2,16,1024]{3,2,1,0:T(8,128)(2,1)}, u32[]{:S(2)}, u32[]{:S(2)}) async-start(bf16[64,2,16,1024]{3,2,1,0:T(8,128)(2,1)} %pick.1), calls=%async_computation | async-start | bytes 8388608 | tf_op jit(solution)/shard_map/all_to_all | solution.py:356
  17.4 22.4 %collective-permute-start = (bf16[440,1024]{1,0:T(8,128)(2,1)S(1)}, bf16[440,1024]{1,0:T(8,128)(2,1)}, u32[]{:S(2)}, u32[]{:S(2)}) collective-permute-start(bf16[440,1024]{1,0:T(8,128)(2,1)S(1)} %copy-done.1), channel_id=1, source_target_pairs={{0,1},{1,2},{2,3},{3,0},{4,5},{5,6},{6,7},{7,4},{8,9},{9,10},{10,1... | collective-permute-start | bytes 2703368 | tf_op jit(solution)/shard_map/ppermute | solution.py:343
  18.6 21.1 %collective-permute-start.4 = (bf16[440,1024]{1,0:T(8,128)(2,1)}, bf16[440,1024]{1,0:T(8,128)(2,1)}, u32[]{:S(2)}, u32[]{:S(2)}) collective-permute-start(bf16[440,1024]{1,0:T(8,128)(2,1)} %param.7), channel_id=1, source_target_pairs={{0,3},{1,0},{2,1},{3,2},{4,7},{5,4},{6,5},{7,6},{8,11},{9,8},{10,9... | collective-permute-start | bytes 2703368 | tf_op jit(solution)/shard_map/ppermute | solution.py:344
  20.1 38.9 %collective-permute-start.1 = (bf16[440,1024]{1,0:T(8,128)(2,1)S(1)}, bf16[440,1024]{1,0:T(8,128)(2,1)}, u32[]{:S(2)}, u32[]{:S(2)}) collective-permute-start(bf16[440,1024]{1,0:T(8,128)(2,1)S(1)} %copy-done.1), channel_id=1, source_target_pairs={{0,3},{1,0},{2,1},{3,2},{4,7},{5,4},{6,5},{7,6},{8,11},{9,8},{10,9... | collective-permute-start | bytes 2703368 | tf_op jit(solution)/shard_map/ppermute | solution.py:346
  21.4 39.1 %collective-permute-start.3 = (bf16[440,1024]{1,0:T(8,128)(2,1)}, bf16[440,1024]{1,0:T(8,128)(2,1)}, u32[]{:S(2)}, u32[]{:S(2)}) collective-permute-start(bf16[440,1024]{1,0:T(8,128)(2,1)} %param.7), channel_id=1, source_target_pairs={{0,1},{1,2},{2,3},{3,0},{4,5},{5,6},{6,7},{7,4},{8,9},{9,10},{10,1... | collective-permute-start | bytes 2703368 | tf_op jit(solution)/shard_map/ppermute | solution.py:345
  39.8 38.6 %collective-permute-start.2 = (bf16[440,1024]{1,0:T(8,128)(2,1)}, bf16[440,1024]{1,0:T(8,128)(2,1)}, u32[]{:S(2)}, u32[]{:S(2)}) collective-permute-start(bf16[440,1024]{1,0:T(8,128)(2,1)} %collective-permute-done), channel_id=1, source_target_pairs={{0,1},{1,2},{2,3},{3,0},{4,5},{5,6},{6,7},{7,4},{8,9},{9,10},{10,1... | collective-permute-start | bytes 2703368 | tf_op jit(solution)/shard_map/ppermute | solution.py:348
  39.8 53.5 %collective-permute-start.5 = (bf16[440,1024]{1,0:T(8,128)(2,1)}, bf16[440,1024]{1,0:T(8,128)(2,1)}, u32[]{:S(2)}, u32[]{:S(2)}) collective-permute-start(bf16[440,1024]{1,0:T(8,128)(2,1)} %collective-permute-done.4), channel_id=1, source_target_pairs={{0,3},{1,0},{2,1},{3,2},{4,7},{5,4},{6,5},{7,6},{8,11},{9,8},{10,9... | collective-permute-start | bytes 2703368 | tf_op jit(solution)/shard_map/ppermute | solution.py:347
  127.1 57.0 %all-to-all-start.2 = ((bf16[64,16,1024]{2,1,0:T(8,128)(2,1)}), bf16[64,16,1024]{2,1,0:T(8,128)(2,1)S(1)}, u32[]{:S(2)}, u32[]{:S(2)}) async-start(bf16[64,16,1024]{2,1,0:T(8,128)(2,1)} %delta_down.1.earlier), calls=%async_computation.2 | async-start | bytes 4194304 | tf_op jit(solution)/shard_map/all_to_all | solution.py:356
  152.9 37.2 %copy-start.2 = (s32[64,1]{0,1:T(1,128)S(1)}, s32[64,1]{0,1:T(1,128)}, u32[]{:S(2)}) copy-start(s32[64,1]{0,1:T(1,128)} %param.10) | copy-start | bytes 772
  184.1 8.1 %copy-start = (bf16[64,16,1024]{2,1,0:T(8,128)(2,1)}, bf16[64,16,1024]{2,1,0:T(8,128)(2,1)S(1)}, u32[]{:S(2)}) copy-start(bf16[64,16,1024]{2,1,0:T(8,128)(2,1)S(1)} %all-to-all-done.2.received) | copy-start | bytes 6291460
  184.1 57.2 %all-to-all-start.1 = ((bf16[64,16,1024]{2,1,0:T(8,128)(2,1)}), bf16[64,16,1024]{2,1,0:T(8,128)(2,1)}, u32[]{:S(2)}, u32[]{:S(2)}) async-start(bf16[64,16,1024]{2,1,0:T(8,128)(2,1)} %delta_up.1), calls=%async_computation.1 | async-start | bytes 4194304 | tf_op jit(solution)/shard_map/all_to_all | solution.py:356

commit v4 on v3

v4 whole, which is shorter than its diff:
```python
import functools
import math

import jax
import jax.numpy as jnp
from jax import lax
from jax.experimental import pallas as pl
from jax.experimental.pallas import tpu as pltpu
from jax.sharding import PartitionSpec as P

inner_rate = 10.0
outer_rate = 0.7
outer_decay = 0.9

VMEM_LIMIT = 56 * 1024 * 1024
FIRST_LIMIT = 24 * 1024 * 1024
ANY = pl.BlockSpec(memory_space=pl.ANY)
SMEM = pl.BlockSpec(memory_space=pltpu.SMEM)
VMEM = pl.BlockSpec(memory_space=pltpu.VMEM)


def params(limit=VMEM_LIMIT):
    return pltpu.CompilerParams(vmem_limit_bytes=limit)


def cost(flops, moved):
    return pl.CostEstimate(flops=flops, bytes_accessed=moved, transcendentals=0)


def wait_bytes(ref, sem):
    pltpu.make_async_copy(ref, ref, sem).wait()


def f32_dot(left, right):
    return jnp.dot(left, right, preferred_element_type=jnp.float32)


def pick_kernel(module_of, stored, out, sem):
    @pl.loop(0, out.shape[0], unroll=8)
    def _(path):
        pltpu.make_async_copy(stored.at[module_of[path]], out.at[path], sem).start()

    wait_bytes(out, sem)


def pick(module_of, stored):
    paths = module_of.shape[0]
    shape = (paths,) + stored.shape[1:]
    return pl.pallas_call(
        pick_kernel,
        out_shape=jax.ShapeDtypeStruct(shape, stored.dtype),
        in_specs=[SMEM, VMEM],
        out_specs=ANY,
        scratch_shapes=[pltpu.SemaphoreType.DMA],
        compiler_params=params(),
        cost_estimate=cost(0, 2 * math.prod(shape)),
        name="pick",
    )(module_of, stored)


def slabs_of(cols, cut):
    first = [(1, 0)]
    rest = [(1, c) for c in range(cut, cols, cut)] + [(0, c) for c in range(0, cols, cut)]
    return first, rest


def load_logical(owner, arrived, half, cols, weight, sem):
    rows = arrived.shape[2]

    @pl.loop(0, arrived.shape[0], unroll=8)
    def _(block):
        pltpu.make_async_copy(
            arrived.at[owner[block], half, :, cols],
            weight.at[pl.ds(pl.multiple_of(block * rows, rows), rows)],
            sem,
        ).start()


def sigmoid(values):
    return 1.0 / (1.0 + jnp.exp(-values))


def delta_rows(owner, left, pieces, rate, delta, out, sem, tile):
    rows = out.shape[2]

    @pl.loop(0, delta.shape[1] // tile)
    def _(step):
        at = pl.ds(pl.multiple_of(step * tile, tile), tile)
        for slab, (lhs, rhs, cols, scale) in enumerate(pieces):
            grad = f32_dot(lhs[at, :], rhs[:, cols]) * scale
            delta[slab, at, :] = (grad * rate).astype(jnp.bfloat16)

        @pl.loop(0, tile // rows, unroll=8)
        def _(inner):
            block = step * (tile // rows) + inner
            pltpu.make_async_copy(
                delta.at[:, pl.ds(pl.multiple_of(block * rows, rows), rows)],
                out.at[owner[block]],
                sem,
            ).start()

    wait_bytes(delta, sem)


def first_kernel(scales, owner, arrived, tokens, grads_t, out, weight, act, delta, sems):
    scale_in, scale_hid, rate = scales
    cut = act.shape[1]
    load_logical(owner, arrived, 0, pl.ds(0, cut), weight, sems.at[0])
    wait_bytes(weight, sems.at[0])
    part = act.shape[0] // 2

    @pl.loop(0, 2)
    def _(step):
        at = pl.ds(pl.multiple_of(step * part, part), part)
        pre = f32_dot(tokens[at, :], weight[...]) * scale_in
        act[at, :] = (pre * sigmoid(pre)).astype(jnp.bfloat16)

    pieces = [(grads_t, act, pl.ds(0, cut), scale_hid)]
    delta_rows(owner, grads_t, pieces, rate, delta, out, sems.at[1], 512)


def rest_kernel(
    scales, slabs, owner, arrived, tokens, grads, tokens_t, grads_t, earlier, out,
    up_weight, down_weight, tok, grd, tok_t, grd_t, act, slope, delta, sems,
):
    scale_in, scale_hid, rate = scales
    cols = slope.shape[1]
    cut = delta.shape[2]
    skip = cols - act.shape[1]
    pairs = [(tokens, tok), (grads, grd), (tokens_t, tok_t), (grads_t, grd_t)]
    copies = [
        pltpu.make_async_copy(source, target, sems.at[3 + i])
        for i, (source, target) in enumerate(pairs)
    ]
    for copy in copies:
        copy.start()
    load_logical(owner, arrived, 0, pl.ds(0, cols), up_weight, sems.at[0])
    load_logical(owner, arrived, 1, pl.ds(0, cols), down_weight, sems.at[1])
    wait_bytes(up_weight, sems.at[0])
    wait_bytes(down_weight, sems.at[1])
    for copy in copies:
        copy.wait()
    part = slope.shape[0] // 2
    for c in range(0, cols, cut):

        @pl.loop(0, 2)
        def _(step):
            at = pl.ds(pl.multiple_of(step * part, part), part)
            pre = f32_dot(tok[at, :], up_weight[:, pl.ds(c, cut)]) * scale_in
            back = f32_dot(grd[at, :], down_weight[:, pl.ds(c, cut)]) * scale_hid
            sig = sigmoid(pre)
            if c >= skip:
                act[at, pl.ds(c - skip, cut)] = (pre * sig).astype(jnp.bfloat16)
            slope[at, pl.ds(c, cut)] = (back * (sig * (1.0 + pre * (1.0 - sig)))).astype(
                jnp.bfloat16
            )

    pieces = [
        (tok_t, slope, pl.ds(c, cut), scale_in)
        if half == 0
        else (grd_t, act, pl.ds(c - skip, cut), scale_hid)
        for half, c in slabs
    ]
    delta_rows(owner, tok_t, pieces, rate, delta, out, sems.at[2], 512)


def delta_first(scales, cut, owner, arrived, tokens, grads_t):
    paths, _, rows, _ = arrived.shape
    count, width = tokens.shape
    bf16 = jnp.bfloat16
    return pl.pallas_call(
        functools.partial(first_kernel, scales),
        out_shape=jax.ShapeDtypeStruct((paths, 1, rows, cut), bf16),
        in_specs=[SMEM, ANY, VMEM, VMEM],
        out_specs=ANY,
        scratch_shapes=[
            pltpu.VMEM((width, cut), bf16),
            pltpu.VMEM((count, cut), bf16),
            pltpu.VMEM((1, width, cut), bf16),
            pltpu.SemaphoreType.DMA((2,)),
        ],
        compiler_params=params(FIRST_LIMIT),
        cost_estimate=cost(4 * count * width * cut, 4 * (2 * count * width + 2 * width * cut)),
        name="delta_first",
    )(owner, arrived, tokens, grads_t)


def delta_rest(scales, cut, slabs, owner, arrived, tokens, grads, tokens_t, grads_t, earlier):
    paths, _, rows, cols = arrived.shape
    count, width = tokens.shape
    bf16 = jnp.bfloat16
    return pl.pallas_call(
        functools.partial(rest_kernel, scales, slabs),
        out_shape=jax.ShapeDtypeStruct((paths, len(slabs), rows, cut), bf16),
        in_specs=[SMEM] + [ANY] * 6,
        out_specs=ANY,
        scratch_shapes=[
            pltpu.VMEM((width, cols), bf16),
            pltpu.VMEM((width, cols), bf16),
            pltpu.VMEM((count, width), bf16),
            pltpu.VMEM((count, width), bf16),
            pltpu.VMEM((width, count), bf16),
            pltpu.VMEM((width, count), bf16),
            pltpu.VMEM((count, cols - cut), bf16),
            pltpu.VMEM((count, cols), bf16),
            pltpu.VMEM((len(slabs), width, cut), bf16),
            pltpu.SemaphoreType.DMA((7,)),
        ],
        compiler_params=params(),
        cost_estimate=cost(8 * count * width * cols, 4 * (4 * count * width + 3 * width * cols)),
        name="delta_rest",
    )(owner, arrived, tokens, grads, tokens_t, grads_t, earlier)


def begin_of(module_of, first):
    modules = first.shape[0] - 1
    for module in range(modules + 1):
        first[module] = 0

    @pl.loop(0, module_of.shape[0])
    def _(path):
        first[module_of[path] + 1] += 1

    for module in range(modules):
        first[module + 1] += first[module]


def step_module(module, begin, end, order, got, slabs, mas, mom, state, updated):
    _, _, rows, cut = got.shape
    totals = lax.fori_loop(
        begin,
        end,
        lambda i, acc: tuple(
            a + got[order[i], s].astype(jnp.float32) for s, a in enumerate(acc)
        ),
        tuple(jnp.zeros((rows, cut), jnp.float32) for _ in slabs),
    )
    count = jnp.full((rows, cut), end - begin, jnp.int32).astype(jnp.float32)
    for (half, c), total in zip(slabs, totals, strict=True):
        at = (module, half, slice(None), pl.ds(c, cut))
        averaged = total / count
        new = outer_decay * mom[at] + averaged
        state[at] = new
        weights = mas[at].astype(jnp.float32)
        updated[at] = (weights - outer_rate * (averaged + outer_decay * new)).astype(
            jnp.bfloat16
        )


def outer_first_kernel(
    slabs, module_of, order, received, master, momentum, state_out, updated_out,
    got, mas, mom, state, updated, first, sems,
):
    ((half, c),) = slabs
    cut = got.shape[3]
    copies = [
        pltpu.make_async_copy(received, got, sems.at[0]),
        pltpu.make_async_copy(master.at[:, pl.ds(half, 1), :, pl.ds(c, cut)], mas, sems.at[1]),
        pltpu.make_async_copy(
            momentum.at[:, pl.ds(half, 1), :, pl.ds(c, cut)], mom, sems.at[2]
        ),
    ]
    for copy in copies:
        copy.start()
    begin_of(module_of, first)
    for copy in copies:
        copy.wait()

    @pl.loop(0, state.shape[0])
    def _(module):
        step_module(
            module, first[module], first[module + 1], order, got, [(0, 0)], mas, mom, state, updated
        )

    stores = [
        pltpu.make_async_copy(state, state_out, sems.at[0]),
        pltpu.make_async_copy(updated, updated_out, sems.at[1]),
    ]
    for store in stores:
        store.start()
    for store in stores:
        store.wait()


def outer_first(slabs, module_of, order, received, master, momentum):
    paths, _, rows, cut = received.shape
    modules = master.shape[0]
    f32, bf16 = jnp.float32, jnp.bfloat16
    shape = (modules, 1, rows, cut)
    return pl.pallas_call(
        functools.partial(outer_first_kernel, slabs),
        out_shape=(jax.ShapeDtypeStruct(shape, f32), jax.ShapeDtypeStruct(shape, bf16)),
        in_specs=[SMEM, SMEM, ANY, ANY, ANY],
        out_specs=(ANY, ANY),
        scratch_shapes=[
            pltpu.VMEM(received.shape, bf16),
            pltpu.VMEM(shape, bf16),
            pltpu.VMEM(shape, f32),
            pltpu.VMEM(shape, f32),
            pltpu.VMEM(shape, bf16),
            pltpu.SMEM((modules + 1,), jnp.int32),
            pltpu.SemaphoreType.DMA((3,)),
        ],
        compiler_params=params(),
        cost_estimate=cost(paths * rows * cut, 4 * paths * rows * cut),
        name="outer_first",
    )(module_of, order, received, master, momentum)


def outer_rest_kernel(
    slabs, module_of, order, received, master, momentum, state_first, updated_first,
    new_state, sending, got, mas, mom, state, updated, first, sems,
):
    modules = state.shape[0]
    cut = got.shape[3]
    early = (slice(None), pl.ds(1, 1), slice(None), pl.ds(0, cut))
    copies = [
        pltpu.make_async_copy(received, got, sems.at[0]),
        pltpu.make_async_copy(master, mas, sems.at[1]),
        pltpu.make_async_copy(momentum, mom, sems.at[2]),
        pltpu.make_async_copy(state_first, state.at[early], sems.at[3]),
        pltpu.make_async_copy(updated_first, updated.at[early], sems.at[4]),
    ]
    for copy in copies:
        copy.start()
    begin_of(module_of, first)
    for copy in copies:
        copy.wait()

    @pl.loop(0, modules)
    def _(module):
        begin, end = first[module], first[module + 1]
        step_module(module, begin, end, order, got, slabs, mas, mom, state, updated)
        pltpu.make_async_copy(state.at[module], new_state.at[module], sems.at[5]).start()

        @pl.loop(begin, end)
        def _(i):
            pltpu.make_async_copy(updated.at[module], sending.at[order[i]], sems.at[6]).start()

    wait_bytes(sending, sems.at[6])
    wait_bytes(state, sems.at[5])


def outer_rest(slabs, module_of, order, received, master, momentum, earlier):
    paths, _, rows, _ = received.shape
    modules, halves, _, cols = master.shape
    f32, bf16 = jnp.float32, jnp.bfloat16
    return pl.pallas_call(
        functools.partial(outer_rest_kernel, slabs),
        out_shape=(
            jax.ShapeDtypeStruct(momentum.shape, f32),
            jax.ShapeDtypeStruct((paths, halves, rows, cols), bf16),
        ),
        in_specs=[SMEM, SMEM] + [ANY] * 5,
        out_specs=(ANY, ANY),
        scratch_shapes=[
            pltpu.VMEM(received.shape, bf16),
            pltpu.VMEM(master.shape, bf16),
            pltpu.VMEM(momentum.shape, f32),
            pltpu.VMEM(momentum.shape, f32),
            pltpu.VMEM(master.shape, bf16),
            pltpu.SMEM((modules + 1,), jnp.int32),
            pltpu.SemaphoreType.DMA((7,)),
        ],
        compiler_params=params(),
        cost_estimate=cost(paths * rows * cols, 4 * paths * rows * cols),
        name="outer_rest",
    )(module_of, order, received, master, momentum, *earlier)


def home_kernel(groups, owner, back, out, buf, sems):
    per = out.shape[1] // groups
    for group in range(groups):

        @pl.loop(group * per, (group + 1) * per, unroll=8)
        def _(block):
            pltpu.make_async_copy(
                back.at[owner[block]], buf.at[:, block], sems.at[group]
            ).start()

    stores = []
    for group in range(groups):
        part = pl.ds(group * per, per)
        wait_bytes(buf.at[:, part], sems.at[group])
        store = pltpu.make_async_copy(
            buf.at[:, part], out.at[:, part], sems.at[groups + group]
        )
        store.start()
        stores.append(store)
    for store in stores:
        store.wait()


def bring_home(owner, back):
    paths, halves, rows, cols = back.shape
    shape = (halves, paths, rows, cols)
    groups = 4
    return pl.pallas_call(
        functools.partial(home_kernel, groups),
        out_shape=jax.ShapeDtypeStruct(shape, back.dtype),
        in_specs=[SMEM, ANY],
        out_specs=ANY,
        scratch_shapes=[
            pltpu.VMEM(shape, back.dtype),
            pltpu.SemaphoreType.DMA((2 * groups,)),
        ],
        compiler_params=params(),
        cost_estimate=cost(0, 4 * paths * halves * rows * cols),
        name="bring_home",
    )(owner, back)


def collect(tokens, grads):
    count = lax.axis_size("fsdp")
    right = [(i, (i + 1) % count) for i in range(count)]
    left = [(i, (i - 1) % count) for i in range(count)]
    tok_left = lax.ppermute(tokens, "fsdp", right)
    grd_right = lax.ppermute(grads, "fsdp", left)
    grd_left = lax.ppermute(grads, "fsdp", right)
    tok_right = lax.ppermute(tokens, "fsdp", left)
    grd_far = lax.ppermute(grd_right, "fsdp", left)
    tok_far = lax.ppermute(tok_left, "fsdp", right)
    return (
        jnp.concatenate([tokens, tok_left, tok_right, tok_far]),
        jnp.concatenate([grads, grd_left, grd_right, grd_far]),
    )


def exchange(blocks):
    return lax.all_to_all(blocks, "path", split_axis=0, concat_axis=0, tiled=True)


def shards(inputs, cotangent, master, momentum, sharing, block_owner):
    block_cols = master.shape[3]
    module_of = sharing[:, 0]
    order = jnp.argsort(module_of)
    tokens_all, grads_all = collect(inputs, cotangent)
    tok_rows, model_width = tokens_all.shape
    hidden_units = block_cols * lax.axis_size("fsdp")
    scales = (
        1.0 / math.sqrt(model_width),
        1.0 / math.sqrt(hidden_units),
        inner_rate / math.sqrt(tok_rows),
    )
    arrived = exchange(pick(module_of, master))
    cut = block_cols // 2
    early, late = slabs_of(block_cols, cut)
    grads_t = grads_all.T
    begun = delta_first(scales, cut, block_owner, arrived, tokens_all, grads_t)
    got_first = exchange(begun)
    rest = delta_rest(
        scales, cut, late, block_owner, arrived, tokens_all, grads_all, tokens_all.T, grads_t, begun
    )
    got_rest = exchange(rest)
    earlier = outer_first(early, module_of, order, got_first, master, momentum)
    new_state, sending = outer_rest(late, module_of, order, got_rest, master, momentum, earlier)
    own_module = bring_home(block_owner, exchange(sending))
    return (new_state, own_module.reshape(1, 2, model_width, block_cols))


def solution(mesh):
    placed = (
        P(("path", "fsdp"), None),
        P(("path", "fsdp"), None),
        P(None, None, "path", "fsdp"),
        P(None, None, "path", "fsdp"),
        P(),
        P(),
    )
    return jax.shard_map(
        shards,
        mesh=mesh,
        in_specs=placed,
        out_specs=(P(None, None, "path", "fsdp"), P("path", None, None, "fsdp")),
        check_vma=False,
    )
```

time: 355 us -> 361 us (1.017)
  local copies, waits for them, and re-layouts: 33 us -> 47.3 us
  waiting for transfers between devices: 131 us -> 122 us
  starting transfers between devices: 32.2 us -> 36.5 us
    concatenate x1 -> x2, local copies, waits for them, and re-layouts: 2.21 us -> 12.6 us  [collect(): jnp.concatenate([grads, grd_left, grd_right, grd_far])]
    all_to_all x3, waiting for transfers between devices: 87 us -> 77.8 us  [exchange(): lax.all_to_all(blocks, 'path', split_axis=0, concat_axis=0, tiled=True)]
    transpose x1 -> x0, local copies, waits for them, and re-layouts: 5.97 us -> none  [shards(): down = delta_down(scales, block_owner, arrived, tokens_all, grads_all.T)]
    ppermute x0 -> x3, local copies, waits for them, and re-layouts: none -> 5.15 us  [the longest x1 2.24 us: collect(): grd_far = lax.ppermute(grd_right, 'fsdp', left)]
    all_to_all x3, starting transfers between devices: 25.3 us -> 29.6 us  [exchange(): lax.all_to_all(blocks, 'path', split_axis=0, concat_axis=0, tiled=True)]
    unnamed x10 -> x16, local copies, waits for them, and re-layouts: 7.04 us -> 9.43 us
  transfers between devices with their start and end apart: 9 -> 9, of which waited for: 6 -> 5; matrix products, arithmetic and copies ran while one was open for 10% -> 12% of each run, Pallas kernels for 7% -> 7%
where the time goes in v4:
time: 361 us; the launch traced here: 359 us
  waiting for transfers between devices  122 us (34%)
  blocking collectives  102 us (28%)
  Pallas kernels  48.5 us (13%)
  local copies, waits for them, and re-layouts  47.3 us (13%)
  starting transfers between devices  36.5 us (10%)
    all_to_all x1, blocking collectives, exchange(): lax.all_to_all(blocks, 'path', split_axis=0, concat_axis=0, tiled=True)  102 us
    all_to_all x3, waiting for transfers between devices, exchange(): lax.all_to_all(blocks, 'path', split_axis=0, concat_axis=0, tiled=True)  77.8 us
    all_to_all x3, starting transfers between devices, exchange(): lax.all_to_all(blocks, 'path', split_axis=0, concat_axis=0, tiled=True)  29.6 us
    pallas_call x1, Pallas kernels, delta_rest(): pl.pallas_call(functools.partial(rest_kernel, scales, slabs), out_shape=j...  23 us
    ppermute x1, waiting for transfers between devices, collect(): tok_left = lax.ppermute(tokens, 'fsdp', right)  18.2 us
    ppermute x1, waiting for transfers between devices, collect(): tok_far = lax.ppermute(tok_left, 'fsdp', right)  15.7 us
    concatenate x2, local copies, waits for them, and re-layouts, collect(): jnp.concatenate([tokens, tok_left, tok_right, tok_far])  13.4 us
    concatenate x2, local copies, waits for them, and re-layouts, collect(): jnp.concatenate([grads, grd_left, grd_right, grd_far])  12.6 us
  transfers between devices with their start and end apart: 9, of which 5 were waited for; matrix products, arithmetic and copies ran while one was open for 12% of the time, Pallas kernels for 7%

profile of v4, /device:TPU:1, one launch (start us, length us, event | category | flops | bytes accessed | tf_op | source)
XLA Modules:
  0.0 359.4 jit_solution(9113729630914547063)
XLA Ops:
  0.6 3.2 pick.1
  3.9 13.5 %all-to-all-start = ((bf16[64,2,16,1024]{3,2,1,0:T(8,128)(2,1)}), bf16[64,2,16,1024]{3,2,1,0:T(8,128)(2,1)}, u32[]{:S(2)}, u32[]{:S(2)}) async-start(bf16[64,2,16,1024]{3,2,1,0:T(8,128)(2,1)} %pick.1), calls=%async_computation | async-start | bytes 8388608 | tf_op jit(solution)/shard_map/all_to_all | solution.py:430
  21.6 18.2 %collective-permute-done = bf16[440,1024]{1,0:T(8,128)(2,1)} collective-permute-done((bf16[440,1024]{1,0:T(8,128)(2,1)S(1)}, bf16[440,1024]{1,0:T(8,128)(2,1)}, u32[]{:S(2)}, u32[]{:S(2)}) %collective-permute-start) | collective-permute-done | bytes 901152 | tf_op jit(solution)/shard_map/ppermute | solution.py:417
  39.8 2.7 collective-permute-start.5
  45.2 2.3 copy.18
  49.0 10.0 %collective-permute-done.1 = bf16[440,1024]{1,0:T(8,128)(2,1)} collective-permute-done((bf16[440,1024]{1,0:T(8,128)(2,1)S(1)}, bf16[440,1024]{1,0:T(8,128)(2,1)}, u32[]{:S(2)}, u32[]{:S(2)}) %collective-permute-start.1) | collective-permute-done | bytes 901152 | tf_op jit(solution)/shard_map/ppermute | solution.py:420
  59.0 2.2 copy.19
  62.7 15.7 %collective-permute-done.2 = bf16[440,1024]{1,0:T(8,128)(2,1)} collective-permute-done((bf16[440,1024]{1,0:T(8,128)(2,1)}, bf16[440,1024]{1,0:T(8,128)(2,1)}, u32[]{:S(2)}, u32[]{:S(2)}) %collective-permute-start.2) | collective-permute-done | bytes 901152 | tf_op jit(solution)/shard_map/ppermute | solution.py:422
  78.4 2.2 copy.20
  80.7 7.4 %concatenate.6 = bf16[1760,1024]{0,1:T(8,128)(2,1)} concatenate(bf16[440,1024]{0,1:T(8,128)(2,1)} %copy.17, bf16[440,1024]{0,1:T(8,128)(2,1)} %copy.18, bf16[440,1024]{0,1:T(8,128)(2,1)} %copy.19, bf16[440,1024]{0,1:T(8,128)(2,1)} %copy.20), dimensions={0} | concatenate | bytes 7208960 | tf_op jit(solution)/shard_map/concatenate | solution.py:424
  88.1 5.9 %copy.26.tokens = bf16[1760,1024]{1,0:T(8,128)(2,1)} copy(bf16[1760,1024]{0,1:T(8,128)(2,1)} %concatenate.6) | data formatting | bytes 7208960 | tf_op jit(solution)/shard_map/concatenate | solution.py:424
  94.0 2.2 copy.24
  96.3 6.7 %concatenate.7 = bf16[1760,1024]{0,1:T(8,128)(2,1)} concatenate(bf16[440,1024]{0,1:T(8,128)(2,1)S(1)} %copy.21, bf16[440,1024]{0,1:T(8,128)(2,1)S(1)} %copy.22, bf16[440,1024]{0,1:T(8,128)(2,1)S(1)} %copy.23, bf16[440,1024]{0,1:T(8,128)(2,1)} %copy.24), dimensions={0} | concatenate | bytes 7208960 | tf_op jit(solution)/shard_map/concatenate | solution.py:425
  103.0 10.3 %all-to-all-done.arrived = bf16[64,2,16,1024]{3,2,1,0:T(8,128)(2,1)} async-done(((bf16[64,2,16,1024]{3,2,1,0:T(8,128)(2,1)}), bf16[64,2,16,1024]{3,2,1,0:T(8,128)(2,1)}, u32[]{:S(2)}, u32[]{:S(2)}) %all-to-all-start) | async-done | bytes 4194336 | tf_op jit(solution)/shard_map/all_to_all | solution.py:430
  117.3 7.6 %delta_first.1.earlier = bf16[64,1,16,512]{3,2,1,0:T(8,128)(2,1)} custom-call(s32[64]{0:T(128)S(1)} %copy-done.2, bf16[64,2,16,1024]{3,2,1,0:T(8,128)(2,1)} %all-to-all-done.arrived, bf16[1760,1024]{1,0:T(8,128)(2,1)S(1)} %copy-done.1, bf16[1024,1760]{1,0:T(8,128)(2,1)S(1)} %bitcast.5), custom_call_target="tpu_custom_call" | custom-call | flops 3690987520 | bytes 18612224 | tf_op jit(solution)/shard_map/delta_first/pallas_call | solution.py:171
  124.9 5.8 %all-to-all-start.2 = ((bf16[64,1,16,512]{3,2,1,0:T(8,128)(2,1)}), bf16[64,1,16,512]{3,2,1,0:T(8,128)(2,1)S(1)}, u32[]{:S(2)}, u32[]{:S(2)}) async-start(bf16[64,1,16,512]{3,2,1,0:T(8,128)(2,1)} %delta_first.1.earlier), calls=%async_computation.2 | async-start | bytes 2097152 | tf_op jit(solution)/shard_map/all_to_all | solution.py:430
  130.7 5.9 %copy.27.grads = bf16[1760,1024]{1,0:T(8,128)(2,1)} copy(bf16[1760,1024]{0,1:T(8,128)(2,1)} %concatenate.7) | data formatting | bytes 7208960 | tf_op jit(solution)/shard_map/concatenate | solution.py:425
  136.6 23.0 %delta_rest.1 = bf16[64,3,16,512]{3,2,1,0:T(8,128)(2,1)} custom-call(s32[64]{0:T(128)} %owner.5, bf16[64,2,16,1024]{3,2,1,0:T(8,128)(2,1)} %all-to-all-done.arrived, bf16[1760,1024]{1,0:T(8,128)(2,1)} %copy.26.tokens, bf16[1760,1024]{1,0:T(8,128)(2,1)} %copy.27.grads, bf16[1024,1760]{1,0:T(8,128)(2,1)} %bitcast.6, bf16[1024,1760]{1,0:T(8,128)(2,1)} %bitcast.4, ...), custom_call_target="tpu_custom_call" | custom-call | flops 14763950080 | bytes 41418752 | tf_op jit(solution)/shard_map/delta_rest/pallas_call | solution.py:192
  160.6 10.3 %all-to-all-start.1 = ((bf16[64,3,16,512]{3,2,1,0:T(8,128)(2,1)}), bf16[64,3,16,512]{3,2,1,0:T(8,128)(2,1)S(1)}, u32[]{:S(2)}, u32[]{:S(2)}) async-start(bf16[64,3,16,512]{3,2,1,0:T(8,128)(2,1)} %delta_rest.1), calls=%async_computation.1 | async-start | bytes 6291456 | tf_op jit(solution)/shard_map/all_to_all | solution.py:430
  173.0 3.9 %outer_first.1 = (f32[16,1,16,512]{3,2,1,0:T(8,128)}, bf16[16,1,16,512]{3,2,1,0:T(8,128)(2,1)}) custom-call(s32[64]{0:T(128)} %bitcast.9, s32[64]{0:T(128)} %get-tuple-element.7.order, bf16[64,1,16,512]{3,2,1,0:T(8,128)(2,1)} %copy-done.4, bf16[16,2,16,1024]{3,2,1,0:T(8,128)(2,1)} %master.3, f32[16,2,16,1024]{3,2,1,0:T(8,128)} %momentum.3), custom_call_target="tpu_custom_call" | custom-call | flops 524288 | bytes 2097152 | tf_op jit(solution)/shard_map/outer_first/pallas_call | solution.py:290
  176.9 67.5 %all-to-all-done.1.received = bf16[64,3,16,512]{3,2,1,0:T(8,128)(2,1)S(1)} async-done(((bf16[64,3,16,512]{3,2,1,0:T(8,128)(2,1)}), bf16[64,3,16,512]{3,2,1,0:T(8,128)(2,1)S(1)}, u32[]{:S(2)}, u32[]{:S(2)}) %all-to-all-start.1) | async-done | bytes 3145760 | tf_op jit(solution)/shard_map/all_to_all | solution.py:430
  246.1 6.7 %outer_rest.1 = (f32[16,2,16,1024]{3,2,1,0:T(8,128)}, bf16[64,2,16,1024]{3,2,1,0:T(8,128)(2,1)}) custom-call(s32[64]{0:T(128)} %bitcast.10, s32[64]{0:T(128)} %get-tuple-element.7.order, bf16[64,3,16,512]{3,2,1,0:T(8,128)(2,1)} %copy-done.3, bf16[16,2,16,1024]{3,2,1,0:T(8,128)(2,1)} %master.3, f32[16,2,16,1024]{3,2,1,0:T(8,128)} %momentum.3, ...), custom_call_target="tpu_custom_call" | custom-call | flops 1048576 | bytes 4194304 | tf_op jit(solution)/shard_map/outer_rest/pallas_call | solution.py:348
  252.8 102.4 %all_to_all.20.back = bf16[64,2,16,1024]{3,2,1,0:T(8,128)(2,1)} all-to-all(bf16[64,2,16,1024]{3,2,1,0:T(8,128)(2,1)} %get-tuple-element.11), channel_id=1, replica_groups=mesh['path'=64,'fsdp'=4] {'path'}, dimensions={0} | all-to-all | bytes 8388608 | tf_op jit(solution)/shard_map/all_to_all | solution.py:430
  355.2 4.1 %bring_home.1 = bf16[2,64,16,1024]{3,2,1,0:T(8,128)(2,1)} custom-call(s32[64]{0:T(128)} %owner.5, bf16[64,2,16,1024]{3,2,1,0:T(8,128)(2,1)} %all_to_all.20.back), custom_call_target="tpu_custom_call" | custom-call | bytes 8388608 | tf_op jit(solution)/shard_map/bring_home/pallas_call | solution.py:398
  (29 shorter events, 18.6 us)
Async XLA Ops:
  3.8 13.5 %copy-start.5 = (bf16[440,1024]{1,0:T(8,128)(2,1)S(1)}, bf16[440,1024]{1,0:T(8,128)(2,1)}, u32[]{:S(2)}) copy-start(bf16[440,1024]{1,0:T(8,128)(2,1)} %param.6) | copy-start | bytes 2703364
  3.9 109.4 %all-to-all-start = ((bf16[64,2,16,1024]{3,2,1,0:T(8,128)(2,1)}), bf16[64,2,16,1024]{3,2,1,0:T(8,128)(2,1)}, u32[]{:S(2)}, u32[]{:S(2)}) async-start(bf16[64,2,16,1024]{3,2,1,0:T(8,128)(2,1)} %pick.1), calls=%async_computation | async-start | bytes 8388608 | tf_op jit(solution)/shard_map/all_to_all | solution.py:430
  17.4 22.4 %collective-permute-start = (bf16[440,1024]{1,0:T(8,128)(2,1)S(1)}, bf16[440,1024]{1,0:T(8,128)(2,1)}, u32[]{:S(2)}, u32[]{:S(2)}) collective-permute-start(bf16[440,1024]{1,0:T(8,128)(2,1)S(1)} %copy-done.5), channel_id=1, source_target_pairs={{0,1},{1,2},{2,3},{3,0},{4,5},{5,6},{6,7},{7,4},{8,9},{9,10},{10,1... | collective-permute-start | bytes 2703368 | tf_op jit(solution)/shard_map/ppermute | solution.py:417
  18.6 21.1 %collective-permute-start.4 = (bf16[440,1024]{1,0:T(8,128)(2,1)}, bf16[440,1024]{1,0:T(8,128)(2,1)}, u32[]{:S(2)}, u32[]{:S(2)}) collective-permute-start(bf16[440,1024]{1,0:T(8,128)(2,1)} %param.7), channel_id=1, source_target_pairs={{0,3},{1,0},{2,1},{3,2},{4,7},{5,4},{6,5},{7,6},{8,11},{9,8},{10,9... | collective-permute-start | bytes 2703368 | tf_op jit(solution)/shard_map/ppermute | solution.py:418
  20.1 38.9 %collective-permute-start.1 = (bf16[440,1024]{1,0:T(8,128)(2,1)S(1)}, bf16[440,1024]{1,0:T(8,128)(2,1)}, u32[]{:S(2)}, u32[]{:S(2)}) collective-permute-start(bf16[440,1024]{1,0:T(8,128)(2,1)S(1)} %copy-done.5), channel_id=1, source_target_pairs={{0,3},{1,0},{2,1},{3,2},{4,7},{5,4},{6,5},{7,6},{8,11},{9,8},{10,9... | collective-permute-start | bytes 2703368 | tf_op jit(solution)/shard_map/ppermute | solution.py:420
  21.4 39.9 %collective-permute-start.3 = (bf16[440,1024]{1,0:T(8,128)(2,1)}, bf16[440,1024]{1,0:T(8,128)(2,1)}, u32[]{:S(2)}, u32[]{:S(2)}) collective-permute-start(bf16[440,1024]{1,0:T(8,128)(2,1)} %param.7), channel_id=1, source_target_pairs={{0,1},{1,2},{2,3},{3,0},{4,5},{5,6},{6,7},{7,4},{8,9},{9,10},{10,1... | collective-permute-start | bytes 2703368 | tf_op jit(solution)/shard_map/ppermute | solution.py:419
  39.8 38.6 %collective-permute-start.2 = (bf16[440,1024]{1,0:T(8,128)(2,1)}, bf16[440,1024]{1,0:T(8,128)(2,1)}, u32[]{:S(2)}, u32[]{:S(2)}) collective-permute-start(bf16[440,1024]{1,0:T(8,128)(2,1)} %collective-permute-done), channel_id=1, source_target_pairs={{0,1},{1,2},{2,3},{3,0},{4,5},{5,6},{6,7},{7,4},{8,9},{9,10},{10,1... | collective-permute-start | bytes 2703368 | tf_op jit(solution)/shard_map/ppermute | solution.py:422
  39.8 54.2 %collective-permute-start.5 = (bf16[440,1024]{1,0:T(8,128)(2,1)}, bf16[440,1024]{1,0:T(8,128)(2,1)}, u32[]{:S(2)}, u32[]{:S(2)}) collective-permute-start(bf16[440,1024]{1,0:T(8,128)(2,1)} %collective-permute-done.4), channel_id=1, source_target_pairs={{0,3},{1,0},{2,1},{3,2},{4,7},{5,4},{6,5},{7,6},{8,11},{9,8},{10,9... | collective-permute-start | bytes 2703368 | tf_op jit(solution)/shard_map/ppermute | solution.py:421
  96.3 17.0 %copy-start.2 = (s32[64]{0:T(128)S(1)}, s32[64]{0:T(128)}, u32[]{:S(2)}) copy-start(s32[64]{0:T(128)} %owner.5) | copy-start | bytes 772
  113.2 2.0 copy-start
  115.3 2.0 copy-start.1
  124.9 34.7 %all-to-all-start.2 = ((bf16[64,1,16,512]{3,2,1,0:T(8,128)(2,1)}), bf16[64,1,16,512]{3,2,1,0:T(8,128)(2,1)S(1)}, u32[]{:S(2)}, u32[]{:S(2)}) async-start(bf16[64,1,16,512]{3,2,1,0:T(8,128)(2,1)} %delta_first.1.earlier), calls=%async_computation.2 | async-start | bytes 2097152 | tf_op jit(solution)/shard_map/all_to_all | solution.py:430
  159.6 11.3 %copy-start.6 = (s32[64,1]{0,1:T(1,128)S(1)}, s32[64,1]{0,1:T(1,128)}, u32[]{:S(2)}) copy-start(s32[64,1]{0,1:T(1,128)} %param.10) | copy-start | bytes 772
  159.6 1.0 copy-start.4
  160.6 83.8 %all-to-all-start.1 = ((bf16[64,3,16,512]{3,2,1,0:T(8,128)(2,1)}), bf16[64,3,16,512]{3,2,1,0:T(8,128)(2,1)S(1)}, u32[]{:S(2)}, u32[]{:S(2)}) async-start(bf16[64,3,16,512]{3,2,1,0:T(8,128)(2,1)} %delta_rest.1), calls=%async_computation.1 | async-start | bytes 6291456 | tf_op jit(solution)/shard_map/all_to_all | solution.py:430
  244.4 1.6 copy-start.3

commit v5 on v0

v5 whole, which is shorter than its diff:
```python
import functools
import math

import jax
import jax.numpy as jnp
from jax import lax
from jax.experimental import pallas as pl
from jax.experimental.pallas import tpu as pltpu
from jax.sharding import PartitionSpec as P

inner_rate = 10.0
outer_rate = 0.7
outer_decay = 0.9

VMEM_LIMIT = 56 * 1024 * 1024
MAIN_LIMIT = 40 * 1024 * 1024
OUTER_LIMIT = 40 * 1024 * 1024
LAST_LIMIT = 36 * 1024 * 1024
ANY = pl.BlockSpec(memory_space=pl.ANY)
SMEM = pl.BlockSpec(memory_space=pltpu.SMEM)
VMEM = pl.BlockSpec(memory_space=pltpu.VMEM)


def params(limit=VMEM_LIMIT):
    return pltpu.CompilerParams(vmem_limit_bytes=limit)


def cost(flops, moved):
    return pl.CostEstimate(flops=flops, bytes_accessed=moved, transcendentals=0)


def wait_bytes(ref, sem):
    pltpu.make_async_copy(ref, ref, sem).wait()


def f32_dot(left, right):
    return jnp.dot(left, right, preferred_element_type=jnp.float32)


def pick_kernel(pieces, module_of, stored, out, held, sem, load_sems):
    at, loads = 0, []
    for i, (half, col, cols) in enumerate(pieces):
        loads.append(
            pltpu.make_async_copy(
                stored.at[:, half, :, pl.ds(col, cols)],
                held.at[:, :, pl.ds(at, cols)],
                load_sems.at[i],
            )
        )
        loads[-1].start()
        at += cols
    for load in loads:
        load.wait()

    @pl.loop(0, out.shape[0], unroll=8)
    def _(path):
        pltpu.make_async_copy(held.at[module_of[path]], out.at[path], sem).start()

    wait_bytes(out, sem)


def pick(pieces, module_of, stored):
    paths, (modules, _, rows, _) = module_of.shape[0], stored.shape
    cols = sum(piece[2] for piece in pieces)
    return pl.pallas_call(
        functools.partial(pick_kernel, pieces),
        out_shape=jax.ShapeDtypeStruct((paths, rows, cols), stored.dtype),
        in_specs=[SMEM, ANY],
        out_specs=ANY,
        scratch_shapes=[
            pltpu.VMEM((modules, rows, cols), stored.dtype),
            pltpu.SemaphoreType.DMA,
            pltpu.SemaphoreType.DMA((len(pieces),)),
        ],
        compiler_params=params(),
        cost_estimate=cost(0, 2 * paths * rows * cols),
        name="pick",
    )(module_of, stored)


def sigmoid(values):
    return 1.0 / (1.0 + jnp.exp(-values))


def starter(sems):
    def start(source, target, sem):
        copy = pltpu.make_async_copy(source, target, sems.at[sem])
        copy.start()
        return copy

    return start


def load_shards(start, shards_in, target, first_sem):
    each = shards_in[0].shape[0]
    return [
        start(shard, target.at[pl.ds(i * each, each)], first_sem + i)
        for i, shard in enumerate(shards_in)
    ]


def main_kernel(
    scales, late, owner, arrived, tokens_t, grads_t, *refs,
):
    scale_in, scale_hid, rate = scales
    count = 4
    tok_in, grd_in = refs[:count], refs[count : 2 * count]
    (
        out, grd, tok_t, factor,
        weight, tok, grd_t, act, slope, up, down, sems,
    ) = refs[2 * count :]
    rows, cols = out.shape[2:]
    early = cols - late
    start = starter(sems)
    toks = load_shards(start, tok_in[:2], tok, 4)

    @pl.loop(0, arrived.shape[0], unroll=8)
    def _(block):
        pltpu.make_async_copy(
            arrived.at[owner[block]],
            weight.at[pl.ds(pl.multiple_of(block * rows, rows), rows)],
            sems.at[0],
        ).start()

    grds = load_shards(start, grd_in[:2], grd, 4 + count)
    half = tok.shape[0] // 2
    toks += load_shards(start, tok_in[2:], tok.at[pl.ds(half, half)], 6)
    grds += load_shards(start, grd_in[2:], grd.at[pl.ds(half, half)], 6 + count)
    grd_t_copy = start(grads_t, grd_t, 2)
    tok_t_copy = start(tokens_t, tok_t, 3)
    wait_bytes(weight, sems.at[0])
    mid = cols // 2
    for part in range(2):
        at = pl.ds(part * half, half)
        for copy in toks[2 * part : 2 * part + 2] + grds[2 * part : 2 * part + 2]:
            copy.wait()
        for col, width, known in ((0, mid, mid), (mid, cols - mid, early - mid)):
            pre = f32_dot(tok[at, :], weight[:, pl.ds(col, width)]) * scale_in
            back = f32_dot(grd[at, :], weight[:, pl.ds(cols + col, known)]) * scale_hid
            sig = sigmoid(pre)
            act[at, pl.ds(col, width)] = (pre * sig).astype(jnp.bfloat16)
            turn = sig * (1.0 + pre * (1.0 - sig))
            slope[at, pl.ds(col, known)] = (back * turn[:, :known]).astype(jnp.bfloat16)
            if known < width:
                factor[at, :] = turn[:, known:]
    grd_t_copy.wait()
    tok_t_copy.wait()
    tile = 512

    @pl.loop(0, down.shape[0] // tile)
    def _(step):
        at = pl.ds(pl.multiple_of(step * tile, tile), tile)
        down[at, :] = (f32_dot(grd_t[at, :], act[...]) * scale_hid * rate).astype(jnp.bfloat16)
        up[at, :] = (f32_dot(tok_t[at, :], slope[...]) * scale_in * rate).astype(jnp.bfloat16)

        @pl.loop(0, tile // rows, unroll=8)
        def _(inner):
            block = step * (tile // rows) + inner
            at = pl.ds(pl.multiple_of(block * rows, rows), rows)
            place = owner[block]
            pltpu.make_async_copy(down.at[at], out.at[place, 1], sems.at[2]).start()
            pltpu.make_async_copy(
                up.at[at], out.at[place, 0, :, pl.ds(0, early)], sems.at[3]
            ).start()

    wait_bytes(down, sems.at[2])
    wait_bytes(up, sems.at[3])


def main_delta(scales, late, owner, arrived, tokens, grads, tokens_t, grads_t):
    paths, rows, both = arrived.shape
    width, count = tokens_t.shape
    cols = (both + late) // 2
    f32, bf16 = jnp.float32, jnp.bfloat16
    return pl.pallas_call(
        functools.partial(main_kernel, scales, late),
        out_shape=(
            pltpu.HBM((paths, 2, rows, cols), bf16),
            pltpu.VMEM((count, width), bf16),
            pltpu.VMEM((width, count), bf16),
            pltpu.VMEM((count, late), f32),
        ),
        in_specs=[SMEM] + [ANY] * 11,
        out_specs=(ANY, VMEM, VMEM, VMEM),
        scratch_shapes=[
            pltpu.VMEM((width, both), bf16),
            pltpu.VMEM((count, width), bf16),
            pltpu.VMEM((width, count), bf16),
            pltpu.VMEM((count, cols), bf16),
            pltpu.VMEM((count, cols - late), bf16),
            pltpu.VMEM((width, cols - late), bf16),
            pltpu.VMEM((width, cols), bf16),
            pltpu.SemaphoreType.DMA((12,)),
        ],
        compiler_params=params(MAIN_LIMIT),
        cost_estimate=cost(8 * count * width * cols, 8 * (count * width + width * cols)),
        name="main_delta",
    )(owner, arrived, tokens_t, grads_t, *tokens, *grads)


def last_kernel(
    scales, owner, arrived, grads, tokens_t, factor, begun, out, got, weight, sending, sems
):
    scale_in, scale_hid, rate = scales
    blocks, rows, late = got.shape
    start = starter(sems)
    start(arrived, got, 0).wait()

    @pl.loop(0, blocks, unroll=4)
    def _(block):
        weight[pl.ds(pl.multiple_of(block * rows, rows), rows), :] = got[owner[block]]

    back = f32_dot(grads[...], weight[...]) * scale_hid
    slope = (back * factor[...]).astype(jnp.bfloat16)
    weight[...] = (f32_dot(tokens_t[...], slope) * scale_in * rate).astype(jnp.bfloat16)

    @pl.loop(0, blocks, unroll=4)
    def _(block):
        sending[owner[block]] = weight[pl.ds(pl.multiple_of(block * rows, rows), rows), :]

    start(sending, out.at[:, 0, :, pl.ds(out.shape[3] - late, late)], 1).wait()


def last_delta(scales, owner, arrived, begun, grads, tokens_t, factor):
    paths, rows, late = arrived.shape
    width, count = tokens_t.shape
    bf16 = jnp.bfloat16
    return pl.pallas_call(
        functools.partial(last_kernel, scales),
        out_shape=pltpu.HBM(begun.shape, bf16),
        in_specs=[SMEM, ANY, VMEM, VMEM, VMEM, ANY],
        out_specs=ANY,
        scratch_shapes=[
            pltpu.VMEM((paths, rows, late), bf16),
            pltpu.VMEM((width, late), bf16),
            pltpu.VMEM((paths, rows, late), bf16),
            pltpu.SemaphoreType.DMA((2,)),
        ],
        input_output_aliases={5: 0},
        compiler_params=params(LAST_LIMIT),
        cost_estimate=cost(4 * count * width * late, 4 * count * width),
        name="last_delta",
    )(owner, arrived, grads, tokens_t, factor, begun)


def ready_kernel(module_of, master, momentum, base, kept, share, first, mas, mom, sems):
    copies = [
        pltpu.make_async_copy(master, mas, sems.at[0]),
        pltpu.make_async_copy(momentum, mom, sems.at[1]),
    ]
    for copy in copies:
        copy.start()
    modules = first.shape[0] - 1
    for module in range(modules + 1):
        first[module] = 0

    @pl.loop(0, module_of.shape[0])
    def _(path):
        first[module_of[path] + 1] += 1

    for module in range(modules):
        count = jnp.full(share.shape[1:], first[module + 1], jnp.int32)
        share[module] = 1.0 / count.astype(jnp.float32)
        first[module + 1] += first[module]
    for copy in copies:
        copy.wait()

    @pl.loop(0, modules)
    def _(module):
        old = outer_decay * mom[module]
        kept[module] = old
        base[module] = mas[module].astype(jnp.float32) - (outer_rate * outer_decay) * old


def ready(module_of, master, momentum):
    f32 = jnp.float32
    modules = master.shape[0]
    return pl.pallas_call(
        ready_kernel,
        out_shape=(
            pltpu.VMEM(momentum.shape, f32),
            pltpu.VMEM(momentum.shape, f32),
            pltpu.VMEM((modules, 8, momentum.shape[3]), f32),
            jax.ShapeDtypeStruct((modules + 1,), jnp.int32),
        ),
        in_specs=[SMEM, ANY, ANY],
        out_specs=(VMEM, VMEM, VMEM, SMEM),
        scratch_shapes=[
            pltpu.VMEM(master.shape, master.dtype),
            pltpu.VMEM(momentum.shape, f32),
            pltpu.SemaphoreType.DMA((2,)),
        ],
        compiler_params=params(OUTER_LIMIT),
        cost_estimate=cost(0, 8 * momentum.size),
        name="ready",
    )(module_of, master, momentum)


def outer_kernel(
    first, order, received, base, kept, share, new_state, sending, got, state, updated, sems
):
    modules, halves, rows, cols = state.shape
    step = outer_rate * (1.0 + outer_decay)
    loads = [
        pltpu.make_async_copy(received.at[:, half], got.at[half], sems.at[half])
        for half in range(halves)
    ]
    for load in loads:
        load.start()
    for half in range(halves):
        loads[half].wait()

        @pl.loop(0, modules)
        def _(module):
            begin, end = first[module], first[module + 1]
            total = lax.fori_loop(
                begin,
                end,
                lambda i, acc: acc + got[half, order[i]].astype(jnp.float32),
                jnp.zeros((rows, cols), jnp.float32),
            )
            averaged = (total.reshape(-1, 8, cols) * share[module]).reshape(rows, cols)
            state[module, half] = kept[module, half] + averaged
            updated[module, half] = (base[module, half] - step * averaged).astype(jnp.bfloat16)
            if half == halves - 1:
                pltpu.make_async_copy(
                    state.at[module], new_state.at[module], sems.at[halves]
                ).start()

                @pl.loop(begin, end)
                def _(i):
                    pltpu.make_async_copy(
                        updated.at[module], sending.at[order[i]], sems.at[halves + 1]
                    ).start()

    wait_bytes(sending, sems.at[halves + 1])
    wait_bytes(state, sems.at[halves])


def outer(first, order, received, base, kept, share):
    paths, halves, rows, cols = received.shape
    f32, bf16 = jnp.float32, jnp.bfloat16
    return pl.pallas_call(
        outer_kernel,
        out_shape=(
            jax.ShapeDtypeStruct(kept.shape, f32),
            jax.ShapeDtypeStruct(received.shape, bf16),
        ),
        in_specs=[SMEM, SMEM, ANY, VMEM, VMEM, VMEM],
        out_specs=(ANY, ANY),
        scratch_shapes=[
            pltpu.VMEM((halves, paths, rows, cols), bf16),
            pltpu.VMEM(kept.shape, f32),
            pltpu.VMEM(kept.shape, bf16),
            pltpu.SemaphoreType.DMA((halves + 2,)),
        ],
        compiler_params=params(OUTER_LIMIT),
        cost_estimate=cost(2 * paths * rows * cols, 8 * paths * rows * cols),
        name="outer",
    )(first, order, received, base, kept, share)


def home_kernel(groups, owner, back, out, buf, place, sems):
    per = back.shape[0] // groups
    loads = []
    for group in range(groups):
        part = pl.ds(group * per, per)
        loads.append(
            pltpu.make_async_copy(back.at[part], buf.at[part], sems.at[group])
        )
        loads[-1].start()

    @pl.loop(0, back.shape[0], unroll=8)
    def _(block):
        place[owner[block]] = block

    for group in range(groups):
        loads[group].wait()

        @pl.loop(0, per, unroll=8)
        def _(inner):
            holder = group * per + inner
            pltpu.make_async_copy(
                buf.at[holder], out.at[:, place[holder]], sems.at[groups]
            ).start()

    wait_bytes(buf, sems.at[groups])


def bring_home(owner, back):
    paths, halves, rows, cols = back.shape
    groups = 4
    return pl.pallas_call(
        functools.partial(home_kernel, groups),
        out_shape=jax.ShapeDtypeStruct((halves, paths, rows, cols), back.dtype),
        in_specs=[SMEM, ANY],
        out_specs=ANY,
        scratch_shapes=[
            pltpu.VMEM(back.shape, back.dtype),
            pltpu.SMEM((paths,), jnp.int32),
            pltpu.SemaphoreType.DMA((groups + 1,)),
        ],
        compiler_params=params(),
        cost_estimate=cost(0, 4 * paths * halves * rows * cols),
        name="bring_home",
    )(owner, back)


def collect(tokens, grads):
    count = lax.axis_size("fsdp")
    right = [(i, (i + 1) % count) for i in range(count)]
    left = [(i, (i - 1) % count) for i in range(count)]
    tok_left = lax.ppermute(tokens, "fsdp", right)
    grd_right = lax.ppermute(grads, "fsdp", left)
    grd_left = lax.ppermute(grads, "fsdp", right)
    tok_right = lax.ppermute(tokens, "fsdp", left)
    grd_far = lax.ppermute(grd_right, "fsdp", left)
    tok_far = lax.ppermute(tok_left, "fsdp", right)
    return (tokens, tok_left, tok_right, tok_far), (grads, grd_left, grd_right, grd_far)


def exchange(blocks):
    return lax.all_to_all(blocks, "path", split_axis=0, concat_axis=0, tiled=True)


def shards(inputs, cotangent, master, momentum, sharing, block_owner):
    block_cols = master.shape[3]
    module_of = sharing[:, 0]
    order = jnp.argsort(module_of)
    fsdp = lax.axis_size("fsdp")
    rows, model_width = inputs.shape
    fill = ((0, -rows % 64), (0, 0))
    tokens, grads = collect(
        *lax.optimization_barrier((jnp.pad(inputs, fill), jnp.pad(cotangent, fill)))
    )
    tokens_t, grads_t = jnp.concatenate(tokens).T, jnp.concatenate(grads).T
    scales = (
        1.0 / math.sqrt(model_width),
        1.0 / math.sqrt(block_cols * fsdp),
        inner_rate / math.sqrt(rows * fsdp),
    )
    late = block_cols // 4
    early = block_cols - late
    arrived = exchange(pick([(0, 0, block_cols), (1, 0, early)], module_of, master))
    arrived_late = exchange(pick([(1, early, late)], module_of, master))
    held = main_delta(
        scales, late, block_owner, arrived, tokens, grads, tokens_t, grads_t
    )
    delta = last_delta(scales, block_owner, arrived_late, *held)
    base, kept, share, first = ready(module_of, master, momentum)
    new_state, sending = outer(first, order, exchange(delta), base, kept, share)
    own_module = bring_home(block_owner, exchange(sending))
    return (new_state, own_module.reshape(1, 2, model_width, block_cols))


def solution(mesh):
    placed = (
        P(("path", "fsdp"), None),
        P(("path", "fsdp"), None),
        P(None, None, "path", "fsdp"),
        P(None, None, "path", "fsdp"),
        P(),
        P(),
    )
    return jax.shard_map(
        shards,
        mesh=mesh,
        in_specs=placed,
        out_specs=(P(None, None, "path", "fsdp"), P("path", None, None, "fsdp")),
        check_vma=False,
    )
```

time: 435 us -> 372 us (0.86)
  waiting for transfers between devices: 283 us -> 139 us
  blocking collectives: 0 us -> 102 us
  Pallas kernels: 0 us -> 49.8 us
  matrix products: 37.7 us -> 0 us
  local copies, waits for them, and re-layouts: 46.7 us -> 30.7 us
  other arithmetic: 26.6 us -> 11 us
  between operations: 14.2 us -> 1.02 us
  starting transfers between devices: 25.4 us -> 37.6 us
    all_to_all x3, waiting for transfers between devices: 282 us -> 95.2 us  [exchange(): lax.all_to_all(blocks, 'path', split_axis=0, concat_axis=0, tiled=True)]
    all_to_all x0 -> x1, blocking collectives: none -> 102 us  [exchange(): lax.all_to_all(blocks, 'path', split_axis=0, concat_axis=0, tiled=True)]
    pallas_call x0 -> x7, Pallas kernels: none -> 49.8 us  [the longest x1 21.1 us: main_delta(): pl.pallas_call(functools.partial(main_kernel, scales, late), out_shape=(p...]
    ppermute x0 -> x6, waiting for transfers between devices: none -> 44.2 us  [the longest x1 19 us: collect(): grd_right = lax.ppermute(grads, 'fsdp', left)]
    dot_general x4 -> x0, matrix products: 37.7 us -> none  [the longest x1 15.5 us: shards(): lax.dot_general(tokens_all, slope_grad, (((0,), (0,)), ((), ())), preferr...]
    gather x5 -> x0, local copies, waits for them, and re-layouts: 21.8 us -> none  [the longest x1 5.01 us: shards(): jnp.take(arrived, block_owner, axis=1).reshape(2, model_width, block_cols)]
    select_n x8 -> x0, other arithmetic: 19.8 us -> none  [the longest x2 5.3 us: shards(): outgoing = jnp.take(ordered, module_of, axis=1)]
    unnamed x9 -> x38, local copies, waits for them, and re-layouts: 2.55 us -> 18.7 us
  transfers between devices with their start and end apart: 5 -> 9, of which waited for: 3 -> 6; matrix products, arithmetic and copies ran while one was open for 8% -> 6% of each run, Pallas kernels for 0% -> 7%
where the time goes in v5:
time: 372 us; the launch traced here: 371 us
  waiting for transfers between devices  139 us (37%)
  blocking collectives  102 us (27%)
  Pallas kernels  49.8 us (13%)
  starting transfers between devices  37.6 us (10%)
  local copies, waits for them, and re-layouts  30.7 us (8%)
  other arithmetic  11 us (3%)
    all_to_all x1, blocking collectives, exchange(): lax.all_to_all(blocks, 'path', split_axis=0, concat_axis=0, tiled=True)  102 us
    all_to_all x3, waiting for transfers between devices, exchange(): lax.all_to_all(blocks, 'path', split_axis=0, concat_axis=0, tiled=True)  95.2 us
    all_to_all x3, starting transfers between devices, exchange(): lax.all_to_all(blocks, 'path', split_axis=0, concat_axis=0, tiled=True)  29.9 us
    pallas_call x1, Pallas kernels, main_delta(): pl.pallas_call(functools.partial(main_kernel, scales, late), out_shape=(p...  21.1 us
    ppermute x1, waiting for transfers between devices, collect(): grd_right = lax.ppermute(grads, 'fsdp', left)  19 us
    unnamed x38, local copies, waits for them, and re-layouts  18.7 us
    ppermute x1, waiting for transfers between devices, collect(): grd_left = lax.ppermute(grads, 'fsdp', right)  15.4 us
    transpose x2, local copies, waits for them, and re-layouts, shards(): tokens_t, grads_t = (jnp.concatenate(tokens).T, jnp.concatenate(grads).T)  11.8 us
  transfers between devices with their start and end apart: 9, of which 6 were waited for; matrix products, arithmetic and copies ran while one was open for 6% of the time, Pallas kernels for 7%

profile of v5, /device:TPU:1, one launch (start us, length us, event | category | flops | bytes accessed | tf_op | source)
XLA Modules:
  0.0 371.3 jit_solution(715790122852722610)
XLA Ops:
  0.6 3.6 pick.3
  4.3 13.5 %all-to-all-start.1 = ((bf16[64,16,1792]{2,1,0:T(8,128)(2,1)}), bf16[64,16,1792]{2,1,0:T(8,128)(2,1)}, u32[]{:S(2)}, u32[]{:S(2)}) async-start(bf16[64,16,1792]{2,1,0:T(8,128)(2,1)} %pick.3), calls=%async_computation.1 | async-start | bytes 7340032 | tf_op jit(solution)/shard_map/all_to_all | solution.py:423
  17.9 2.6 collective-permute-start.4
  20.7 19.0 %collective-permute-done.4.refs_6_ = bf16[448,1024]{1,0:T(8,128)(2,1)S(1)} collective-permute-done((bf16[448,1024]{1,0:T(8,128)(2,1)S(1)}, bf16[448,1024]{1,0:T(8,128)(2,1)S(1)}, u32[]{:S(2)}, u32[]{:S(2)}) %collective-permute-start.4) | collective-permute-done | bytes 917536 | tf_op jit(solution)/shard_map/ppermute | solution.py:414
  39.7 3.5 collective-permute-start.5
  44.7 2.4 pick.2
  47.1 15.4 %collective-permute-done.3.refs_5_ = bf16[448,1024]{1,0:T(8,128)(2,1)S(1)} collective-permute-done((bf16[448,1024]{1,0:T(8,128)(2,1)S(1)}, bf16[448,1024]{1,0:T(8,128)(2,1)S(1)}, u32[]{:S(2)}, u32[]{:S(2)}) %collective-permute-start.3) | collective-permute-done | bytes 917536 | tf_op jit(solution)/shard_map/ppermute | solution.py:415
  64.4 2.1 maximum_bitcast_fusion.1
  66.5 5.9 %copy.10.grads_t = bf16[1024,1792]{1,0:T(8,128)(2,1)} copy(bf16[1024,1792]{0,1:T(8,128)(2,1)} %maximum_bitcast_fusion.1) | data formatting | bytes 7340032 | tf_op jit(solution)/shard_map/transpose | solution.py:436
  72.5 8.7 %collective-permute-done.1.refs_2_ = bf16[448,1024]{1,0:T(8,128)(2,1)} collective-permute-done((bf16[448,1024]{1,0:T(8,128)(2,1)S(1)}, bf16[448,1024]{1,0:T(8,128)(2,1)}, u32[]{:S(2)}, u32[]{:S(2)}) %collective-permute-start.1) | collective-permute-done | bytes 917536 | tf_op jit(solution)/shard_map/ppermute | solution.py:416
  82.2 6.9 %maximum_bitcast_fusion = bf16[1024,1792]{0,1:T(8,128)(2,1)} fusion(bf16[448,1024]{1,0:T(8,128)(2,1)} %collective-permute-done.2.refs_3_, bf16[448,1024]{1,0:T(8,128)(2,1)} %collective-permute-done.1.refs_2_, bf16[448,1024]{1,0:T(8,128)(2,1)S(1)} %collective-permute-done.refs_1_, bf16[448,1024]{1,0:T(8,128)(2,1)S(1)} %pad.7.refs_0_), kind=kLoop, calls=%fused_computation | loop fusion | flops 14680064 | bytes 7340032 | tf_op jit(solution)/shard_map/transpose | solution.py:436
  89.1 5.9 %copy.9.tokens_t = bf16[1024,1792]{1,0:T(8,128)(2,1)} copy(bf16[1024,1792]{0,1:T(8,128)(2,1)} %maximum_bitcast_fusion) | data formatting | bytes 7340032 | tf_op jit(solution)/shard_map/transpose | solution.py:436
  95.0 7.5 %all-to-all-done.1.arrived = bf16[64,16,1792]{2,1,0:T(8,128)(2,1)} async-done(((bf16[64,16,1792]{2,1,0:T(8,128)(2,1)}), bf16[64,16,1792]{2,1,0:T(8,128)(2,1)}, u32[]{:S(2)}, u32[]{:S(2)}) %all-to-all-start.1) | async-done | bytes 3670048 | tf_op jit(solution)/shard_map/all_to_all | solution.py:423
  102.4 5.7 %all-to-all-start = ((bf16[64,16,256]{2,1,0:T(8,128)(2,1)}), bf16[64,16,256]{2,1,0:T(8,128)(2,1)S(1)}, u32[]{:S(2)}, u32[]{:S(2)}) async-start(bf16[64,16,256]{2,1,0:T(8,128)(2,1)} %pick.2), calls=%async_computation | async-start | bytes 1048576 | tf_op jit(solution)/shard_map/all_to_all | solution.py:423
  108.2 21.1 %main_delta.1 = (bf16[64,2,16,1024]{3,2,1,0:T(8,128)(2,1)}, bf16[1792,1024]{1,0:T(8,128)(2,1)S(1)}, bf16[1024,1792]{1,0:T(8,128)(2,1)S(1)}, f32[1792,256]{1,0:T(8,128)S(1)}) custom-call(s32[64]{0:T(128)S(1)} %copy-done.13, bf16[64,16,1792]{2,1,0:T(8,128)(2,1)} %all-to-all-done.1.arrived, bf16[1024,1792]{1,0:T(8,128)(2,1)} %copy.9.tokens_t, ...), custom_call_target="tpu_custom_call" | custom-call | flops 15032385536 | bytes 23068672 | tf_op jit(solution)/shard_map/main_delta/pallas_call | solution.py:175
  134.2 2.0 copy-done.2
  139.7 5.7 %last_delta.1 = bf16[64,2,16,1024]{3,2,1,0:T(8,128)(2,1)} custom-call(s32[64]{0:T(128)S(1)} %copy-done.13, bf16[64,16,256]{2,1,0:T(8,128)(2,1)S(1)} %all-to-all-done.arrived, bf16[1792,1024]{1,0:T(8,128)(2,1)S(1)} %copy-done.2, bf16[1024,1792]{1,0:T(8,128)(2,1)S(1)} %copy-done.4, f32[1792,256]{1,0:T(8,128)S(1)} %copy-done.9, ...), custom_call_target="tpu_custom_call", output_to_operand_aliasing={{}: (5, {})} | custom-call | flops 1879048192 | bytes 7340032 | tf_op jit(solution)/shard_map/last_delta/pallas_call | solution.py:228
  145.4 10.7 %all-to-all-start.2 = ((bf16[64,2,16,1024]{3,2,1,0:T(8,128)(2,1)}), bf16[64,2,16,1024]{3,2,1,0:T(8,128)(2,1)}, u32[]{:S(2)}, u32[]{:S(2)}) async-start(bf16[64,2,16,1024]{3,2,1,0:T(8,128)(2,1)} %last_delta.1), calls=%async_computation.2 | async-start | bytes 8388608 | tf_op jit(solution)/shard_map/all_to_all | solution.py:423
  157.7 2.4 ready.1
  162.2 2.1 sort.17
  164.3 87.7 %all-to-all-done.2.received = bf16[64,2,16,1024]{3,2,1,0:T(8,128)(2,1)} async-done(((bf16[64,2,16,1024]{3,2,1,0:T(8,128)(2,1)}), bf16[64,2,16,1024]{3,2,1,0:T(8,128)(2,1)}, u32[]{:S(2)}, u32[]{:S(2)}) %all-to-all-start.2) | async-done | bytes 4194336 | tf_op jit(solution)/shard_map/all_to_all | solution.py:423
  254.6 10.7 %outer.1 = (f32[16,2,16,1024]{3,2,1,0:T(8,128)}, bf16[64,2,16,1024]{3,2,1,0:T(8,128)(2,1)S(1)}) custom-call(s32[17]{0:T(128)S(1)} %get-tuple-element.15.first, s32[64]{0:T(128)S(1)} %get-tuple-element.16.order, bf16[64,2,16,1024]{3,2,1,0:T(8,128)(2,1)} %all-to-all-done.2.received, f32[16,2,16,1024]{3,2,1,0:T(8,128)S(1)} %get-tuple-element.23.base, ...), custom_call_target="tpu_custom_call" | custom-call | flops 2097152 | bytes 8388608 | tf_op jit(solution)/shard_map/outer/pallas_call | solution.py:343
  265.4 101.8 %all_to_all.20.back = bf16[64,2,16,1024]{3,2,1,0:T(8,128)(2,1)} all-to-all(bf16[64,2,16,1024]{3,2,1,0:T(8,128)(2,1)S(1)} %get-tuple-element.27), channel_id=1, replica_groups=mesh['path'=64,'fsdp'=4] {'path'}, dimensions={0} | all-to-all | bytes 8388608 | tf_op jit(solution)/shard_map/all_to_all | solution.py:423
  367.2 3.9 %bring_home.1 = bf16[2,64,16,1024]{3,2,1,0:T(8,128)(2,1)} custom-call(s32[64]{0:T(128)} %owner.5, bf16[64,2,16,1024]{3,2,1,0:T(8,128)(2,1)} %all_to_all.20.back), custom_call_target="tpu_custom_call" | custom-call | bytes 8388608 | tf_op jit(solution)/shard_map/bring_home/pallas_call | solution.py:393
  (48 shorter events, 19.4 us)
Async XLA Ops:
  4.3 13.5 %copy-start.17 = (bf16[440,1024]{1,0:T(8,128)(2,1)S(1)}, bf16[440,1024]{1,0:T(8,128)(2,1)}, u32[]{:S(2)}) copy-start(bf16[440,1024]{1,0:T(8,128)(2,1)} %param.6) | copy-start | bytes 2703364
  4.3 13.6 %copy-start.18 = (bf16[440,1024]{1,0:T(8,128)(2,1)S(1)}, bf16[440,1024]{1,0:T(8,128)(2,1)}, u32[]{:S(2)}) copy-start(bf16[440,1024]{1,0:T(8,128)(2,1)} %param.7) | copy-start | bytes 2703364
  4.3 98.1 %all-to-all-start.1 = ((bf16[64,16,1792]{2,1,0:T(8,128)(2,1)}), bf16[64,16,1792]{2,1,0:T(8,128)(2,1)}, u32[]{:S(2)}, u32[]{:S(2)}) async-start(bf16[64,16,1792]{2,1,0:T(8,128)(2,1)} %pick.3), calls=%async_computation.1 | async-start | bytes 7340032 | tf_op jit(solution)/shard_map/all_to_all | solution.py:423
  17.9 21.8 %collective-permute-start.4 = (bf16[448,1024]{1,0:T(8,128)(2,1)S(1)}, bf16[448,1024]{1,0:T(8,128)(2,1)S(1)}, u32[]{:S(2)}, u32[]{:S(2)}) collective-permute-start(bf16[448,1024]{1,0:T(8,128)(2,1)S(1)} %pad.8.refs_4_), channel_id=1, source_target_pairs={{0,3},{1,0},{2,1},{3,2},{4,7},{5,4},{6,5},{7,6},{8,11},{9,8},{10,9... | collective-permute-start | bytes 2752520 | tf_op jit(solution)/shard_map/ppermute | solution.py:414
  20.5 22.7 %collective-permute-start = (bf16[448,1024]{1,0:T(8,128)(2,1)S(1)}, bf16[448,1024]{1,0:T(8,128)(2,1)S(1)}, u32[]{:S(2)}, u32[]{:S(2)}) collective-permute-start(bf16[448,1024]{1,0:T(8,128)(2,1)S(1)} %pad.7.refs_0_), channel_id=1, source_target_pairs={{0,1},{1,2},{2,3},{3,0},{4,5},{5,6},{6,7},{7,4},{8,9},{9,10},{10,1... | collective-permute-start | bytes 2752520 | tf_op jit(solution)/shard_map/ppermute | solution.py:413
  20.5 42.1 %collective-permute-start.3 = (bf16[448,1024]{1,0:T(8,128)(2,1)S(1)}, bf16[448,1024]{1,0:T(8,128)(2,1)S(1)}, u32[]{:S(2)}, u32[]{:S(2)}) collective-permute-start(bf16[448,1024]{1,0:T(8,128)(2,1)S(1)} %pad.8.refs_4_), channel_id=1, source_target_pairs={{0,1},{1,2},{2,3},{3,0},{4,5},{5,6},{6,7},{7,4},{8,9},{9,10},{10,1... | collective-permute-start | bytes 2752520 | tf_op jit(solution)/shard_map/ppermute | solution.py:415
  39.7 22.9 %copy-start.14 = (bf16[448,1024]{1,0:T(8,128)(2,1)}, bf16[448,1024]{1,0:T(8,128)(2,1)S(1)}, u32[]{:S(2)}) copy-start(bf16[448,1024]{1,0:T(8,128)(2,1)S(1)} %collective-permute-done.4.refs_6_) | copy-start | bytes 2752516
  39.7 22.9 %collective-permute-start.5 = (bf16[448,1024]{1,0:T(8,128)(2,1)S(1)}, bf16[448,1024]{1,0:T(8,128)(2,1)S(1)}, u32[]{:S(2)}, u32[]{:S(2)}) collective-permute-start(bf16[448,1024]{1,0:T(8,128)(2,1)S(1)} %collective-permute-done.4.refs_6_), channel_id=1, source_target_pairs={{0,3},{1,0},{2,1},{3,2},{4,7},{5,4},{6,5},{7,6},{8,11},{9,8},{10,9... | collective-permute-start | bytes 2752520 | tf_op jit(solution)/shard_map/ppermute | solution.py:417
  43.2 38.0 %collective-permute-start.1 = (bf16[448,1024]{1,0:T(8,128)(2,1)S(1)}, bf16[448,1024]{1,0:T(8,128)(2,1)}, u32[]{:S(2)}, u32[]{:S(2)}) collective-permute-start(bf16[448,1024]{1,0:T(8,128)(2,1)S(1)} %pad.7.refs_0_), channel_id=1, source_target_pairs={{0,3},{1,0},{2,1},{3,2},{4,7},{5,4},{6,5},{7,6},{8,11},{9,8},{10,9... | collective-permute-start | bytes 2752520 | tf_op jit(solution)/shard_map/ppermute | solution.py:416
  43.2 39.0 %collective-permute-start.2 = (bf16[448,1024]{1,0:T(8,128)(2,1)S(1)}, bf16[448,1024]{1,0:T(8,128)(2,1)}, u32[]{:S(2)}, u32[]{:S(2)}) collective-permute-start(bf16[448,1024]{1,0:T(8,128)(2,1)S(1)} %collective-permute-done.refs_1_), channel_id=1, source_target_pairs={{0,1},{1,2},{2,3},{3,0},{4,5},{5,6},{6,7},{7,4},{8,9},{9,10},{10,1... | collective-permute-start | bytes 2752520 | tf_op jit(solution)/shard_map/ppermute | solution.py:418
  89.1 19.1 %copy-start.13 = (s32[64]{0:T(128)S(1)}, s32[64]{0:T(128)}, u32[]{:S(2)}) copy-start(s32[64]{0:T(128)} %owner.5) | copy-start | bytes 772
  102.4 31.7 %all-to-all-start = ((bf16[64,16,256]{2,1,0:T(8,128)(2,1)}), bf16[64,16,256]{2,1,0:T(8,128)(2,1)S(1)}, u32[]{:S(2)}, u32[]{:S(2)}) async-start(bf16[64,16,256]{2,1,0:T(8,128)(2,1)} %pick.2), calls=%async_computation | async-start | bytes 1048576 | tf_op jit(solution)/shard_map/all_to_all | solution.py:423
  129.3 1.8 copy-start.1
  131.1 1.8 copy-start.3
  132.9 1.2 copy-start.8
  134.2 2.0 copy-start.2
  136.2 2.0 copy-start.4
  138.2 1.5 copy-start.9
  145.4 10.7 %copy-start = (bf16[16,2,16,1024]{3,2,1,0:T(8,128)(2,1)S(1)}, bf16[16,2,16,1024]{3,2,1,0:T(8,128)(2,1)}, u32[]{:S(2)}) copy-start(bf16[16,2,16,1024]{3,2,1,0:T(8,128)(2,1)} %stored.3) | copy-start | bytes 3145732
  145.4 10.7 %copy-start.12 = (s32[64,1]{0,1:T(1,128)S(1)}, s32[64,1]{0,1:T(1,128)}, u32[]{:S(2)}) copy-start(s32[64,1]{0,1:T(1,128)} %param.10) | copy-start | bytes 772
  145.4 106.5 %all-to-all-start.2 = ((bf16[64,2,16,1024]{3,2,1,0:T(8,128)(2,1)}), bf16[64,2,16,1024]{3,2,1,0:T(8,128)(2,1)}, u32[]{:S(2)}, u32[]{:S(2)}) async-start(bf16[64,2,16,1024]{3,2,1,0:T(8,128)(2,1)} %last_delta.1), calls=%async_computation.2 | async-start | bytes 8388608 | tf_op jit(solution)/shard_map/all_to_all | solution.py:423
  156.1 1.6 copy-start.7
  160.1 1.3 copy-start.5
  252.0 1.6 copy-start.6
  (4 other events, 3.8 us)

commit v6 on v0

v6 whole, which is shorter than its diff:
```python
import functools
import math

import jax
import jax.numpy as jnp
from jax import lax
from jax.experimental import pallas as pl
from jax.experimental.pallas import tpu as pltpu
from jax.sharding import PartitionSpec as P

inner_rate = 10.0
outer_rate = 0.7
outer_decay = 0.9

VMEM_LIMIT = 56 * 1024 * 1024
ANY = pl.BlockSpec(memory_space=pl.ANY)
SMEM = pl.BlockSpec(memory_space=pltpu.SMEM)
VMEM = pl.BlockSpec(memory_space=pltpu.VMEM)


def params():
    return pltpu.CompilerParams(vmem_limit_bytes=VMEM_LIMIT)


def cost(flops, moved):
    return pl.CostEstimate(flops=flops, bytes_accessed=moved, transcendentals=0)


def wait_bytes(ref, sem):
    pltpu.make_async_copy(ref, ref, sem).wait()


def f32_dot(left, right):
    return jnp.dot(left, right, preferred_element_type=jnp.float32)


def pick_kernel(module_of, stored, out, sem):
    @pl.loop(0, out.shape[0], unroll=8)
    def _(path):
        pltpu.make_async_copy(stored.at[module_of[path]], out.at[path], sem).start()

    wait_bytes(out, sem)


def pick(module_of, stored):
    paths = module_of.shape[0]
    shape = (paths,) + stored.shape[1:]
    return pl.pallas_call(
        pick_kernel,
        out_shape=jax.ShapeDtypeStruct(shape, stored.dtype),
        in_specs=[SMEM, VMEM],
        out_specs=ANY,
        scratch_shapes=[pltpu.SemaphoreType.DMA],
        compiler_params=params(),
        cost_estimate=cost(0, 2 * math.prod(shape)),
        name="pick",
    )(module_of, stored)


def sigmoid(values):
    return 1.0 / (1.0 + jnp.exp(-values))


def delta_kernel(scales, tiles, owner, arrived, order, tokens_t, grads_t, *refs):
    scale_in, scale_hid, rate = scales
    tile_cols, tile_rows = tiles
    tok_in, grd_in = refs[:4], refs[4:8]
    out, weight, tok, grd, tok_t, grd_t, act, slope, delta, sems = refs[8:]
    rows = arrived.shape[2]
    each = tok_in[0].shape[0]

    def start(source, target, sem):
        copy = pltpu.make_async_copy(source, target, sems.at[sem])
        copy.start()
        return copy

    def load(shards_in, target, i, sem):
        return start(shards_in[i], target.at[pl.ds(i * each, each)], sem + i)

    loads = [[load(tok_in, tok, 0, 4), load(tok_in, tok, 1, 4)]]

    @pl.loop(0, arrived.shape[0], unroll=8)
    def _(block):
        pltpu.make_async_copy(
            arrived.at[owner[block]],
            weight.at[:, pl.ds(pl.multiple_of(block * rows, rows), rows)],
            sems.at[0],
        ).start()

    loads[0] += [load(grd_in, grd, 0, 8), load(grd_in, grd, 1, 8)]
    wait_bytes(weight, sems.at[0])
    for part in range(2):
        at = pl.ds(part * 2 * each, 2 * each)
        for copy in loads[part]:
            copy.wait()
        if part == 0:
            loads.append([load(tok_in, tok, i, 4) for i in (2, 3)])
            loads[1] += [load(grd_in, grd, i, 8) for i in (2, 3)]
            late = [start(grads_t, grd_t, 2), start(tokens_t, tok_t, 3)]

        @pl.loop(0, act.shape[1] // tile_cols)
        def _(step):
            cols = pl.ds(pl.multiple_of(step * tile_cols, tile_cols), tile_cols)
            pre = f32_dot(tok[at, :], weight[0, :, cols]) * scale_in
            back = f32_dot(grd[at, :], weight[1, :, cols]) * scale_hid
            sig = sigmoid(pre)
            act[at, cols] = (pre * sig).astype(jnp.bfloat16)
            slope[at, cols] = (back * (sig * (1.0 + pre * (1.0 - sig)))).astype(jnp.bfloat16)

    for copy in late:
        copy.wait()

    @pl.loop(0, delta.shape[1] // tile_rows)
    def _(step):
        at = pl.ds(pl.multiple_of(step * tile_rows, tile_rows), tile_rows)
        grad_down = f32_dot(grd_t[at, :], act[...]) * scale_hid
        delta[1, at, :] = (grad_down * rate).astype(jnp.bfloat16)
        grad_up = f32_dot(tok_t[at, :], slope[...]) * scale_in
        delta[0, at, :] = (grad_up * rate).astype(jnp.bfloat16)

        @pl.loop(0, tile_rows // rows, unroll=8)
        def _(inner):
            block = step * (tile_rows // rows) + inner
            pltpu.make_async_copy(
                delta.at[:, pl.ds(pl.multiple_of(block * rows, rows), rows)],
                out.at[owner[block]],
                sems.at[1],
            ).start()

    wait_bytes(delta, sems.at[1])


def path_delta(scales, owner, arrived, order, tokens, grads, tokens_t, grads_t):
    _, halves, _, cols = arrived.shape
    width, count = tokens_t.shape
    bf16 = jnp.bfloat16
    return pl.pallas_call(
        functools.partial(delta_kernel, scales, (1024, 512)),
        out_shape=jax.ShapeDtypeStruct(arrived.shape, bf16),
        in_specs=[SMEM] + [ANY] * 12,
        out_specs=ANY,
        scratch_shapes=[
            pltpu.VMEM((halves, width, cols), bf16),
            pltpu.VMEM((count, width), bf16),
            pltpu.VMEM((count, width), bf16),
            pltpu.VMEM((width, count), bf16),
            pltpu.VMEM((width, count), bf16),
            pltpu.VMEM((count, cols), bf16),
            pltpu.VMEM((count, cols), bf16),
            pltpu.VMEM((halves, width, cols), bf16),
            pltpu.SemaphoreType.DMA((12,)),
        ],
        compiler_params=params(),
        cost_estimate=cost(8 * count * width * cols, 8 * (count * width + width * cols)),
        name="path_delta",
    )(owner, arrived, order, tokens_t, grads_t, *tokens, *grads)


def outer_kernel(
    module_of, order, received, master, momentum, new_state, sending,
    got, mas, mom, state, updated, share, first, sems,
):
    modules, halves, rows, cols = state.shape
    step = outer_rate * (1.0 + outer_decay)
    loads = []
    for half in range(halves):
        sources = (received.at[:, half], master.at[:, half], momentum.at[:, half])
        targets = (got.at[half], mas.at[half], mom.at[half])
        loads.append(
            [
                pltpu.make_async_copy(source, target, sems.at[3 * half + i])
                for i, (source, target) in enumerate(zip(sources, targets, strict=True))
            ]
        )
        for load in loads[half]:
            load.start()

    for module in range(modules + 1):
        first[module] = 0

    @pl.loop(0, module_of.shape[0], unroll=8)
    def _(path):
        first[module_of[path] + 1] += 1

    for module in range(modules):
        count = jnp.full(share.shape[1:], first[module + 1], jnp.int32)
        share[module] = 1.0 / count.astype(jnp.float32)
        first[module + 1] += first[module]

    for half in range(halves):
        for load in loads[half]:
            load.wait()

        @pl.loop(0, modules)
        def _(module):
            begin, end = first[module], first[module + 1]
            total = lax.fori_loop(
                begin,
                end,
                lambda i, acc: acc + got[half, order[i]].astype(jnp.float32),
                jnp.zeros((rows, cols), jnp.float32),
            )
            averaged = (total.reshape(-1, 8, cols) * share[module]).reshape(rows, cols)
            kept = outer_decay * mom[half, module]
            state[module, half] = kept + averaged
            weights = mas[half, module].astype(jnp.float32)
            updated[module, half] = (
                weights - (outer_rate * outer_decay) * kept - step * averaged
            ).astype(jnp.bfloat16)
            if half == halves - 1:
                pltpu.make_async_copy(
                    state.at[module], new_state.at[module], sems.at[6]
                ).start()

                @pl.loop(begin, end)
                def _(i):
                    pltpu.make_async_copy(
                        updated.at[module], sending.at[order[i]], sems.at[7]
                    ).start()

    wait_bytes(sending, sems.at[7])
    wait_bytes(state, sems.at[6])


def outer(module_of, order, received, master, momentum):
    paths, halves, rows, cols = received.shape
    modules = master.shape[0]
    f32, bf16 = jnp.float32, jnp.bfloat16
    return pl.pallas_call(
        outer_kernel,
        out_shape=(
            jax.ShapeDtypeStruct(momentum.shape, f32),
            jax.ShapeDtypeStruct(received.shape, bf16),
        ),
        in_specs=[SMEM, SMEM, ANY, ANY, ANY],
        out_specs=(ANY, ANY),
        scratch_shapes=[
            pltpu.VMEM((halves, paths, rows, cols), bf16),
            pltpu.VMEM((halves, modules, rows, cols), bf16),
            pltpu.VMEM((halves, modules, rows, cols), f32),
            pltpu.VMEM(momentum.shape, f32),
            pltpu.VMEM(master.shape, bf16),
            pltpu.VMEM((modules, 8, cols), f32),
            pltpu.SMEM((modules + 1,), jnp.int32),
            pltpu.SemaphoreType.DMA((8,)),
        ],
        compiler_params=params(),
        cost_estimate=cost(2 * paths * rows * cols, 8 * paths * rows * cols),
        name="outer",
    )(module_of, order, received, master, momentum)


def home_kernel(groups, owner, back, out, buf, place, sems):
    per = back.shape[0] // groups
    loads = []
    for group in range(groups):
        part = pl.ds(group * per, per)
        loads.append(
            pltpu.make_async_copy(back.at[part], buf.at[part], sems.at[group])
        )
        loads[-1].start()

    @pl.loop(0, back.shape[0], unroll=8)
    def _(block):
        place[owner[block]] = block

    for group in range(groups):
        loads[group].wait()

        @pl.loop(0, per, unroll=8)
        def _(inner):
            holder = group * per + inner
            pltpu.make_async_copy(
                buf.at[holder], out.at[:, place[holder]], sems.at[groups]
            ).start()

    wait_bytes(buf, sems.at[groups])


def bring_home(owner, back):
    paths, halves, rows, cols = back.shape
    groups = 4
    return pl.pallas_call(
        functools.partial(home_kernel, groups),
        out_shape=jax.ShapeDtypeStruct((halves, paths, rows, cols), back.dtype),
        in_specs=[SMEM, ANY],
        out_specs=ANY,
        scratch_shapes=[
            pltpu.VMEM(back.shape, back.dtype),
            pltpu.SMEM((paths,), jnp.int32),
            pltpu.SemaphoreType.DMA((groups + 1,)),
        ],
        compiler_params=params(),
        cost_estimate=cost(0, 4 * paths * halves * rows * cols),
        name="bring_home",
    )(owner, back)


def collect(tokens, grads):
    count = lax.axis_size("fsdp")
    right = [(i, (i + 1) % count) for i in range(count)]
    left = [(i, (i - 1) % count) for i in range(count)]
    tok_left = lax.ppermute(tokens, "fsdp", right)
    grd_right = lax.ppermute(grads, "fsdp", left)
    grd_left = lax.ppermute(grads, "fsdp", right)
    tok_right = lax.ppermute(tokens, "fsdp", left)
    grd_far = lax.ppermute(grd_right, "fsdp", left)
    tok_far = lax.ppermute(tok_left, "fsdp", right)
    return (tokens, tok_left, tok_right, tok_far), (grads, grd_left, grd_right, grd_far)


def exchange(blocks):
    return lax.all_to_all(blocks, "path", split_axis=0, concat_axis=0, tiled=True)


def shards(inputs, cotangent, master, momentum, sharing, block_owner):
    block_cols = master.shape[3]
    module_of = sharing[:, 0]
    order = jnp.argsort(module_of)
    fsdp = lax.axis_size("fsdp")
    rows, model_width = inputs.shape
    fill = ((0, -rows % 64), (0, 0))
    tokens, grads = collect(
        *lax.optimization_barrier((jnp.pad(inputs, fill), jnp.pad(cotangent, fill)))
    )
    tokens_t, grads_t = jnp.concatenate(tokens).T, jnp.concatenate(grads).T
    scales = (
        1.0 / math.sqrt(model_width),
        1.0 / math.sqrt(block_cols * fsdp),
        inner_rate / math.sqrt(rows * fsdp),
    )
    arrived = exchange(pick(module_of, master))
    delta = path_delta(
        scales, block_owner, arrived, order, tokens, grads, tokens_t, grads_t
    )
    new_state, sending = outer(module_of, order, exchange(delta), master, momentum)
    own_module = bring_home(block_owner, exchange(sending))
    return (new_state, own_module.reshape(1, 2, model_width, block_cols))


def solution(mesh):
    placed = (
        P(("path", "fsdp"), None),
        P(("path", "fsdp"), None),
        P(None, None, "path", "fsdp"),
        P(None, None, "path", "fsdp"),
        P(),
        P(),
    )
    return jax.shard_map(
        shards,
        mesh=mesh,
        in_specs=placed,
        out_specs=(P(None, None, "path", "fsdp"), P("path", None, None, "fsdp")),
        check_vma=False,
    )
```

time: 435 us -> 351 us (0.81)
  waiting for transfers between devices: 283 us -> 64.7 us
  blocking collectives: 0 us -> 204 us
  matrix products: 37.7 us -> 0 us
  Pallas kernels: 0 us -> 36.4 us
  local copies, waits for them, and re-layouts: 46.7 us -> 12.1 us
  other arithmetic: 26.6 us -> 12.3 us
  between operations: 14.2 us -> 0.93 us
  starting transfers between devices: 25.4 us -> 20.2 us
    all_to_all x3 -> x1, waiting for transfers between devices: 282 us -> 22.1 us  [exchange(): lax.all_to_all(blocks, 'path', split_axis=0, concat_axis=0, tiled=True)]
    all_to_all x0 -> x2, blocking collectives: none -> 204 us  [exchange(): lax.all_to_all(blocks, 'path', split_axis=0, concat_axis=0, tiled=True)]
    ppermute x0 -> x6, waiting for transfers between devices: none -> 42.6 us  [the longest x1 18.8 us: collect(): tok_left = lax.ppermute(tokens, 'fsdp', right)]
    dot_general x4 -> x0, matrix products: 37.7 us -> none  [the longest x1 15.5 us: shards(): lax.dot_general(tokens_all, slope_grad, (((0,), (0,)), ((), ())), preferr...]
    pallas_call x0 -> x4, Pallas kernels: none -> 36.4 us  [the longest x1 22.6 us: path_delta(): pl.pallas_call(functools.partial(delta_kernel, scales, (1024, 512)), out_...]
    gather x5 -> x0, local copies, waits for them, and re-layouts: 21.8 us -> none  [the longest x1 5.01 us: shards(): jnp.take(arrived, block_owner, axis=1).reshape(2, model_width, block_cols)]
    select_n x8 -> x0, other arithmetic: 19.8 us -> none  [the longest x2 5.3 us: shards(): outgoing = jnp.take(ordered, module_of, axis=1)]
    reshape x2 -> x0, local copies, waits for them, and re-layouts: 12.4 us -> none  [shards(): received.reshape(2, path_count, block_rows * block_cols)]
  transfers between devices with their start and end apart: 5 -> 7, of which waited for: 3 -> 5; matrix products, arithmetic and copies ran while one was open for 8% -> 7% of each run, Pallas kernels for 0% -> 0%
where the time goes in v6:
time: 351 us
  blocking collectives  204 us (58%)
  waiting for transfers between devices  64.7 us (18%)
  Pallas kernels  36.4 us (10%)
  starting transfers between devices  20.2 us (6%)
  other arithmetic  12.3 us (4%)
  local copies, waits for them, and re-layouts  12.1 us (3%)
    all_to_all x2, blocking collectives, exchange(): lax.all_to_all(blocks, 'path', split_axis=0, concat_axis=0, tiled=True)  204 us
    pallas_call x1, Pallas kernels, path_delta(): pl.pallas_call(functools.partial(delta_kernel, scales, (1024, 512)), out_...  22.6 us
    all_to_all x1, waiting for transfers between devices, exchange(): lax.all_to_all(blocks, 'path', split_axis=0, concat_axis=0, tiled=True)  22.1 us
    ppermute x1, waiting for transfers between devices, collect(): tok_left = lax.ppermute(tokens, 'fsdp', right)  18.8 us
    ppermute x1, waiting for transfers between devices, collect(): tok_right = lax.ppermute(tokens, 'fsdp', left)  14.5 us
    all_to_all x1, starting transfers between devices, exchange(): lax.all_to_all(blocks, 'path', split_axis=0, concat_axis=0, tiled=True)  13.5 us
    transpose x2, local copies, waits for them, and re-layouts, shards(): tokens_t, grads_t = (jnp.concatenate(tokens).T, jnp.concatenate(grads).T)  11.9 us
    transpose x2, other arithmetic, shards(): tokens_t, grads_t = (jnp.concatenate(tokens).T, jnp.concatenate(grads).T)  10.2 us
  transfers between devices with their start and end apart: 7, of which 5 were waited for; matrix products, arithmetic and copies ran while one was open for 7% of the time, Pallas kernels for 0%

profile of v6, /device:TPU:1, one launch (start us, length us, event | category | flops | bytes accessed | tf_op | source)
XLA Modules:
  0.0 350.8 jit_solution(7364703101616429386)
XLA Ops:
  0.6 3.2 pick.1
  3.9 13.5 %all-to-all-start = ((bf16[64,2,16,1024]{3,2,1,0:T(8,128)(2,1)}), bf16[64,2,16,1024]{3,2,1,0:T(8,128)(2,1)}, u32[]{:S(2)}, u32[]{:S(2)}) async-start(bf16[64,2,16,1024]{3,2,1,0:T(8,128)(2,1)} %pick.1), calls=%async_computation | async-start | bytes 8388608 | tf_op jit(solution)/shard_map/all_to_all | solution.py:313
  17.4 0.1 pad.7.refs_0_
  17.5 0.1 pad.8.refs_4_
  17.6 1.3 collective-permute-start
  18.8 1.5 collective-permute-start.4
  20.3 1.3 collective-permute-start.1
  21.6 18.8 %collective-permute-done.refs_1_ = bf16[448,1024]{1,0:T(8,128)(2,1)S(1)} collective-permute-done((bf16[448,1024]{1,0:T(8,128)(2,1)S(1)}, bf16[448,1024]{1,0:T(8,128)(2,1)S(1)}, u32[]{:S(2)}, u32[]{:S(2)}) %collective-permute-start) | collective-permute-done | bytes 917536 | tf_op jit(solution)/shard_map/ppermute | solution.py:303
  40.3 1.2 collective-permute-start.3
  41.5 1.5 collective-permute-start.5
  43.1 2.1 sort.17
  45.1 14.5 %collective-permute-done.1.refs_2_ = bf16[448,1024]{1,0:T(8,128)(2,1)} collective-permute-done((bf16[448,1024]{1,0:T(8,128)(2,1)S(1)}, bf16[448,1024]{1,0:T(8,128)(2,1)}, u32[]{:S(2)}, u32[]{:S(2)}) %collective-permute-start.1) | collective-permute-done | bytes 917536 | tf_op jit(solution)/shard_map/ppermute | solution.py:306
  59.7 2.5 collective-permute-done.2.refs_3_
  62.2 6.9 %maximum_bitcast_fusion = bf16[1024,1792]{0,1:T(8,128)(2,1)} fusion(bf16[448,1024]{1,0:T(8,128)(2,1)} %collective-permute-done.2.refs_3_, bf16[448,1024]{1,0:T(8,128)(2,1)} %collective-permute-done.1.refs_2_, bf16[448,1024]{1,0:T(8,128)(2,1)S(1)} %collective-permute-done.refs_1_, bf16[448,1024]{1,0:T(8,128)(2,1)S(1)} %pad.7.refs_0_), kind=kLoop, calls=%fused_computation | loop fusion | flops 14680064 | bytes 7340032 | tf_op jit(solution)/shard_map/transpose | solution.py:326
  69.1 6.0 %copy.8.tokens_t = bf16[1024,1792]{1,0:T(8,128)(2,1)} copy(bf16[1024,1792]{0,1:T(8,128)(2,1)} %maximum_bitcast_fusion) | data formatting | bytes 7340032 | tf_op jit(solution)/shard_map/transpose | solution.py:326
  75.1 6.8 %collective-permute-done.3.refs_5_ = bf16[448,1024]{1,0:T(8,128)(2,1)} collective-permute-done((bf16[448,1024]{1,0:T(8,128)(2,1)S(1)}, bf16[448,1024]{1,0:T(8,128)(2,1)}, u32[]{:S(2)}, u32[]{:S(2)}) %collective-permute-start.3) | collective-permute-done | bytes 917536 | tf_op jit(solution)/shard_map/ppermute | solution.py:305
  81.9 3.3 maximum_bitcast_fusion.1
  85.2 5.9 %copy.9.grads_t = bf16[1024,1792]{1,0:T(8,128)(2,1)} copy(bf16[1024,1792]{0,1:T(8,128)(2,1)} %maximum_bitcast_fusion.1) | data formatting | bytes 7340032 | tf_op jit(solution)/shard_map/transpose | solution.py:326
  91.1 22.1 %all-to-all-done.arrived = bf16[64,2,16,1024]{3,2,1,0:T(8,128)(2,1)} async-done(((bf16[64,2,16,1024]{3,2,1,0:T(8,128)(2,1)}), bf16[64,2,16,1024]{3,2,1,0:T(8,128)(2,1)}, u32[]{:S(2)}, u32[]{:S(2)}) %all-to-all-start) | async-done | bytes 4194336 | tf_op jit(solution)/shard_map/all_to_all | solution.py:313
  113.3 22.6 %path_delta.1 = bf16[64,2,16,1024]{3,2,1,0:T(8,128)(2,1)} custom-call(s32[64]{0:T(128)} %owner.3, bf16[64,2,16,1024]{3,2,1,0:T(8,128)(2,1)} %all-to-all-done.arrived, s32[64]{0:T(128)} %get-tuple-element.7.order, bf16[1024,1792]{1,0:T(8,128)(2,1)} %copy.8.tokens_t, bf16[1024,1792]{1,0:T(8,128)(2,1)} %copy.9.grads_t, bf16[448,1024]{1,0:T(8,128)(2,1)} %copy-done, ...), custom_call_target="tpu_custom_call" | custom-call | flops 15032385536 | bytes 23068672 | tf_op jit(solution)/shard_map/path_delta/pallas_call | solution.py:137
  135.9 102.0 %all_to_all.15.received = bf16[64,2,16,1024]{3,2,1,0:T(8,128)(2,1)} all-to-all(bf16[64,2,16,1024]{3,2,1,0:T(8,128)(2,1)} %path_delta.1), channel_id=1, replica_groups=mesh['path'=64,'fsdp'=4] {'path'}, dimensions={0} | all-to-all | bytes 8388608 | tf_op jit(solution)/shard_map/all_to_all | solution.py:313
  238.0 6.6 %outer.1 = (f32[16,2,16,1024]{3,2,1,0:T(8,128)}, bf16[64,2,16,1024]{3,2,1,0:T(8,128)(2,1)}) custom-call(s32[64]{0:T(128)} %bitcast.8, s32[64]{0:T(128)} %get-tuple-element.7.order, bf16[64,2,16,1024]{3,2,1,0:T(8,128)(2,1)} %all_to_all.15.received, bf16[16,2,16,1024]{3,2,1,0:T(8,128)(2,1)} %master.1, f32[16,2,16,1024]{3,2,1,0:T(8,128)} %momentum.1), custom_call_target="tpu_custom_call" | custom-call | flops 2097152 | bytes 8388608 | tf_op jit(solution)/shard_map/outer/pallas_call | solution.py:229
  244.6 102.1 %all_to_all.16.back = bf16[64,2,16,1024]{3,2,1,0:T(8,128)(2,1)} all-to-all(bf16[64,2,16,1024]{3,2,1,0:T(8,128)(2,1)} %get-tuple-element.11), channel_id=1, replica_groups=mesh['path'=64,'fsdp'=4] {'path'}, dimensions={0} | all-to-all | bytes 8388608 | tf_op jit(solution)/shard_map/all_to_all | solution.py:313
  346.7 3.9 %bring_home.1 = bf16[2,64,16,1024]{3,2,1,0:T(8,128)(2,1)} custom-call(s32[64]{0:T(128)} %owner.3, bf16[64,2,16,1024]{3,2,1,0:T(8,128)(2,1)} %all_to_all.16.back), custom_call_target="tpu_custom_call" | custom-call | bytes 8388608 | tf_op jit(solution)/shard_map/bring_home/pallas_call | solution.py:283
  (16 shorter events, 0.0 us)
Async XLA Ops:
  3.8 13.5 %copy-start.3 = (bf16[440,1024]{1,0:T(8,128)(2,1)S(1)}, bf16[440,1024]{1,0:T(8,128)(2,1)}, u32[]{:S(2)}) copy-start(bf16[440,1024]{1,0:T(8,128)(2,1)} %param.6) | copy-start | bytes 2703364
  3.9 13.6 %copy-start.4 = (bf16[440,1024]{1,0:T(8,128)(2,1)S(1)}, bf16[440,1024]{1,0:T(8,128)(2,1)}, u32[]{:S(2)}) copy-start(bf16[440,1024]{1,0:T(8,128)(2,1)} %param.7) | copy-start | bytes 2703364
  3.9 39.2 %copy-start.5 = (s32[64,1]{0,1:T(1,128)S(1)}, s32[64,1]{0,1:T(1,128)}, u32[]{:S(2)}) copy-start(s32[64,1]{0,1:T(1,128)} %param.10) | copy-start | bytes 772
  3.9 109.4 %all-to-all-start = ((bf16[64,2,16,1024]{3,2,1,0:T(8,128)(2,1)}), bf16[64,2,16,1024]{3,2,1,0:T(8,128)(2,1)}, u32[]{:S(2)}, u32[]{:S(2)}) async-start(bf16[64,2,16,1024]{3,2,1,0:T(8,128)(2,1)} %pick.1), calls=%async_computation | async-start | bytes 8388608 | tf_op jit(solution)/shard_map/all_to_all | solution.py:313
  17.5 51.6 %copy-start = (bf16[448,1024]{1,0:T(8,128)(2,1)}, bf16[448,1024]{1,0:T(8,128)(2,1)S(1)}, u32[]{:S(2)}) copy-start(bf16[448,1024]{1,0:T(8,128)(2,1)S(1)} %pad.7.refs_0_) | copy-start | bytes 2752516
  17.5 64.3 %copy-start.1 = (bf16[448,1024]{1,0:T(8,128)(2,1)}, bf16[448,1024]{1,0:T(8,128)(2,1)S(1)}, u32[]{:S(2)}) copy-start(bf16[448,1024]{1,0:T(8,128)(2,1)S(1)} %pad.8.refs_4_) | copy-start | bytes 2752516
  17.6 22.8 %collective-permute-start = (bf16[448,1024]{1,0:T(8,128)(2,1)S(1)}, bf16[448,1024]{1,0:T(8,128)(2,1)S(1)}, u32[]{:S(2)}, u32[]{:S(2)}) collective-permute-start(bf16[448,1024]{1,0:T(8,128)(2,1)S(1)} %pad.7.refs_0_), channel_id=1, source_target_pairs={{0,1},{1,2},{2,3},{3,0},{4,5},{5,6},{6,7},{7,4},{8,9},{9,10},{10,1... | collective-permute-start | bytes 2752520 | tf_op jit(solution)/shard_map/ppermute | solution.py:303
  18.8 22.7 %collective-permute-start.4 = (bf16[448,1024]{1,0:T(8,128)(2,1)S(1)}, bf16[448,1024]{1,0:T(8,128)(2,1)}, u32[]{:S(2)}, u32[]{:S(2)}) collective-permute-start(bf16[448,1024]{1,0:T(8,128)(2,1)S(1)} %pad.8.refs_4_), channel_id=1, source_target_pairs={{0,3},{1,0},{2,1},{3,2},{4,7},{5,4},{6,5},{7,6},{8,11},{9,8},{10,9... | collective-permute-start | bytes 2752520 | tf_op jit(solution)/shard_map/ppermute | solution.py:304
  20.3 39.4 %collective-permute-start.1 = (bf16[448,1024]{1,0:T(8,128)(2,1)S(1)}, bf16[448,1024]{1,0:T(8,128)(2,1)}, u32[]{:S(2)}, u32[]{:S(2)}) collective-permute-start(bf16[448,1024]{1,0:T(8,128)(2,1)S(1)} %pad.7.refs_0_), channel_id=1, source_target_pairs={{0,3},{1,0},{2,1},{3,2},{4,7},{5,4},{6,5},{7,6},{8,11},{9,8},{10,9... | collective-permute-start | bytes 2752520 | tf_op jit(solution)/shard_map/ppermute | solution.py:306
  40.3 34.8 %copy-start.2 = (bf16[448,1024]{1,0:T(8,128)(2,1)}, bf16[448,1024]{1,0:T(8,128)(2,1)S(1)}, u32[]{:S(2)}) copy-start(bf16[448,1024]{1,0:T(8,128)(2,1)S(1)} %collective-permute-done.refs_1_) | copy-start | bytes 2752516
  40.3 21.9 %collective-permute-start.2 = (bf16[448,1024]{1,0:T(8,128)(2,1)S(1)}, bf16[448,1024]{1,0:T(8,128)(2,1)}, u32[]{:S(2)}, u32[]{:S(2)}) collective-permute-start(bf16[448,1024]{1,0:T(8,128)(2,1)S(1)} %collective-permute-done.refs_1_), channel_id=1, source_target_pairs={{0,1},{1,2},{2,3},{3,0},{4,5},{5,6},{6,7},{7,4},{8,9},{9,10},{10,1... | collective-permute-start | bytes 2752520 | tf_op jit(solution)/shard_map/ppermute | solution.py:308
  40.3 41.5 %collective-permute-start.3 = (bf16[448,1024]{1,0:T(8,128)(2,1)S(1)}, bf16[448,1024]{1,0:T(8,128)(2,1)}, u32[]{:S(2)}, u32[]{:S(2)}) collective-permute-start(bf16[448,1024]{1,0:T(8,128)(2,1)S(1)} %pad.8.refs_4_), channel_id=1, source_target_pairs={{0,1},{1,2},{2,3},{3,0},{4,5},{5,6},{6,7},{7,4},{8,9},{9,10},{10,1... | collective-permute-start | bytes 2752520 | tf_op jit(solution)/shard_map/ppermute | solution.py:305
  41.5 40.3 %collective-permute-start.5 = (bf16[448,1024]{1,0:T(8,128)(2,1)}, bf16[448,1024]{1,0:T(8,128)(2,1)}, u32[]{:S(2)}, u32[]{:S(2)}) collective-permute-start(bf16[448,1024]{1,0:T(8,128)(2,1)} %collective-permute-done.4.refs_6_), channel_id=1, source_target_pairs={{0,3},{1,0},{2,1},{3,2},{4,7},{5,4},{6,5},{7,6},{8,11},{9,8},{10,9... | collective-permute-start | bytes 2752520 | tf_op jit(solution)/shard_map/ppermute | solution.py:307

commit v7 on v6

--- a/solution.py
+++ b/solution.py
@@ -61,23 +61,105 @@
     return 1.0 / (1.0 + jnp.exp(-values))
 
 
-def delta_kernel(scales, tiles, owner, arrived, order, tokens_t, grads_t, *refs):
-    scale_in, scale_hid, rate = scales
-    tile_cols, tile_rows = tiles
-    tok_in, grd_in = refs[:4], refs[4:8]
-    out, weight, tok, grd, tok_t, grd_t, act, slope, delta, sems = refs[8:]
-    rows = arrived.shape[2]
-    each = tok_in[0].shape[0]
-
+def starter(sems):
     def start(source, target, sem):
         copy = pltpu.make_async_copy(source, target, sems.at[sem])
         copy.start()
         return copy
 
-    def load(shards_in, target, i, sem):
-        return start(shards_in[i], target.at[pl.ds(i * each, each)], sem + i)
-
-    loads = [[load(tok_in, tok, 0, 4), load(tok_in, tok, 1, 4)]]
+    return start
+
+
+def load_pair(start, shards_in, target, pair, sem):
+    each = shards_in[0].shape[0]
+    return [
+        start(shards_in[i], target.at[pl.ds(i * each, each)], sem + i)
+        for i in (2 * pair, 2 * pair + 1)
+    ]
+
+
+def send_rows(owner, delta, out, step, tile, sem):
+    rows = out.shape[-2]
+
+    @pl.loop(0, tile // rows, unroll=8)
+    def _(inner):
+        block = step * (tile // rows) + inner
+        pltpu.make_async_copy(
+            delta.at[:, pl.ds(pl.multiple_of(block * rows, rows), rows)],
+            out.at[owner[block]],
+            sem,
+        ).start()
+
+
+def first_kernel(scales, owner, arrived, order, grads_t, *refs):
+    scale_in, scale_hid, rate = scales
+    tok_in = refs[:4]
+    out, weight, tok, grd_t, act, delta, sems = refs[4:]
+    rows, cut = out.shape[2:]
+    start = starter(sems)
+    loads = [load_pair(start, tok_in, tok, 0, 3)]
+
+    @pl.loop(0, arrived.shape[0], unroll=8)
+    def _(block):
+        pltpu.make_async_copy(
+            arrived.at[owner[block], 0, :, pl.ds(0, cut)],
+            weight.at[pl.ds(pl.multiple_of(block * rows, rows), rows)],
+            sems.at[0],
+        ).start()
+
+    loads.append(load_pair(start, tok_in, tok, 1, 3))
+    grads_copy = start(grads_t, grd_t, 2)
+    wait_bytes(weight, sems.at[0])
+    half = tok.shape[0] // 2
+    for part in range(2):
+        at = pl.ds(part * half, half)
+        for copy in loads[part]:
+            copy.wait()
+        pre = f32_dot(tok[at, :], weight[...]) * scale_in
+        act[at, :] = (pre * sigmoid(pre)).astype(jnp.bfloat16)
+    grads_copy.wait()
+    tile = 512
+
+    @pl.loop(0, delta.shape[1] // tile)
+    def _(step):
+        at = pl.ds(pl.multiple_of(step * tile, tile), tile)
+        grad = f32_dot(grd_t[at, :], act[...]) * scale_hid
+        delta[0, at, :] = (grad * rate).astype(jnp.bfloat16)
+        send_rows(owner, delta, out, step, tile, sems.at[1])
+
+    wait_bytes(delta, sems.at[1])
+
+
+def delta_first(scales, cut, owner, arrived, order, tokens, grads_t):
+    paths, _, rows, _ = arrived.shape
+    width, count = grads_t.shape
+    bf16 = jnp.bfloat16
+    return pl.pallas_call(
+        functools.partial(first_kernel, scales),
+        out_shape=jax.ShapeDtypeStruct((paths, 1, rows, cut), bf16),
+        in_specs=[SMEM] + [ANY] * 7,
+        out_specs=ANY,
+        scratch_shapes=[
+            pltpu.VMEM((width, cut), bf16),
+            pltpu.VMEM((count, width), bf16),
+            pltpu.VMEM((width, count), bf16),
+            pltpu.VMEM((count, cut), bf16),
+            pltpu.VMEM((1, width, cut), bf16),
+            pltpu.SemaphoreType.DMA((7,)),
+        ],
+        compiler_params=params(),
+        cost_estimate=cost(4 * count * width * cut, 4 * (count * width + width * cut)),
+        name="delta_first",
+    )(owner, arrived, order, grads_t, *tokens)
+
+
+def rest_kernel(scales, owner, arrived, earlier, tokens_t, grads_t, *refs):
+    scale_in, scale_hid, rate = scales
+    tok_in, grd_in = refs[:4], refs[4:8]
+    out, weight, tok, grd, tok_t, grd_t, act, slope, delta, sems = refs[8:]
+    rows, cut = out.shape[2:]
+    start = starter(sems)
+    loads = [load_pair(start, tok_in, tok, 0, 4)]
 
     @pl.loop(0, arrived.shape[0], unroll=8)
     def _(block):
@@ -87,56 +169,46 @@
             sems.at[0],
         ).start()
 
-    loads[0] += [load(grd_in, grd, 0, 8), load(grd_in, grd, 1, 8)]
+    loads[0] += load_pair(start, grd_in, grd, 0, 8)
     wait_bytes(weight, sems.at[0])
+    half = tok.shape[0] // 2
     for part in range(2):
-        at = pl.ds(part * 2 * each, 2 * each)
+        at = pl.ds(part * half, half)
         for copy in loads[part]:
             copy.wait()
         if part == 0:
-            loads.append([load(tok_in, tok, i, 4) for i in (2, 3)])
-            loads[1] += [load(grd_in, grd, i, 8) for i in (2, 3)]
+            loads.append(load_pair(start, tok_in, tok, 1, 4) + load_pair(start, grd_in, grd, 1, 8))
             late = [start(grads_t, grd_t, 2), start(tokens_t, tok_t, 3)]
-
-        @pl.loop(0, act.shape[1] // tile_cols)
-        def _(step):
-            cols = pl.ds(pl.multiple_of(step * tile_cols, tile_cols), tile_cols)
-            pre = f32_dot(tok[at, :], weight[0, :, cols]) * scale_in
-            back = f32_dot(grd[at, :], weight[1, :, cols]) * scale_hid
-            sig = sigmoid(pre)
-            act[at, cols] = (pre * sig).astype(jnp.bfloat16)
-            slope[at, cols] = (back * (sig * (1.0 + pre * (1.0 - sig)))).astype(jnp.bfloat16)
-
+        pre = f32_dot(tok[at, :], weight[0]) * scale_in
+        back = f32_dot(grd[at, :], weight[1]) * scale_hid
+        sig = sigmoid(pre)
+        act[at, :] = (pre[:, cut:] * sig[:, cut:]).astype(jnp.bfloat16)
+        slope[at, :] = (back * (sig * (1.0 + pre * (1.0 - sig)))).astype(jnp.bfloat16)
     for copy in late:
         copy.wait()
-
-    @pl.loop(0, delta.shape[1] // tile_rows)
+    tile = 512
+
+    @pl.loop(0, delta.shape[1] // tile)
     def _(step):
-        at = pl.ds(pl.multiple_of(step * tile_rows, tile_rows), tile_rows)
+        at = pl.ds(pl.multiple_of(step * tile, tile), tile)
         grad_down = f32_dot(grd_t[at, :], act[...]) * scale_hid
-        delta[1, at, :] = (grad_down * rate).astype(jnp.bfloat16)
+        delta[0, at, :] = (grad_down * rate).astype(jnp.bfloat16)
         grad_up = f32_dot(tok_t[at, :], slope[...]) * scale_in
-        delta[0, at, :] = (grad_up * rate).astype(jnp.bfloat16)
-
-        @pl.loop(0, tile_rows // rows, unroll=8)
-        def _(inner):
-            block = step * (tile_rows // rows) + inner
-            pltpu.make_async_copy(
-                delta.at[:, pl.ds(pl.multiple_of(block * rows, rows), rows)],
-                out.at[owner[block]],
-                sems.at[1],
-            ).start()
+        up = (grad_up * rate).astype(jnp.bfloat16)
+        delta[1, at, :] = up[:, :cut]
+        delta[2, at, :] = up[:, cut:]
+        send_rows(owner, delta, out, step, tile, sems.at[1])
 
     wait_bytes(delta, sems.at[1])
 
 
-def path_delta(scales, owner, arrived, order, tokens, grads, tokens_t, grads_t):
-    _, halves, _, cols = arrived.shape
+def delta_rest(scales, cut, owner, arrived, earlier, tokens, grads, tokens_t, grads_t):
+    paths, halves, rows, cols = arrived.shape
     width, count = tokens_t.shape
     bf16 = jnp.bfloat16
     return pl.pallas_call(
-        functools.partial(delta_kernel, scales, (1024, 512)),
-        out_shape=jax.ShapeDtypeStruct(arrived.shape, bf16),
+        functools.partial(rest_kernel, scales),
+        out_shape=jax.ShapeDtypeStruct((paths, 3, rows, cut), bf16),
         in_specs=[SMEM] + [ANY] * 12,
         out_specs=ANY,
         scratch_shapes=[
@@ -145,31 +217,36 @@
             pltpu.VMEM((count, width), bf16),
             pltpu.VMEM((width, count), bf16),
             pltpu.VMEM((width, count), bf16),
+            pltpu.VMEM((count, cols - cut), bf16),
             pltpu.VMEM((count, cols), bf16),
-            pltpu.VMEM((count, cols), bf16),
-            pltpu.VMEM((halves, width, cols), bf16),
+            pltpu.VMEM((3, width, cut), bf16),
             pltpu.SemaphoreType.DMA((12,)),
         ],
         compiler_params=params(),
-        cost_estimate=cost(8 * count * width * cols, 8 * (count * width + width * cols)),
-        name="path_delta",
-    )(owner, arrived, order, tokens_t, grads_t, *tokens, *grads)
+        cost_estimate=cost(7 * count * width * cols, 8 * (count * width + width * cols)),
+        name="delta_rest",
+    )(owner, arrived, earlier, tokens_t, grads_t, *tokens, *grads)
 
 
 def outer_kernel(
-    module_of, order, received, master, momentum, new_state, sending,
+    module_of, order, received_first, received, master, momentum, new_state, sending,
     got, mas, mom, state, updated, share, first, sems,
 ):
     modules, halves, rows, cols = state.shape
     step = outer_rate * (1.0 + outer_decay)
+    cut = received.shape[3]
+    low, high = pl.ds(0, cut), pl.ds(cut, cols - cut)
     loads = []
     for half in range(halves):
-        sources = (received.at[:, half], master.at[:, half], momentum.at[:, half])
-        targets = (got.at[half], mas.at[half], mom.at[half])
+        pieces = ((received, 1, low), (received, 2, high))
+        if half == 1:
+            pieces = ((received_first, 0, low), (received, 0, high))
+        pairs = [(source.at[:, slab], got.at[half, :, :, at]) for source, slab, at in pieces]
+        pairs += [(master.at[:, half], mas.at[half]), (momentum.at[:, half], mom.at[half])]
         loads.append(
             [
-                pltpu.make_async_copy(source, target, sems.at[3 * half + i])
-                for i, (source, target) in enumerate(zip(sources, targets, strict=True))
+                pltpu.make_async_copy(source, target, sems.at[4 * half + i])
+                for i, (source, target) in enumerate(pairs)
             ]
         )
         for load in loads[half]:
@@ -209,30 +286,30 @@
             ).astype(jnp.bfloat16)
             if half == halves - 1:
                 pltpu.make_async_copy(
-                    state.at[module], new_state.at[module], sems.at[6]
+                    state.at[module], new_state.at[module], sems.at[8]
                 ).start()
 
                 @pl.loop(begin, end)
                 def _(i):
                     pltpu.make_async_copy(
-                        updated.at[module], sending.at[order[i]], sems.at[7]
+                        updated.at[module], sending.at[order[i]], sems.at[9]
                     ).start()
 
-    wait_bytes(sending, sems.at[7])
-    wait_bytes(state, sems.at[6])
-
-
-def outer(module_of, order, received, master, momentum):
-    paths, halves, rows, cols = received.shape
-    modules = master.shape[0]
+    wait_bytes(sending, sems.at[9])
+    wait_bytes(state, sems.at[8])
+
+
+def outer(module_of, order, received_first, received, master, momentum):
+    paths = received.shape[0]
+    modules, halves, rows, cols = master.shape
     f32, bf16 = jnp.float32, jnp.bfloat16
     return pl.pallas_call(
         outer_kernel,
         out_shape=(
             jax.ShapeDtypeStruct(momentum.shape, f32),
-            jax.ShapeDtypeStruct(received.shape, bf16),
+            jax.ShapeDtypeStruct((paths, halves, rows, cols), bf16),
         ),
-        in_specs=[SMEM, SMEM, ANY, ANY, ANY],
+        in_specs=[SMEM, SMEM, ANY, ANY, ANY, ANY],
         out_specs=(ANY, ANY),
         scratch_shapes=[
             pltpu.VMEM((halves, paths, rows, cols), bf16),
@@ -242,12 +319,12 @@
             pltpu.VMEM(master.shape, bf16),
             pltpu.VMEM((modules, 8, cols), f32),
             pltpu.SMEM((modules + 1,), jnp.int32),
-            pltpu.SemaphoreType.DMA((8,)),
+            pltpu.SemaphoreType.DMA((10,)),
         ],
         compiler_params=params(),
         cost_estimate=cost(2 * paths * rows * cols, 8 * paths * rows * cols),
         name="outer",
-    )(module_of, order, received, master, momentum)
+    )(module_of, order, received_first, received, master, momentum)
 
 
 def home_kernel(groups, owner, back, out, buf, place, sems):
@@ -330,10 +407,13 @@
         inner_rate / math.sqrt(rows * fsdp),
     )
     arrived = exchange(pick(module_of, master))
-    delta = path_delta(
-        scales, block_owner, arrived, order, tokens, grads, tokens_t, grads_t
+    cut = block_cols // 2
+    begun = delta_first(scales, cut, block_owner, arrived, order, tokens, grads_t)
+    rest = delta_rest(
+        scales, cut, block_owner, arrived, begun, tokens, grads, tokens_t, grads_t
     )
-    new_state, sending = outer(module_of, order, exchange(delta), master, momentum)
+    got_first, got = exchange(begun), exchange(rest)
+    new_state, sending = outer(module_of, order, got_first, got, master, momentum)
     own_module = bring_home(block_owner, exchange(sending))
     return (new_state, own_module.reshape(1, 2, model_width, block_cols))
 

time: 351 us -> 355 us (1.011)
  blocking collectives: 204 us -> 186 us
  waiting for transfers between devices: 64.7 us -> 76.8 us
  starting transfers between devices: 20.2 us -> 27 us
  Pallas kernels: 36.4 us -> 42.4 us
  other arithmetic: 12.3 us -> 8.56 us
    ppermute x1, waiting for transfers between devices: 0.01 us -> 19 us  [collect(): grd_right = lax.ppermute(grads, 'fsdp', left)]
    ppermute x1, waiting for transfers between devices: 18.8 us -> 0.01 us  [collect(): tok_left = lax.ppermute(tokens, 'fsdp', right)]
    all_to_all x2, blocking collectives: 204 us -> 186 us  [exchange(): lax.all_to_all(blocks, 'path', split_axis=0, concat_axis=0, tiled=True)]
    all_to_all x1 -> x2, waiting for transfers between devices: 22.1 us -> 31.4 us  [exchange(): lax.all_to_all(blocks, 'path', split_axis=0, concat_axis=0, tiled=True)]
    ppermute x1, waiting for transfers between devices: 6.76 us -> 15.8 us  [collect(): grd_left = lax.ppermute(grads, 'fsdp', right)]
    pallas_call x1 -> x2, Pallas kernels: 22.6 us -> 28.6 us  [the longest x1 20.2 us: delta_rest(): pl.pallas_call(functools.partial(rest_kernel, scales), out_shape=jax.Shap...]
    all_to_all x1 -> x2, starting transfers between devices: 13.5 us -> 19.3 us  [exchange(): lax.all_to_all(blocks, 'path', split_axis=0, concat_axis=0, tiled=True)]
    ppermute x1, waiting for transfers between devices: 14.5 us -> 9.58 us  [collect(): tok_right = lax.ppermute(tokens, 'fsdp', left)]
  transfers between devices with their start and end apart: 7 -> 8, of which waited for: 5 -> 5; matrix products, arithmetic and copies ran while one was open for 7% -> 6% of each run, Pallas kernels for 0% -> 6%
where the time goes in v7:
time: 355 us; the launch traced here: 354 us
  blocking collectives  186 us (52%)
  waiting for transfers between devices  76.8 us (22%)
  Pallas kernels  42.4 us (12%)
  starting transfers between devices  27 us (8%)
  local copies, waits for them, and re-layouts  12 us (3%)
  other arithmetic  8.56 us (2%)
    all_to_all x2, blocking collectives, exchange(): lax.all_to_all(blocks, 'path', split_axis=0, concat_axis=0, tiled=True)  186 us
    all_to_all x2, waiting for transfers between devices, exchange(): lax.all_to_all(blocks, 'path', split_axis=0, concat_axis=0, tiled=True)  31.4 us
    pallas_call x1, Pallas kernels, delta_rest(): pl.pallas_call(functools.partial(rest_kernel, scales), out_shape=jax.Shap...  20.2 us
    all_to_all x2, starting transfers between devices, exchange(): lax.all_to_all(blocks, 'path', split_axis=0, concat_axis=0, tiled=True)  19.3 us
    ppermute x1, waiting for transfers between devices, collect(): grd_right = lax.ppermute(grads, 'fsdp', left)  19 us
    ppermute x1, waiting for transfers between devices, collect(): grd_left = lax.ppermute(grads, 'fsdp', right)  15.8 us
    transpose x2, local copies, waits for them, and re-layouts, shards(): tokens_t, grads_t = (jnp.concatenate(tokens).T, jnp.concatenate(grads).T)  11.8 us
    ppermute x1, waiting for transfers between devices, collect(): tok_right = lax.ppermute(tokens, 'fsdp', left)  9.58 us
  transfers between devices with their start and end apart: 8, of which 5 were waited for; matrix products, arithmetic and copies ran while one was open for 6% of the time, Pallas kernels for 6%

profile of v7, /device:TPU:1, one launch (start us, length us, event | category | flops | bytes accessed | tf_op | source)
XLA Modules:
  0.0 354.1 jit_solution(13690416619543715440)
XLA Ops:
  0.6 3.2 pick.1
  3.9 13.5 %all-to-all-start = ((bf16[64,2,16,1024]{3,2,1,0:T(8,128)(2,1)}), bf16[64,2,16,1024]{3,2,1,0:T(8,128)(2,1)}, u32[]{:S(2)}, u32[]{:S(2)}) async-start(bf16[64,2,16,1024]{3,2,1,0:T(8,128)(2,1)} %pick.1), calls=%async_computation | async-start | bytes 8388608 | tf_op jit(solution)/shard_map/all_to_all | solution.py:390
  17.4 0.1 pad.7.refs_0_
  17.6 2.6 collective-permute-start.1
  20.1 0.2 collective-permute-start
  20.3 19.0 %collective-permute-done.1.refs_6_ = bf16[448,1024]{1,0:T(8,128)(2,1)S(1)} collective-permute-done((bf16[448,1024]{1,0:T(8,128)(2,1)S(1)}, bf16[448,1024]{1,0:T(8,128)(2,1)S(1)}, u32[]{:S(2)}, u32[]{:S(2)}) %collective-permute-start.1) | collective-permute-done | bytes 917536 | tf_op jit(solution)/shard_map/ppermute | solution.py:381
  39.3 3.5 collective-permute-start.2
  42.8 1.4 collective-permute-start.5
  44.3 2.0 sort.17
  46.3 15.8 %collective-permute-done.refs_5_ = bf16[448,1024]{1,0:T(8,128)(2,1)} collective-permute-done((bf16[448,1024]{1,0:T(8,128)(2,1)S(1)}, bf16[448,1024]{1,0:T(8,128)(2,1)}, u32[]{:S(2)}, u32[]{:S(2)}) %collective-permute-start) | collective-permute-done | bytes 917536 | tf_op jit(solution)/shard_map/ppermute | solution.py:382
  62.2 3.2 maximum_bitcast_fusion
  65.4 5.9 %copy.8.grads_t = bf16[1024,1792]{1,0:T(8,128)(2,1)} copy(bf16[1024,1792]{0,1:T(8,128)(2,1)} %maximum_bitcast_fusion) | data formatting | bytes 7340032 | tf_op jit(solution)/shard_map/transpose | solution.py:403
  71.3 9.6 %collective-permute-done.4.refs_2_ = bf16[448,1024]{1,0:T(8,128)(2,1)} collective-permute-done((bf16[448,1024]{1,0:T(8,128)(2,1)S(1)}, bf16[448,1024]{1,0:T(8,128)(2,1)}, u32[]{:S(2)}, u32[]{:S(2)}) %collective-permute-start.4) | collective-permute-done | bytes 917536 | tf_op jit(solution)/shard_map/ppermute | solution.py:383
  80.8 1.0 collective-permute-done.5.refs_3_
  81.8 31.4 %all-to-all-done.arrived = bf16[64,2,16,1024]{3,2,1,0:T(8,128)(2,1)} async-done(((bf16[64,2,16,1024]{3,2,1,0:T(8,128)(2,1)}), bf16[64,2,16,1024]{3,2,1,0:T(8,128)(2,1)}, u32[]{:S(2)}, u32[]{:S(2)}) %all-to-all-start) | async-done | bytes 4194336 | tf_op jit(solution)/shard_map/all_to_all | solution.py:390
  113.3 8.5 %delta_first.1.earlier = bf16[64,1,16,512]{3,2,1,0:T(8,128)(2,1)} custom-call(s32[64]{0:T(128)} %owner.5, bf16[64,2,16,1024]{3,2,1,0:T(8,128)(2,1)} %all-to-all-done.arrived, s32[64]{0:T(128)} %get-tuple-element.7.order, bf16[1024,1792]{1,0:T(8,128)(2,1)} %copy.8.grads_t, bf16[448,1024]{1,0:T(8,128)(2,1)} %copy-done.1, ...), custom_call_target="tpu_custom_call" | custom-call | flops 3758096384 | bytes 9437184 | tf_op jit(solution)/shard_map/delta_first/pallas_call | solution.py:137
  121.7 5.8 %all-to-all-start.1 = ((bf16[64,1,16,512]{3,2,1,0:T(8,128)(2,1)}), bf16[64,1,16,512]{3,2,1,0:T(8,128)(2,1)S(1)}, u32[]{:S(2)}, u32[]{:S(2)}) async-start(bf16[64,1,16,512]{3,2,1,0:T(8,128)(2,1)} %delta_first.1.earlier), calls=%async_computation.1 | async-start | bytes 2097152 | tf_op jit(solution)/shard_map/all_to_all | solution.py:390
  127.5 3.3 maximum_bitcast_fusion.1
  130.8 5.9 %copy.9.tokens_t = bf16[1024,1792]{1,0:T(8,128)(2,1)} copy(bf16[1024,1792]{0,1:T(8,128)(2,1)} %maximum_bitcast_fusion.1) | data formatting | bytes 7340032 | tf_op jit(solution)/shard_map/transpose | solution.py:403
  136.7 20.2 %delta_rest.1 = bf16[64,3,16,512]{3,2,1,0:T(8,128)(2,1)} custom-call(s32[64]{0:T(128)} %owner.5, bf16[64,2,16,1024]{3,2,1,0:T(8,128)(2,1)} %all-to-all-done.arrived, bf16[64,1,16,512]{3,2,1,0:T(8,128)(2,1)} %delta_first.1.earlier, bf16[1024,1792]{1,0:T(8,128)(2,1)} %copy.9.tokens_t, bf16[1024,1792]{1,0:T(8,128)(2,1)} %copy.8.grads_t, ...), custom_call_target="tpu_custom_call" | custom-call | flops 13153337344 | bytes 23068672 | tf_op jit(solution)/shard_map/delta_rest/pallas_call | solution.py:209
  156.9 83.9 %all_to_all.20.received = bf16[64,3,16,512]{3,2,1,0:T(8,128)(2,1)} all-to-all(bf16[64,3,16,512]{3,2,1,0:T(8,128)(2,1)} %delta_rest.1), channel_id=1, replica_groups=mesh['path'=64,'fsdp'=4] {'path'}, dimensions={0} | all-to-all | bytes 6291456 | tf_op jit(solution)/shard_map/all_to_all | solution.py:390
  240.9 6.7 %outer.1 = (f32[16,2,16,1024]{3,2,1,0:T(8,128)}, bf16[64,2,16,1024]{3,2,1,0:T(8,128)(2,1)}) custom-call(s32[64]{0:T(128)} %bitcast.8, s32[64]{0:T(128)} %get-tuple-element.7.order, bf16[64,1,16,512]{3,2,1,0:T(8,128)(2,1)} %copy-done, bf16[64,3,16,512]{3,2,1,0:T(8,128)(2,1)} %all_to_all.20.received, bf16[16,2,16,1024]{3,2,1,0:T(8,128)(2,1)} %master.1, ...), custom_call_target="tpu_custom_call" | custom-call | flops 2097152 | bytes 8388608 | tf_op jit(solution)/shard_map/outer/pallas_call | solution.py:306
  247.6 102.5 %all_to_all.21.back = bf16[64,2,16,1024]{3,2,1,0:T(8,128)(2,1)} all-to-all(bf16[64,2,16,1024]{3,2,1,0:T(8,128)(2,1)} %get-tuple-element.11), channel_id=1, replica_groups=mesh['path'=64,'fsdp'=4] {'path'}, dimensions={0} | all-to-all | bytes 8388608 | tf_op jit(solution)/shard_map/all_to_all | solution.py:390
  350.1 3.9 %bring_home.1 = bf16[2,64,16,1024]{3,2,1,0:T(8,128)(2,1)} custom-call(s32[64]{0:T(128)} %owner.5, bf16[64,2,16,1024]{3,2,1,0:T(8,128)(2,1)} %all_to_all.21.back), custom_call_target="tpu_custom_call" | custom-call | bytes 8388608 | tf_op jit(solution)/shard_map/bring_home/pallas_call | solution.py:360
  (23 shorter events, 0.1 us)
Async XLA Ops:
  3.8 13.5 %copy-start.5 = (bf16[440,1024]{1,0:T(8,128)(2,1)S(1)}, bf16[440,1024]{1,0:T(8,128)(2,1)}, u32[]{:S(2)}) copy-start(bf16[440,1024]{1,0:T(8,128)(2,1)} %param.6) | copy-start | bytes 2703364
  3.9 13.6 %copy-start.6 = (bf16[440,1024]{1,0:T(8,128)(2,1)S(1)}, bf16[440,1024]{1,0:T(8,128)(2,1)}, u32[]{:S(2)}) copy-start(bf16[440,1024]{1,0:T(8,128)(2,1)} %param.7) | copy-start | bytes 2703364
  3.9 40.4 %copy-start.7 = (s32[64,1]{0,1:T(1,128)S(1)}, s32[64,1]{0,1:T(1,128)}, u32[]{:S(2)}) copy-start(s32[64,1]{0,1:T(1,128)} %param.10) | copy-start | bytes 772
  3.9 109.4 %all-to-all-start = ((bf16[64,2,16,1024]{3,2,1,0:T(8,128)(2,1)}), bf16[64,2,16,1024]{3,2,1,0:T(8,128)(2,1)}, u32[]{:S(2)}, u32[]{:S(2)}) async-start(bf16[64,2,16,1024]{3,2,1,0:T(8,128)(2,1)} %pick.1), calls=%async_computation | async-start | bytes 8388608 | tf_op jit(solution)/shard_map/all_to_all | solution.py:390
  17.5 47.9 %copy-start.1 = (bf16[448,1024]{1,0:T(8,128)(2,1)}, bf16[448,1024]{1,0:T(8,128)(2,1)S(1)}, u32[]{:S(2)}) copy-start(bf16[448,1024]{1,0:T(8,128)(2,1)S(1)} %pad.7.refs_0_) | copy-start | bytes 2752516
  17.5 53.7 %copy-start.3 = (bf16[448,1024]{1,0:T(8,128)(2,1)}, bf16[448,1024]{1,0:T(8,128)(2,1)S(1)}, u32[]{:S(2)}) copy-start(bf16[448,1024]{1,0:T(8,128)(2,1)S(1)} %pad.8.refs_4_) | copy-start | bytes 2752516
  17.6 21.7 %collective-permute-start.1 = (bf16[448,1024]{1,0:T(8,128)(2,1)S(1)}, bf16[448,1024]{1,0:T(8,128)(2,1)S(1)}, u32[]{:S(2)}, u32[]{:S(2)}) collective-permute-start(bf16[448,1024]{1,0:T(8,128)(2,1)S(1)} %pad.8.refs_4_), channel_id=1, source_target_pairs={{0,3},{1,0},{2,1},{3,2},{4,7},{5,4},{6,5},{7,6},{8,11},{9,8},{10,9... | collective-permute-start | bytes 2752520 | tf_op jit(solution)/shard_map/ppermute | solution.py:381
  20.1 22.7 %collective-permute-start.3 = (bf16[448,1024]{1,0:T(8,128)(2,1)S(1)}, bf16[448,1024]{1,0:T(8,128)(2,1)}, u32[]{:S(2)}, u32[]{:S(2)}) collective-permute-start(bf16[448,1024]{1,0:T(8,128)(2,1)S(1)} %pad.7.refs_0_), channel_id=1, source_target_pairs={{0,1},{1,2},{2,3},{3,0},{4,5},{5,6},{6,7},{7,4},{8,9},{9,10},{10,1... | collective-permute-start | bytes 2752520 | tf_op jit(solution)/shard_map/ppermute | solution.py:380
  20.1 42.0 %collective-permute-start = (bf16[448,1024]{1,0:T(8,128)(2,1)S(1)}, bf16[448,1024]{1,0:T(8,128)(2,1)}, u32[]{:S(2)}, u32[]{:S(2)}) collective-permute-start(bf16[448,1024]{1,0:T(8,128)(2,1)S(1)} %pad.8.refs_4_), channel_id=1, source_target_pairs={{0,1},{1,2},{2,3},{3,0},{4,5},{5,6},{6,7},{7,4},{8,9},{9,10},{10,1... | collective-permute-start | bytes 2752520 | tf_op jit(solution)/shard_map/ppermute | solution.py:382
  39.3 32.0 %copy-start.4 = (bf16[448,1024]{1,0:T(8,128)(2,1)}, bf16[448,1024]{1,0:T(8,128)(2,1)S(1)}, u32[]{:S(2)}) copy-start(bf16[448,1024]{1,0:T(8,128)(2,1)S(1)} %collective-permute-done.1.refs_6_) | copy-start | bytes 2752516
  39.3 22.9 %collective-permute-start.2 = (bf16[448,1024]{1,0:T(8,128)(2,1)S(1)}, bf16[448,1024]{1,0:T(8,128)(2,1)}, u32[]{:S(2)}, u32[]{:S(2)}) collective-permute-start(bf16[448,1024]{1,0:T(8,128)(2,1)S(1)} %collective-permute-done.1.refs_6_), channel_id=1, source_target_pairs={{0,3},{1,0},{2,1},{3,2},{4,7},{5,4},{6,5},{7,6},{8,11},{9,8},{10,9... | collective-permute-start | bytes 2752520 | tf_op jit(solution)/shard_map/ppermute | solution.py:384
  42.8 38.0 %collective-permute-start.4 = (bf16[448,1024]{1,0:T(8,128)(2,1)S(1)}, bf16[448,1024]{1,0:T(8,128)(2,1)}, u32[]{:S(2)}, u32[]{:S(2)}) collective-permute-start(bf16[448,1024]{1,0:T(8,128)(2,1)S(1)} %pad.7.refs_0_), channel_id=1, source_target_pairs={{0,3},{1,0},{2,1},{3,2},{4,7},{5,4},{6,5},{7,6},{8,11},{9,8},{10,9... | collective-permute-start | bytes 2752520 | tf_op jit(solution)/shard_map/ppermute | solution.py:383
  42.8 39.0 %collective-permute-start.5 = (bf16[448,1024]{1,0:T(8,128)(2,1)}, bf16[448,1024]{1,0:T(8,128)(2,1)}, u32[]{:S(2)}, u32[]{:S(2)}) collective-permute-start(bf16[448,1024]{1,0:T(8,128)(2,1)} %collective-permute-done.3.refs_1_), channel_id=1, source_target_pairs={{0,1},{1,2},{2,3},{3,0},{4,5},{5,6},{6,7},{7,4},{8,9},{9,10},{10,1... | collective-permute-start | bytes 2752520 | tf_op jit(solution)/shard_map/ppermute | solution.py:385
  113.3 14.3 %copy-start.2 = (bf16[448,1024]{1,0:T(8,128)(2,1)S(1)}, bf16[448,1024]{1,0:T(8,128)(2,1)}, u32[]{:S(2)}) copy-start(bf16[448,1024]{1,0:T(8,128)(2,1)} %copy-done.1) | copy-start | bytes 2752516
  121.7 35.2 %all-to-all-start.1 = ((bf16[64,1,16,512]{3,2,1,0:T(8,128)(2,1)}), bf16[64,1,16,512]{3,2,1,0:T(8,128)(2,1)S(1)}, u32[]{:S(2)}, u32[]{:S(2)}) async-start(bf16[64,1,16,512]{3,2,1,0:T(8,128)(2,1)} %delta_first.1.earlier), calls=%async_computation.1 | async-start | bytes 2097152 | tf_op jit(solution)/shard_map/all_to_all | solution.py:390
  156.9 84.0 %copy-start = (bf16[64,1,16,512]{3,2,1,0:T(8,128)(2,1)}, bf16[64,1,16,512]{3,2,1,0:T(8,128)(2,1)S(1)}, u32[]{:S(2)}) copy-start(bf16[64,1,16,512]{3,2,1,0:T(8,128)(2,1)S(1)} %all-to-all-done.1.received_first) | copy-start | bytes 3145732

commit v8 on v6

--- a/solution.py
+++ b/solution.py
@@ -61,7 +61,7 @@
     return 1.0 / (1.0 + jnp.exp(-values))
 
 
-def delta_kernel(scales, tiles, owner, arrived, order, tokens_t, grads_t, *refs):
+def delta_kernel(scales, tiles, owner, arrived, order, base, tokens_t, grads_t, *refs):
     scale_in, scale_hid, rate = scales
     tile_cols, tile_rows = tiles
     tok_in, grd_in = refs[:4], refs[4:8]
@@ -130,14 +130,14 @@
     wait_bytes(delta, sems.at[1])
 
 
-def path_delta(scales, owner, arrived, order, tokens, grads, tokens_t, grads_t):
+def path_delta(scales, owner, arrived, order, base, tokens, grads, tokens_t, grads_t):
     _, halves, _, cols = arrived.shape
     width, count = tokens_t.shape
     bf16 = jnp.bfloat16
     return pl.pallas_call(
         functools.partial(delta_kernel, scales, (1024, 512)),
         out_shape=jax.ShapeDtypeStruct(arrived.shape, bf16),
-        in_specs=[SMEM] + [ANY] * 12,
+        in_specs=[SMEM] + [ANY] * 13,
         out_specs=ANY,
         scratch_shapes=[
             pltpu.VMEM((halves, width, cols), bf16),
@@ -153,28 +153,11 @@
         compiler_params=params(),
         cost_estimate=cost(8 * count * width * cols, 8 * (count * width + width * cols)),
         name="path_delta",
-    )(owner, arrived, order, tokens_t, grads_t, *tokens, *grads)
-
-
-def outer_kernel(
-    module_of, order, received, master, momentum, new_state, sending,
-    got, mas, mom, state, updated, share, first, sems,
-):
-    modules, halves, rows, cols = state.shape
-    step = outer_rate * (1.0 + outer_decay)
-    loads = []
-    for half in range(halves):
-        sources = (received.at[:, half], master.at[:, half], momentum.at[:, half])
-        targets = (got.at[half], mas.at[half], mom.at[half])
-        loads.append(
-            [
-                pltpu.make_async_copy(source, target, sems.at[3 * half + i])
-                for i, (source, target) in enumerate(zip(sources, targets, strict=True))
-            ]
-        )
-        for load in loads[half]:
-            load.start()
-
+    )(owner, arrived, order, base, tokens_t, grads_t, *tokens, *grads)
+
+
+def begin_of(module_of, first, share):
+    modules = share.shape[0]
     for module in range(modules + 1):
         first[module] = 0
 
@@ -187,67 +170,122 @@
         share[module] = 1.0 / count.astype(jnp.float32)
         first[module + 1] += first[module]
 
+
+def load_halves(sources, targets, sems):
+    loads = []
+    for half in range(2):
+        loads.append([])
+        for source, target in zip(sources, targets, strict=True):
+            sem = sems.at[half * len(sources) + len(loads[half])]
+            loads[half].append(pltpu.make_async_copy(source.at[:, half], target.at[half], sem))
+            loads[half][-1].start()
+    return loads
+
+
+def average_of(half, module, order, got, first, share):
+    rows, cols = got.shape[2:]
+    total = lax.fori_loop(
+        first[module],
+        first[module + 1],
+        lambda i, acc: acc + got[half, order[i]].astype(jnp.float32),
+        jnp.zeros((rows, cols), jnp.float32),
+    )
+    return (total.reshape(-1, 8, cols) * share[module]).reshape(rows, cols)
+
+
+def update_kernel(
+    module_of, order, received, base_in, sending, first, got, base, updated, share, sems
+):
+    modules, halves = updated.shape[:2]
+    step = outer_rate * (1.0 + outer_decay)
+    loads = load_halves((received, base_in), (got, base), sems)
+    begin_of(module_of, first, share)
     for half in range(halves):
         for load in loads[half]:
             load.wait()
 
         @pl.loop(0, modules)
         def _(module):
-            begin, end = first[module], first[module + 1]
-            total = lax.fori_loop(
-                begin,
-                end,
-                lambda i, acc: acc + got[half, order[i]].astype(jnp.float32),
-                jnp.zeros((rows, cols), jnp.float32),
-            )
-            averaged = (total.reshape(-1, 8, cols) * share[module]).reshape(rows, cols)
-            kept = outer_decay * mom[half, module]
-            state[module, half] = kept + averaged
-            weights = mas[half, module].astype(jnp.float32)
-            updated[module, half] = (
-                weights - (outer_rate * outer_decay) * kept - step * averaged
-            ).astype(jnp.bfloat16)
+            averaged = average_of(half, module, order, got, first, share)
+            updated[module, half] = (base[half, module] - step * averaged).astype(jnp.bfloat16)
             if half == halves - 1:
-                pltpu.make_async_copy(
-                    state.at[module], new_state.at[module], sems.at[6]
-                ).start()
-
-                @pl.loop(begin, end)
+
+                @pl.loop(first[module], first[module + 1])
                 def _(i):
                     pltpu.make_async_copy(
-                        updated.at[module], sending.at[order[i]], sems.at[7]
+                        updated.at[module], sending.at[order[i]], sems.at[4]
                     ).start()
 
-    wait_bytes(sending, sems.at[7])
-    wait_bytes(state, sems.at[6])
-
-
-def outer(module_of, order, received, master, momentum):
+    wait_bytes(sending, sems.at[4])
+
+
+def update(module_of, order, received, base):
     paths, halves, rows, cols = received.shape
-    modules = master.shape[0]
+    modules = base.shape[0]
     f32, bf16 = jnp.float32, jnp.bfloat16
     return pl.pallas_call(
-        outer_kernel,
+        update_kernel,
         out_shape=(
-            jax.ShapeDtypeStruct(momentum.shape, f32),
             jax.ShapeDtypeStruct(received.shape, bf16),
+            jax.ShapeDtypeStruct((modules + 1,), jnp.int32),
         ),
-        in_specs=[SMEM, SMEM, ANY, ANY, ANY],
-        out_specs=(ANY, ANY),
+        in_specs=[SMEM, SMEM, ANY, ANY],
+        out_specs=(ANY, SMEM),
         scratch_shapes=[
             pltpu.VMEM((halves, paths, rows, cols), bf16),
-            pltpu.VMEM((halves, modules, rows, cols), bf16),
+            pltpu.VMEM((halves, modules, rows, cols), f32),
+            pltpu.VMEM(base.shape, bf16),
+            pltpu.VMEM((modules, 8, cols), f32),
+            pltpu.SemaphoreType.DMA((5,)),
+        ],
+        compiler_params=params(),
+        cost_estimate=cost(2 * paths * rows * cols, 8 * paths * rows * cols),
+        name="update",
+    )(module_of, order, received, base)
+
+
+def state_kernel(
+    first, order, received, momentum, new_state, got, mom, state, share, sems
+):
+    modules, halves = state.shape[:2]
+    loads = load_halves((received, momentum), (got, mom), sems)
+    for module in range(modules):
+        count = jnp.full(share.shape[1:], first[module + 1] - first[module], jnp.int32)
+        share[module] = 1.0 / count.astype(jnp.float32)
+    for half in range(halves):
+        for load in loads[half]:
+            load.wait()
+
+        @pl.loop(0, modules)
+        def _(module):
+            averaged = average_of(half, module, order, got, first, share)
+            state[module, half] = outer_decay * mom[half, module] + averaged
+
+    store = pltpu.make_async_copy(state, new_state, sems.at[4])
+    store.start()
+    store.wait()
+
+
+def next_state(first, order, received, momentum):
+    paths, halves, rows, cols = received.shape
+    modules = momentum.shape[0]
+    f32, bf16 = jnp.float32, jnp.bfloat16
+    return pl.pallas_call(
+        state_kernel,
+        out_shape=jax.ShapeDtypeStruct(momentum.shape, f32),
+        in_specs=[SMEM, SMEM, ANY, ANY],
+        out_specs=ANY,
+        scratch_shapes=[
+            pltpu.VMEM((halves, paths, rows, cols), bf16),
             pltpu.VMEM((halves, modules, rows, cols), f32),
             pltpu.VMEM(momentum.shape, f32),
-            pltpu.VMEM(master.shape, bf16),
             pltpu.VMEM((modules, 8, cols), f32),
-            pltpu.SMEM((modules + 1,), jnp.int32),
-            pltpu.SemaphoreType.DMA((8,)),
+            pltpu.SemaphoreType.DMA((5,)),
         ],
         compiler_params=params(),
         cost_estimate=cost(2 * paths * rows * cols, 8 * paths * rows * cols),
-        name="outer",
-    )(module_of, order, received, master, momentum)
+        name="next_state",
+    )(first, order, received, momentum)
 
 
 def home_kernel(groups, owner, back, out, buf, place, sems):
@@ -330,10 +368,13 @@
         inner_rate / math.sqrt(rows * fsdp),
     )
     arrived = exchange(pick(module_of, master))
+    base = master.astype(jnp.float32) - (outer_rate * outer_decay * outer_decay) * momentum
     delta = path_delta(
-        scales, block_owner, arrived, order, tokens, grads, tokens_t, grads_t
-    )
-    new_state, sending = outer(module_of, order, exchange(delta), master, momentum)
+        scales, block_owner, arrived, order, base, tokens, grads, tokens_t, grads_t
+    )
+    received = exchange(delta)
+    sending, first = update(module_of, order, received, base)
+    new_state = next_state(first, order, received, momentum)
     own_module = bring_home(block_owner, exchange(sending))
     return (new_state, own_module.reshape(1, 2, model_width, block_cols))
 

time: 351 us -> 351 us (level)
  blocking collectives: 204 us -> 102 us
  waiting for transfers between devices: 64.7 us -> 151 us
  starting transfers between devices: 20.2 us -> 26.9 us
  Pallas kernels: 36.4 us -> 41.6 us
  local copies, waits for them, and re-layouts: 12.1 us -> 16.3 us
    all_to_all x2 -> x1, blocking collectives: 204 us -> 102 us  [exchange(): lax.all_to_all(blocks, 'path', split_axis=0, concat_axis=0, tiled=True)]
    all_to_all x1 -> x2, waiting for transfers between devices: 22.1 us -> 108 us  [exchange(): lax.all_to_all(blocks, 'path', split_axis=0, concat_axis=0, tiled=True)]
    ppermute x1, waiting for transfers between devices: 0.01 us -> 19.3 us  [collect(): grd_right = lax.ppermute(grads, 'fsdp', left)]
    ppermute x1, waiting for transfers between devices: 18.8 us -> 0.01 us  [collect(): tok_left = lax.ppermute(tokens, 'fsdp', right)]
    ppermute x1, waiting for transfers between devices: 6.76 us -> 14.1 us  [collect(): grd_left = lax.ppermute(grads, 'fsdp', right)]
    all_to_all x1 -> x2, starting transfers between devices: 13.5 us -> 19.4 us  [exchange(): lax.all_to_all(blocks, 'path', split_axis=0, concat_axis=0, tiled=True)]
    pallas_call x1 -> x2, Pallas kernels: 6.63 us -> 12.1 us  [the longest x1 6.23 us: update(): pl.pallas_call(update_kernel, out_shape=(jax.ShapeDtypeStruct(received.sh...]
    ppermute x1, waiting for transfers between devices: 14.5 us -> 9.55 us  [collect(): tok_right = lax.ppermute(tokens, 'fsdp', left)]
  transfers between devices with their start and end apart: 7 -> 8, of which waited for: 5 -> 6; matrix products, arithmetic and copies ran while one was open for 7% -> 8% of each run, Pallas kernels for 0% -> 2%
where the time goes in v8:
time: 351 us; the launch traced here: 350 us
  waiting for transfers between devices  151 us (43%)
  blocking collectives  102 us (29%)
  Pallas kernels  41.6 us (12%)
  starting transfers between devices  26.9 us (8%)
  local copies, waits for them, and re-layouts  16.3 us (5%)
  other arithmetic  10.7 us (3%)
    all_to_all x2, waiting for transfers between devices, exchange(): lax.all_to_all(blocks, 'path', split_axis=0, concat_axis=0, tiled=True)  108 us
    all_to_all x1, blocking collectives, exchange(): lax.all_to_all(blocks, 'path', split_axis=0, concat_axis=0, tiled=True)  102 us
    pallas_call x1, Pallas kernels, path_delta(): pl.pallas_call(functools.partial(delta_kernel, scales, (1024, 512)), out_...  22.4 us
    all_to_all x2, starting transfers between devices, exchange(): lax.all_to_all(blocks, 'path', split_axis=0, concat_axis=0, tiled=True)  19.4 us
    ppermute x1, waiting for transfers between devices, collect(): grd_right = lax.ppermute(grads, 'fsdp', left)  19.3 us
    ppermute x1, waiting for transfers between devices, collect(): grd_left = lax.ppermute(grads, 'fsdp', right)  14.1 us
    transpose x2, local copies, waits for them, and re-layouts, shards(): tokens_t, grads_t = (jnp.concatenate(tokens).T, jnp.concatenate(grads).T)  11.7 us
    ppermute x1, waiting for transfers between devices, collect(): tok_right = lax.ppermute(tokens, 'fsdp', left)  9.55 us
  transfers between devices with their start and end apart: 8, of which 6 were waited for; matrix products, arithmetic and copies ran while one was open for 8% of the time, Pallas kernels for 2%

profile of v8, /device:TPU:1, one launch (start us, length us, event | category | flops | bytes accessed | tf_op | source)
XLA Modules:
  0.0 349.8 jit_solution(14365769991461984283)
XLA Ops:
  0.6 3.2 pick.1
  3.9 13.4 %all-to-all-start = ((bf16[64,2,16,1024]{3,2,1,0:T(8,128)(2,1)}), bf16[64,2,16,1024]{3,2,1,0:T(8,128)(2,1)}, u32[]{:S(2)}, u32[]{:S(2)}) async-start(bf16[64,2,16,1024]{3,2,1,0:T(8,128)(2,1)} %pick.1), calls=%async_computation | async-start | bytes 8388608 | tf_op jit(solution)/shard_map/all_to_all | solution.py:351
  17.2 2.3 pad.7.refs_0_
  19.6 2.2 pad.8.refs_4_
  21.8 2.5 collective-permute-start.4
  24.5 19.3 %collective-permute-done.4.refs_6_ = bf16[448,1024]{1,0:T(8,128)(2,1)} collective-permute-done((bf16[448,1024]{1,0:T(8,128)(2,1)}, bf16[448,1024]{1,0:T(8,128)(2,1)}, u32[]{:S(2)}, u32[]{:S(2)}) %collective-permute-start.4) | collective-permute-done | bytes 917536 | tf_op jit(solution)/shard_map/ppermute | solution.py:342
  43.8 3.4 collective-permute-start.5
  47.2 1.4 collective-permute-start.2
  48.6 2.1 sort.17
  50.8 1.6 multiply_subtract_fusion.base.base_in
  52.4 14.1 %collective-permute-done.3.refs_5_ = bf16[448,1024]{1,0:T(8,128)(2,1)} collective-permute-done((bf16[448,1024]{1,0:T(8,128)(2,1)}, bf16[448,1024]{1,0:T(8,128)(2,1)}, u32[]{:S(2)}, u32[]{:S(2)}) %collective-permute-start.3) | collective-permute-done | bytes 917536 | tf_op jit(solution)/shard_map/ppermute | solution.py:343
  66.5 3.5 maximum_bitcast_fusion.1
  70.0 5.9 %copy.9.grads_t = bf16[1024,1792]{1,0:T(8,128)(2,1)} copy(bf16[1024,1792]{0,1:T(8,128)(2,1)} %maximum_bitcast_fusion.1) | data formatting | bytes 7340032 | tf_op jit(solution)/shard_map/transpose | solution.py:364
  75.9 9.6 %collective-permute-done.1.refs_2_ = bf16[448,1024]{1,0:T(8,128)(2,1)} collective-permute-done((bf16[448,1024]{1,0:T(8,128)(2,1)}, bf16[448,1024]{1,0:T(8,128)(2,1)}, u32[]{:S(2)}, u32[]{:S(2)}) %collective-permute-start.1) | collective-permute-done | bytes 917536 | tf_op jit(solution)/shard_map/ppermute | solution.py:344
  86.2 3.4 maximum_bitcast_fusion
  89.6 5.9 %copy.8.tokens_t = bf16[1024,1792]{1,0:T(8,128)(2,1)} copy(bf16[1024,1792]{0,1:T(8,128)(2,1)} %maximum_bitcast_fusion) | data formatting | bytes 7340032 | tf_op jit(solution)/shard_map/transpose | solution.py:364
  95.5 17.6 %all-to-all-done.arrived = bf16[64,2,16,1024]{3,2,1,0:T(8,128)(2,1)} async-done(((bf16[64,2,16,1024]{3,2,1,0:T(8,128)(2,1)}), bf16[64,2,16,1024]{3,2,1,0:T(8,128)(2,1)}, u32[]{:S(2)}, u32[]{:S(2)}) %all-to-all-start) | async-done | bytes 4194336 | tf_op jit(solution)/shard_map/all_to_all | solution.py:351
  113.1 22.4 %path_delta.1 = bf16[64,2,16,1024]{3,2,1,0:T(8,128)(2,1)} custom-call(s32[64]{0:T(128)} %owner.3, bf16[64,2,16,1024]{3,2,1,0:T(8,128)(2,1)} %all-to-all-done.arrived, s32[64]{0:T(128)} %get-tuple-element.7.order, f32[16,2,16,1024]{3,2,1,0:T(8,128)} %multiply_subtract_fusion.base.base_in, bf16[1024,1792]{1,0:T(8,128)(2,1)} %copy.8.tokens_t, ...), custom_call_target="tpu_custom_call" | custom-call | flops 15032385536 | bytes 23068672 | tf_op jit(solution)/shard_map/path_delta/pallas_call | solution.py:137
  135.5 102.1 %all_to_all.15.received = bf16[64,2,16,1024]{3,2,1,0:T(8,128)(2,1)} all-to-all(bf16[64,2,16,1024]{3,2,1,0:T(8,128)(2,1)} %path_delta.1), channel_id=1, replica_groups=mesh['path'=64,'fsdp'=4] {'path'}, dimensions={0} | all-to-all | bytes 8388608 | tf_op jit(solution)/shard_map/all_to_all | solution.py:351
  237.6 6.2 %update.1 = (bf16[64,2,16,1024]{3,2,1,0:T(8,128)(2,1)}, s32[17]{0:T(128)}) custom-call(s32[64]{0:T(128)} %bitcast.8, s32[64]{0:T(128)} %get-tuple-element.7.order, bf16[64,2,16,1024]{3,2,1,0:T(8,128)(2,1)} %all_to_all.15.received, f32[16,2,16,1024]{3,2,1,0:T(8,128)} %multiply_subtract_fusion.base.base_in), custom_call_target="tpu_custom_call" | custom-call | flops 2097152 | bytes 8388608 | tf_op jit(solution)/shard_map/update/pallas_call | solution.py:226
  243.8 6.0 %all-to-all-start.2 = ((bf16[64,2,16,1024]{3,2,1,0:T(8,128)(2,1)}), bf16[64,2,16,1024]{3,2,1,0:T(8,128)(2,1)}, u32[]{:S(2)}, u32[]{:S(2)}) async-start(bf16[64,2,16,1024]{3,2,1,0:T(8,128)(2,1)} %get-tuple-element.11), calls=%async_computation.2 | async-start | bytes 8388608 | tf_op jit(solution)/shard_map/all_to_all | solution.py:351
  249.9 5.9 %next_state.1 = f32[16,2,16,1024]{3,2,1,0:T(8,128)} custom-call(s32[17]{0:T(128)} %get-tuple-element.10.first, s32[64]{0:T(128)} %get-tuple-element.7.order, bf16[64,2,16,1024]{3,2,1,0:T(8,128)(2,1)} %all_to_all.15.received, f32[16,2,16,1024]{3,2,1,0:T(8,128)} %momentum.1), custom_call_target="tpu_custom_call" | custom-call | flops 2097152 | bytes 8388608 | tf_op jit(solution)/shard_map/next_state/pallas_call | solution.py:273
  255.8 90.0 %all-to-all-done.2.back = bf16[64,2,16,1024]{3,2,1,0:T(8,128)(2,1)} async-done(((bf16[64,2,16,1024]{3,2,1,0:T(8,128)(2,1)}), bf16[64,2,16,1024]{3,2,1,0:T(8,128)(2,1)}, u32[]{:S(2)}, u32[]{:S(2)}) %all-to-all-start.2) | async-done | bytes 4194336 | tf_op jit(solution)/shard_map/all_to_all | solution.py:351
  345.7 3.9 %bring_home.1 = bf16[2,64,16,1024]{3,2,1,0:T(8,128)(2,1)} custom-call(s32[64]{0:T(128)} %owner.3, bf16[64,2,16,1024]{3,2,1,0:T(8,128)(2,1)} %all-to-all-done.2.back), custom_call_target="tpu_custom_call" | custom-call | bytes 8388608 | tf_op jit(solution)/shard_map/bring_home/pallas_call | solution.py:321
  (13 shorter events, 1.0 us)
Async XLA Ops:
  3.8 44.8 %copy-start.2 = (s32[64,1]{0,1:T(1,128)S(1)}, s32[64,1]{0,1:T(1,128)}, u32[]{:S(2)}) copy-start(s32[64,1]{0,1:T(1,128)} %param.10) | copy-start | bytes 772
  3.9 109.2 %all-to-all-start = ((bf16[64,2,16,1024]{3,2,1,0:T(8,128)(2,1)}), bf16[64,2,16,1024]{3,2,1,0:T(8,128)(2,1)}, u32[]{:S(2)}, u32[]{:S(2)}) async-start(bf16[64,2,16,1024]{3,2,1,0:T(8,128)(2,1)} %pick.1), calls=%async_computation | async-start | bytes 8388608 | tf_op jit(solution)/shard_map/all_to_all | solution.py:351
  17.2 33.5 %copy-start = (f32[16,2,16,1024]{3,2,1,0:T(8,128)S(1)}, f32[16,2,16,1024]{3,2,1,0:T(8,128)}, u32[]{:S(2)}) copy-start(f32[16,2,16,1024]{3,2,1,0:T(8,128)} %momentum.1) | copy-start | bytes 6291460
  17.2 33.5 %copy-start.1 = (bf16[16,2,16,1024]{3,2,1,0:T(8,128)(2,1)S(1)}, bf16[16,2,16,1024]{3,2,1,0:T(8,128)(2,1)}, u32[]{:S(2)}) copy-start(bf16[16,2,16,1024]{3,2,1,0:T(8,128)(2,1)} %stored.1) | copy-start | bytes 3145732
  21.8 22.0 %collective-permute-start.4 = (bf16[448,1024]{1,0:T(8,128)(2,1)}, bf16[448,1024]{1,0:T(8,128)(2,1)}, u32[]{:S(2)}, u32[]{:S(2)}) collective-permute-start(bf16[448,1024]{1,0:T(8,128)(2,1)} %pad.8.refs_4_), channel_id=1, source_target_pairs={{0,3},{1,0},{2,1},{3,2},{4,7},{5,4},{6,5},{7,6},{8,11},{9,8},{10,9... | collective-permute-start | bytes 2752520 | tf_op jit(solution)/shard_map/ppermute | solution.py:342
  24.3 22.9 %collective-permute-start = (bf16[448,1024]{1,0:T(8,128)(2,1)}, bf16[448,1024]{1,0:T(8,128)(2,1)}, u32[]{:S(2)}, u32[]{:S(2)}) collective-permute-start(bf16[448,1024]{1,0:T(8,128)(2,1)} %pad.7.refs_0_), channel_id=1, source_target_pairs={{0,1},{1,2},{2,3},{3,0},{4,5},{5,6},{6,7},{7,4},{8,9},{9,10},{10,1... | collective-permute-start | bytes 2752520 | tf_op jit(solution)/shard_map/ppermute | solution.py:341
  24.3 42.2 %collective-permute-start.3 = (bf16[448,1024]{1,0:T(8,128)(2,1)}, bf16[448,1024]{1,0:T(8,128)(2,1)}, u32[]{:S(2)}, u32[]{:S(2)}) collective-permute-start(bf16[448,1024]{1,0:T(8,128)(2,1)} %pad.8.refs_4_), channel_id=1, source_target_pairs={{0,1},{1,2},{2,3},{3,0},{4,5},{5,6},{6,7},{7,4},{8,9},{9,10},{10,1... | collective-permute-start | bytes 2752520 | tf_op jit(solution)/shard_map/ppermute | solution.py:343
  43.8 22.8 %collective-permute-start.5 = (bf16[448,1024]{1,0:T(8,128)(2,1)}, bf16[448,1024]{1,0:T(8,128)(2,1)}, u32[]{:S(2)}, u32[]{:S(2)}) collective-permute-start(bf16[448,1024]{1,0:T(8,128)(2,1)} %collective-permute-done.4.refs_6_), channel_id=1, source_target_pairs={{0,3},{1,0},{2,1},{3,2},{4,7},{5,4},{6,5},{7,6},{8,11},{9,8},{10,9... | collective-permute-start | bytes 2752520 | tf_op jit(solution)/shard_map/ppermute | solution.py:345
  47.2 38.2 %collective-permute-start.1 = (bf16[448,1024]{1,0:T(8,128)(2,1)}, bf16[448,1024]{1,0:T(8,128)(2,1)}, u32[]{:S(2)}, u32[]{:S(2)}) collective-permute-start(bf16[448,1024]{1,0:T(8,128)(2,1)} %pad.7.refs_0_), channel_id=1, source_target_pairs={{0,3},{1,0},{2,1},{3,2},{4,7},{5,4},{6,5},{7,6},{8,11},{9,8},{10,9... | collective-permute-start | bytes 2752520 | tf_op jit(solution)/shard_map/ppermute | solution.py:344
  47.2 39.0 %collective-permute-start.2 = (bf16[448,1024]{1,0:T(8,128)(2,1)}, bf16[448,1024]{1,0:T(8,128)(2,1)}, u32[]{:S(2)}, u32[]{:S(2)}) collective-permute-start(bf16[448,1024]{1,0:T(8,128)(2,1)} %collective-permute-done.refs_1_), channel_id=1, source_target_pairs={{0,1},{1,2},{2,3},{3,0},{4,5},{5,6},{6,7},{7,4},{8,9},{9,10},{10,1... | collective-permute-start | bytes 2752520 | tf_op jit(solution)/shard_map/ppermute | solution.py:346
  243.8 101.9 %all-to-all-start.2 = ((bf16[64,2,16,1024]{3,2,1,0:T(8,128)(2,1)}), bf16[64,2,16,1024]{3,2,1,0:T(8,128)(2,1)}, u32[]{:S(2)}, u32[]{:S(2)}) async-start(bf16[64,2,16,1024]{3,2,1,0:T(8,128)(2,1)} %get-tuple-element.11), calls=%async_computation.2 | async-start | bytes 8388608 | tf_op jit(solution)/shard_map/all_to_all | solution.py:351

commit v9 on v8

--- a/solution.py
+++ b/solution.py
@@ -317,7 +317,7 @@
 
 def bring_home(owner, back):
     paths, halves, rows, cols = back.shape
-    groups = 4
+    groups = 8
     return pl.pallas_call(
         functools.partial(home_kernel, groups),
         out_shape=jax.ShapeDtypeStruct((halves, paths, rows, cols), back.dtype),

time: 351 us -> 351 us (level)
  no operation moved by 1% of the time
where the time goes in v9:
time: 351 us; the launch traced here: 350 us
  waiting for transfers between devices  151 us (43%)
  blocking collectives  102 us (29%)
  Pallas kernels  41.9 us (12%)
  starting transfers between devices  26.9 us (8%)
  local copies, waits for them, and re-layouts  16.3 us (5%)
  other arithmetic  10.7 us (3%)
    all_to_all x2, waiting for transfers between devices, exchange(): lax.all_to_all(blocks, 'path', split_axis=0, concat_axis=0, tiled=True)  108 us
    all_to_all x1, blocking collectives, exchange(): lax.all_to_all(blocks, 'path', split_axis=0, concat_axis=0, tiled=True)  102 us
    pallas_call x1, Pallas kernels, path_delta(): pl.pallas_call(functools.partial(delta_kernel, scales, (1024, 512)), out_...  22.4 us
    all_to_all x2, starting transfers between devices, exchange(): lax.all_to_all(blocks, 'path', split_axis=0, concat_axis=0, tiled=True)  19.4 us
    ppermute x1, waiting for transfers between devices, collect(): grd_right = lax.ppermute(grads, 'fsdp', left)  19.3 us
    ppermute x1, waiting for transfers between devices, collect(): grd_left = lax.ppermute(grads, 'fsdp', right)  14.1 us
    transpose x2, local copies, waits for them, and re-layouts, shards(): tokens_t, grads_t = (jnp.concatenate(tokens).T, jnp.concatenate(grads).T)  11.7 us
    ppermute x1, waiting for transfers between devices, collect(): tok_right = lax.ppermute(tokens, 'fsdp', left)  9.55 us
  transfers between devices with their start and end apart: 8, of which 6 were waited for; matrix products, arithmetic and copies ran while one was open for 8% of the time, Pallas kernels for 2%

profile of v9, /device:TPU:1, one launch (start us, length us, event | category | flops | bytes accessed | tf_op | source)
XLA Modules:
  0.0 350.1 jit_solution(5524328515206849795)
XLA Ops:
  0.6 3.2 pick.1
  3.9 13.4 %all-to-all-start = ((bf16[64,2,16,1024]{3,2,1,0:T(8,128)(2,1)}), bf16[64,2,16,1024]{3,2,1,0:T(8,128)(2,1)}, u32[]{:S(2)}, u32[]{:S(2)}) async-start(bf16[64,2,16,1024]{3,2,1,0:T(8,128)(2,1)} %pick.1), calls=%async_computation | async-start | bytes 8388608 | tf_op jit(solution)/shard_map/all_to_all | solution.py:351
  17.2 2.3 pad.7.refs_0_
  19.6 2.2 pad.8.refs_4_
  21.8 2.5 collective-permute-start.4
  24.5 19.3 %collective-permute-done.4.refs_6_ = bf16[448,1024]{1,0:T(8,128)(2,1)} collective-permute-done((bf16[448,1024]{1,0:T(8,128)(2,1)}, bf16[448,1024]{1,0:T(8,128)(2,1)}, u32[]{:S(2)}, u32[]{:S(2)}) %collective-permute-start.4) | collective-permute-done | bytes 917536 | tf_op jit(solution)/shard_map/ppermute | solution.py:342
  43.8 3.4 collective-permute-start.5
  47.2 1.4 collective-permute-start.2
  48.6 2.1 sort.17
  50.8 1.6 multiply_subtract_fusion.base.base_in
  52.4 14.1 %collective-permute-done.3.refs_5_ = bf16[448,1024]{1,0:T(8,128)(2,1)} collective-permute-done((bf16[448,1024]{1,0:T(8,128)(2,1)}, bf16[448,1024]{1,0:T(8,128)(2,1)}, u32[]{:S(2)}, u32[]{:S(2)}) %collective-permute-start.3) | collective-permute-done | bytes 917536 | tf_op jit(solution)/shard_map/ppermute | solution.py:343
  66.5 3.5 maximum_bitcast_fusion.1
  70.0 5.9 %copy.9.grads_t = bf16[1024,1792]{1,0:T(8,128)(2,1)} copy(bf16[1024,1792]{0,1:T(8,128)(2,1)} %maximum_bitcast_fusion.1) | data formatting | bytes 7340032 | tf_op jit(solution)/shard_map/transpose | solution.py:364
  75.9 9.6 %collective-permute-done.1.refs_2_ = bf16[448,1024]{1,0:T(8,128)(2,1)} collective-permute-done((bf16[448,1024]{1,0:T(8,128)(2,1)}, bf16[448,1024]{1,0:T(8,128)(2,1)}, u32[]{:S(2)}, u32[]{:S(2)}) %collective-permute-start.1) | collective-permute-done | bytes 917536 | tf_op jit(solution)/shard_map/ppermute | solution.py:344
  86.2 3.4 maximum_bitcast_fusion
  89.6 5.9 %copy.8.tokens_t = bf16[1024,1792]{1,0:T(8,128)(2,1)} copy(bf16[1024,1792]{0,1:T(8,128)(2,1)} %maximum_bitcast_fusion) | data formatting | bytes 7340032 | tf_op jit(solution)/shard_map/transpose | solution.py:364
  95.5 17.6 %all-to-all-done.arrived = bf16[64,2,16,1024]{3,2,1,0:T(8,128)(2,1)} async-done(((bf16[64,2,16,1024]{3,2,1,0:T(8,128)(2,1)}), bf16[64,2,16,1024]{3,2,1,0:T(8,128)(2,1)}, u32[]{:S(2)}, u32[]{:S(2)}) %all-to-all-start) | async-done | bytes 4194336 | tf_op jit(solution)/shard_map/all_to_all | solution.py:351
  113.1 22.4 %path_delta.1 = bf16[64,2,16,1024]{3,2,1,0:T(8,128)(2,1)} custom-call(s32[64]{0:T(128)} %owner.3, bf16[64,2,16,1024]{3,2,1,0:T(8,128)(2,1)} %all-to-all-done.arrived, s32[64]{0:T(128)} %get-tuple-element.7.order, f32[16,2,16,1024]{3,2,1,0:T(8,128)} %multiply_subtract_fusion.base.base_in, bf16[1024,1792]{1,0:T(8,128)(2,1)} %copy.8.tokens_t, ...), custom_call_target="tpu_custom_call" | custom-call | flops 15032385536 | bytes 23068672 | tf_op jit(solution)/shard_map/path_delta/pallas_call | solution.py:137
  135.5 102.1 %all_to_all.15.received = bf16[64,2,16,1024]{3,2,1,0:T(8,128)(2,1)} all-to-all(bf16[64,2,16,1024]{3,2,1,0:T(8,128)(2,1)} %path_delta.1), channel_id=1, replica_groups=mesh['path'=64,'fsdp'=4] {'path'}, dimensions={0} | all-to-all | bytes 8388608 | tf_op jit(solution)/shard_map/all_to_all | solution.py:351
  237.6 6.3 %update.1 = (bf16[64,2,16,1024]{3,2,1,0:T(8,128)(2,1)}, s32[17]{0:T(128)}) custom-call(s32[64]{0:T(128)} %bitcast.8, s32[64]{0:T(128)} %get-tuple-element.7.order, bf16[64,2,16,1024]{3,2,1,0:T(8,128)(2,1)} %all_to_all.15.received, f32[16,2,16,1024]{3,2,1,0:T(8,128)} %multiply_subtract_fusion.base.base_in), custom_call_target="tpu_custom_call" | custom-call | flops 2097152 | bytes 8388608 | tf_op jit(solution)/shard_map/update/pallas_call | solution.py:226
  243.9 6.0 %all-to-all-start.2 = ((bf16[64,2,16,1024]{3,2,1,0:T(8,128)(2,1)}), bf16[64,2,16,1024]{3,2,1,0:T(8,128)(2,1)}, u32[]{:S(2)}, u32[]{:S(2)}) async-start(bf16[64,2,16,1024]{3,2,1,0:T(8,128)(2,1)} %get-tuple-element.11), calls=%async_computation.2 | async-start | bytes 8388608 | tf_op jit(solution)/shard_map/all_to_all | solution.py:351
  249.9 5.9 %next_state.1 = f32[16,2,16,1024]{3,2,1,0:T(8,128)} custom-call(s32[17]{0:T(128)} %get-tuple-element.10.first, s32[64]{0:T(128)} %get-tuple-element.7.order, bf16[64,2,16,1024]{3,2,1,0:T(8,128)(2,1)} %all_to_all.15.received, f32[16,2,16,1024]{3,2,1,0:T(8,128)} %momentum.1), custom_call_target="tpu_custom_call" | custom-call | flops 2097152 | bytes 8388608 | tf_op jit(solution)/shard_map/next_state/pallas_call | solution.py:273
  255.8 90.0 %all-to-all-done.2.back = bf16[64,2,16,1024]{3,2,1,0:T(8,128)(2,1)} async-done(((bf16[64,2,16,1024]{3,2,1,0:T(8,128)(2,1)}), bf16[64,2,16,1024]{3,2,1,0:T(8,128)(2,1)}, u32[]{:S(2)}, u32[]{:S(2)}) %all-to-all-start.2) | async-done | bytes 4194336 | tf_op jit(solution)/shard_map/all_to_all | solution.py:351
  345.8 4.2 %bring_home.1 = bf16[2,64,16,1024]{3,2,1,0:T(8,128)(2,1)} custom-call(s32[64]{0:T(128)} %owner.3, bf16[64,2,16,1024]{3,2,1,0:T(8,128)(2,1)} %all-to-all-done.2.back), custom_call_target="tpu_custom_call" | custom-call | bytes 8388608 | tf_op jit(solution)/shard_map/bring_home/pallas_call | solution.py:321
  (13 shorter events, 1.0 us)
Async XLA Ops:
  3.8 44.8 %copy-start.2 = (s32[64,1]{0,1:T(1,128)S(1)}, s32[64,1]{0,1:T(1,128)}, u32[]{:S(2)}) copy-start(s32[64,1]{0,1:T(1,128)} %param.10) | copy-start | bytes 772
  3.9 109.2 %all-to-all-start = ((bf16[64,2,16,1024]{3,2,1,0:T(8,128)(2,1)}), bf16[64,2,16,1024]{3,2,1,0:T(8,128)(2,1)}, u32[]{:S(2)}, u32[]{:S(2)}) async-start(bf16[64,2,16,1024]{3,2,1,0:T(8,128)(2,1)} %pick.1), calls=%async_computation | async-start | bytes 8388608 | tf_op jit(solution)/shard_map/all_to_all | solution.py:351
  17.2 33.5 %copy-start = (f32[16,2,16,1024]{3,2,1,0:T(8,128)S(1)}, f32[16,2,16,1024]{3,2,1,0:T(8,128)}, u32[]{:S(2)}) copy-start(f32[16,2,16,1024]{3,2,1,0:T(8,128)} %momentum.1) | copy-start | bytes 6291460
  17.2 33.5 %copy-start.1 = (bf16[16,2,16,1024]{3,2,1,0:T(8,128)(2,1)S(1)}, bf16[16,2,16,1024]{3,2,1,0:T(8,128)(2,1)}, u32[]{:S(2)}) copy-start(bf16[16,2,16,1024]{3,2,1,0:T(8,128)(2,1)} %stored.1) | copy-start | bytes 3145732
  21.8 22.0 %collective-permute-start.4 = (bf16[448,1024]{1,0:T(8,128)(2,1)}, bf16[448,1024]{1,0:T(8,128)(2,1)}, u32[]{:S(2)}, u32[]{:S(2)}) collective-permute-start(bf16[448,1024]{1,0:T(8,128)(2,1)} %pad.8.refs_4_), channel_id=1, source_target_pairs={{0,3},{1,0},{2,1},{3,2},{4,7},{5,4},{6,5},{7,6},{8,11},{9,8},{10,9... | collective-permute-start | bytes 2752520 | tf_op jit(solution)/shard_map/ppermute | solution.py:342
  24.3 22.9 %collective-permute-start = (bf16[448,1024]{1,0:T(8,128)(2,1)}, bf16[448,1024]{1,0:T(8,128)(2,1)}, u32[]{:S(2)}, u32[]{:S(2)}) collective-permute-start(bf16[448,1024]{1,0:T(8,128)(2,1)} %pad.7.refs_0_), channel_id=1, source_target_pairs={{0,1},{1,2},{2,3},{3,0},{4,5},{5,6},{6,7},{7,4},{8,9},{9,10},{10,1... | collective-permute-start | bytes 2752520 | tf_op jit(solution)/shard_map/ppermute | solution.py:341
  24.3 42.2 %collective-permute-start.3 = (bf16[448,1024]{1,0:T(8,128)(2,1)}, bf16[448,1024]{1,0:T(8,128)(2,1)}, u32[]{:S(2)}, u32[]{:S(2)}) collective-permute-start(bf16[448,1024]{1,0:T(8,128)(2,1)} %pad.8.refs_4_), channel_id=1, source_target_pairs={{0,1},{1,2},{2,3},{3,0},{4,5},{5,6},{6,7},{7,4},{8,9},{9,10},{10,1... | collective-permute-start | bytes 2752520 | tf_op jit(solution)/shard_map/ppermute | solution.py:343
  43.8 22.8 %collective-permute-start.5 = (bf16[448,1024]{1,0:T(8,128)(2,1)}, bf16[448,1024]{1,0:T(8,128)(2,1)}, u32[]{:S(2)}, u32[]{:S(2)}) collective-permute-start(bf16[448,1024]{1,0:T(8,128)(2,1)} %collective-permute-done.4.refs_6_), channel_id=1, source_target_pairs={{0,3},{1,0},{2,1},{3,2},{4,7},{5,4},{6,5},{7,6},{8,11},{9,8},{10,9... | collective-permute-start | bytes 2752520 | tf_op jit(solution)/shard_map/ppermute | solution.py:345
  47.2 38.2 %collective-permute-start.1 = (bf16[448,1024]{1,0:T(8,128)(2,1)}, bf16[448,1024]{1,0:T(8,128)(2,1)}, u32[]{:S(2)}, u32[]{:S(2)}) collective-permute-start(bf16[448,1024]{1,0:T(8,128)(2,1)} %pad.7.refs_0_), channel_id=1, source_target_pairs={{0,3},{1,0},{2,1},{3,2},{4,7},{5,4},{6,5},{7,6},{8,11},{9,8},{10,9... | collective-permute-start | bytes 2752520 | tf_op jit(solution)/shard_map/ppermute | solution.py:344
  47.2 39.0 %collective-permute-start.2 = (bf16[448,1024]{1,0:T(8,128)(2,1)}, bf16[448,1024]{1,0:T(8,128)(2,1)}, u32[]{:S(2)}, u32[]{:S(2)}) collective-permute-start(bf16[448,1024]{1,0:T(8,128)(2,1)} %collective-permute-done.refs_1_), channel_id=1, source_target_pairs={{0,1},{1,2},{2,3},{3,0},{4,5},{5,6},{6,7},{7,4},{8,9},{9,10},{10,1... | collective-permute-start | bytes 2752520 | tf_op jit(solution)/shard_map/ppermute | solution.py:346
  243.9 101.9 %all-to-all-start.2 = ((bf16[64,2,16,1024]{3,2,1,0:T(8,128)(2,1)}), bf16[64,2,16,1024]{3,2,1,0:T(8,128)(2,1)}, u32[]{:S(2)}, u32[]{:S(2)}) async-start(bf16[64,2,16,1024]{3,2,1,0:T(8,128)(2,1)} %get-tuple-element.11), calls=%async_computation.2 | async-start | bytes 8388608 | tf_op jit(solution)/shard_map/all_to_all | solution.py:351
